TPU v7x, 32 devices: a whole 2x2x4 slice. The times are simulated.
32 devices in a mesh: grp: 2 (over x), exp: 16 (over z, y, core).
Axes of the slice: x: 2, y: 2, z: 4, core: 2. Of those that a mesh axis runs over, the one named last changes fastest.
Arguments:
- tokens: bfloat16 [4096, 2048], P(('grp', 'exp')), parts along dimension 0, may hold values from -6 to 6
- expert_ids: int32 [4096, 8], P(('grp', 'exp')), parts along dimension 0, may hold values from 0 to 63, all different within a row; in each aligned block of 128 rows (0 to 127, 128 to 255, ...) at most 24 rows name the same one
- route_weight: float32 [4096, 8], P(('grp', 'exp')), parts along dimension 0, may hold values from 0.05 to 0.5
- w_gate: bfloat16 [64, 2048, 768], P('exp'), may hold values from -0.125 to 0.125
- w_up: bfloat16 [64, 2048, 768], P('exp'), may hold values from -0.125 to 0.125
- w_down: bfloat16 [64, 768, 2048], P('exp'), may hold values from -0.21875 to 0.21875
Outputs:
- mixed: bfloat16 [4096, 2048], P(('grp', 'exp')), parts along dimension 0
There are 2 independent parts, one for each index of `grp`. A program takes and returns all parts, laid end to end along the dimension named above; an argument that names none is the same for every part. Nothing has to cross between parts.
Inputs may be any that keep to these rules, and one draw needn't show every extreme that they name: `expert_ids`: among the rows of one device (aligned blocks of 128 tokens) no expert is named more than 24 times, a bound that some block reaches; the experts of one token differ.
All inputs are finite; a program needn't handle non-finite values.
Results may differ from a plain program's by a relative error of at most 0.0057.
Values may be sent and summed in bfloat16 or wider, within the bound.
No kernel may reach another device: no remote copies, remote signals or barrier semaphores. Data moves between devices by JAX's collectives and lax.ppermute only.
A program may use at most 128 MiB of HBM per device.

v0:
```python
import jax
import jax.numpy as jnp
from jax import lax
from jax.sharding import PartitionSpec as P

CAP = 24


def slot_positions(expert_ids, experts_all):
    rows_count = expert_ids.shape[0] * expert_ids.shape[1]
    flat_ids = expert_ids.reshape(rows_count)
    onehot = (flat_ids[:, None] == jnp.arange(experts_all, dtype=jnp.int32)[None, :]).astype(
        jnp.int32
    )
    before = jnp.cumsum(onehot, axis=0) - onehot
    slot_of = jnp.sum(before * onehot, axis=1)
    return flat_ids * CAP + slot_of


def body(tokens, expert_ids, route_weight, w_gate, w_up, w_down):
    tok_rows, model_width = tokens.shape
    top_count = expert_ids.shape[1]
    local_experts = w_gate.shape[0]
    owners = lax.axis_size("exp")
    experts_all = local_experts * owners
    dest_pos = slot_positions(expert_ids, experts_all)
    token_of = jnp.arange(tok_rows * top_count, dtype=jnp.int32) // top_count
    row_index = jnp.full((experts_all * CAP,), tok_rows, jnp.int32).at[dest_pos].set(token_of)
    padded = jnp.concatenate([tokens, jnp.zeros((1, model_width), tokens.dtype)], axis=0)
    outgoing = padded[row_index].reshape(owners, local_experts, CAP, model_width)
    arrived = lax.all_to_all(outgoing, "exp", split_axis=0, concat_axis=0, tiled=True)
    gate = jnp.einsum("nlcd,ldf->nlcf", arrived, w_gate, preferred_element_type=jnp.float32)
    up = jnp.einsum("nlcd,ldf->nlcf", arrived, w_up, preferred_element_type=jnp.float32)
    hidden = (jax.nn.silu(gate) * up).astype(jnp.bfloat16)
    returned = lax.all_to_all(
        jnp.einsum("nlcf,lfd->nlcd", hidden, w_down, preferred_element_type=jnp.float32).astype(
            jnp.bfloat16
        ),
        "exp",
        split_axis=0,
        concat_axis=0,
        tiled=True,
    )
    results = returned.reshape(experts_all * CAP, model_width)[dest_pos]
    results = results.reshape(tok_rows, top_count, model_width)
    mixed = jnp.sum(results.astype(jnp.float32) * route_weight[:, :, None], axis=1)
    return mixed.astype(jnp.bfloat16)


def solution(mesh):
    in_specs = (
        P(("grp", "exp"), None),
        P(("grp", "exp"), None),
        P(("grp", "exp"), None),
        P("exp", None, None),
        P("exp", None, None),
        P("exp", None, None),
    )
    out_specs = P(("grp", "exp"), None)
    return jax.shard_map(body, mesh=mesh, in_specs=in_specs, out_specs=out_specs, check_vma=False)
```

profile of v0, /device:TPU:15, one launch (start us, length us, event | category | flops | bytes accessed | tf_op | source)
XLA Modules:
  0.0 377.4 jit_solution(7164178874283046641)
XLA Ops:
  0.0 0.8 copy.17
  0.8 0.1 eq.29
  0.9 0.1 eq.25
  1.0 0.7 broadcast_multiply_fusion
  1.7 18.0 %reduce-window.6 = s32[64,8,128]{2,1,0:T(8,128)S(1)} reduce-window(s32[64,8,128]{2,1,0:T(8,128)S(1)} %fusion.27, s32[]{:T(128)} %constant.31.clone.1), window={size=1x1x128 pad=0_0x0_0x127_0}, to_apply=%region_0.0 | reduce-window | flops 8323072 | bytes 524292 | tf_op jit(solution)/shard_map/reduce-window
  19.7 0.1 slice.12
  19.8 0.1 copy.19
  20.0 0.1 copy.20
  20.1 0.1 broadcast_add_fusion
  20.3 0.1 copy.16
  20.4 0.1 mul.36
  20.5 0.1 fusion.26
  20.5 4.3 %scatter_custom_fusion = s32[1536]{0:T(1024)S(1)} fusion(s32[1024]{0:T(1024)S(1)} %bitcast.73, s32[1024]{0:T(1024)S(1)} %add_select_fusion, s32[]{:T(128)} %constant.29.clone.1), kind=kCustom, calls=%fused_computation.39 | custom fusion | bytes 6148 | tf_op jit(solution)/shard_map/scatter | solution.py:28
  24.9 1.1 concatenate.3
  26.0 7.1 %gather_fusion = bf16[1536,2048]{1,0:T(8,128)(2,1)} fusion(bf16[129,2048]{1,0:T(8,128)(2,1)S(1)} %concatenate.3, s32[2048]{0:T(1024)S(1)} %pad_clamp_fusion), kind=kCustom, calls=%fused_computation | custom fusion | bytes 12589056 | tf_op jit(solution)/shard_map/gather | solution.py:30
  33.1 143.7 %all_to_all.10 = bf16[16,4,24,2048]{3,2,1,0:T(8,128)(2,1)S(1)} all-to-all(bf16[16,4,24,2048]{3,2,1,0:T(8,128)(2,1)} %bitcast.69), channel_id=1, replica_groups=mesh['grp'=2,'exp'=16] {'exp'}, dimensions={0} | all-to-all | bytes 12582912 | tf_op jit(solution)/shard_map/all_to_all | solution.py:31
  176.8 0.0 copy-start
  176.8 2.7 copy-done
  179.5 10.1 %fusion.2 = f32[4,16,24,768]{3,2,1,0:T(8,128)} fusion(bf16[4,2048,768]{2,1,0:T(8,128)(2,1)} %param.10, bf16[16,4,24,2048]{3,2,1,0:T(8,128)(2,1)S(1)} %all_to_all.10), kind=kOutput, calls=%fused_computation.5 | convolution fusion | flops 4831838208 | bytes 23592960 | tf_op jit(solution)/shard_map/nlcd,ldf->nlcf/dot_general | solution.py:33
  189.6 18.4 %convert_bitcast_fusion = bf16[16,4,24,2048]{3,2,0,1:T(8,128)(2,1)} fusion(bf16[4,768,2048]{2,1,0:T(8,128)(2,1)} %param.11, f32[4,16,24,768]{3,2,1,0:T(8,128)} %fusion.2, bf16[4,2048,768]{2,1,0:T(8,128)(2,1)} %param.9, bf16[16,4,24,2048]{3,2,1,0:T(8,128)(2,1)} %copy-done), kind=kOutput, calls=%fused_computation.11 | convolution fusion | flops 9673900032 | bytes 42467328 | tf_op jit(solution)/shard_map/nlcf,lfd->nlcd/dot_general | solution.py:36
  208.0 6.6 %copy.23 = bf16[16,4,24,2048]{3,2,1,0:T(8,128)(2,1)} copy(bf16[16,4,24,2048]{3,2,0,1:T(8,128)(2,1)} %convert_bitcast_fusion) | data formatting | bytes 12582912 | tf_op jit(solution)/shard_map/convert_element_type | solution.py:36
  214.5 0.0 copy-start.1
  214.5 5.7 %all-to-all-start.1 = ((bf16[16,4,24,2048]{3,2,1,0:T(8,128)(2,1)}), bf16[16,4,24,2048]{3,2,1,0:T(8,128)(2,1)}, u32[]{:S(2)}, u32[]{:S(2)}) async-start(bf16[16,4,24,2048]{3,2,1,0:T(8,128)(2,1)} %copy.23), calls=%async_computation.1 | async-start | bytes 12582912 | tf_op jit(solution)/shard_map/all_to_all | solution.py:35
  220.2 0.0 copy-done.1
  220.2 0.1 copy.24
  220.3 137.3 %all-to-all-done.1 = bf16[16,4,24,2048]{3,2,1,0:T(8,128)(2,1)} async-done(((bf16[16,4,24,2048]{3,2,1,0:T(8,128)(2,1)}), bf16[16,4,24,2048]{3,2,1,0:T(8,128)(2,1)}, u32[]{:S(2)}, u32[]{:S(2)}) %all-to-all-start.1) | async-done | bytes 6291488 | tf_op jit(solution)/shard_map/all_to_all | solution.py:35
  357.6 12.4 %gather_fusion.1 = bf16[1024,2048]{1,0:T(8,128)(2,1)} fusion(bf16[1536,2048]{1,0:T(8,128)(2,1)} %bitcast.14, s32[1024]{0:T(1024)S(1)} %broadcast_clamp_fusion), kind=kCustom, calls=%fused_computation.1 | custom fusion | bytes 8392704 | tf_op jit(solution)/shard_map/gather | solution.py:44
  370.0 7.3 %fusion.6 = bf16[128,2048]{1,0:T(8,128)(2,1)} fusion(bf16[1024,2048]{1,0:T(8,128)(2,1)} %gather_fusion.1, f32[128,8]{1,0:T(8,128)S(1)} %copy.24), kind=kLoop, calls=%fused_computation.10 | loop fusion | flops 6029312 | bytes 4722688 | tf_op jit(solution)/shard_map/reduce_sum | solution.py:46
  (8 shorter events, 0.1 us)
Async XLA Ops:
  176.8 2.7 copy-start
  214.5 5.7 %copy-start.1 = (f32[128,8]{0,1:T(8,128)S(1)}, f32[128,8]{0,1:T(8,128)}, u32[]{:S(2)}) copy-start(f32[128,8]{0,1:T(8,128)} %param.8) | copy-start | bytes 12292
  214.5 143.1 %all-to-all-start.1 = ((bf16[16,4,24,2048]{3,2,1,0:T(8,128)(2,1)}), bf16[16,4,24,2048]{3,2,1,0:T(8,128)(2,1)}, u32[]{:S(2)}, u32[]{:S(2)}) async-start(bf16[16,4,24,2048]{3,2,1,0:T(8,128)(2,1)} %copy.23), calls=%async_computation.1 | async-start | bytes 12582912 | tf_op jit(solution)/shard_map/all_to_all | solution.py:35
where the time goes:
time: 378 us; the launch traced here: 377 us
  blocking collectives  144 us (38%)
  waiting for transfers between devices  137 us (36%)
  local copies, waits for them, and re-layouts  35.7 us (9%)
  matrix products  28.5 us (8%)
  other arithmetic  26.3 us (7%)
  starting transfers between devices  5.68 us (2%)
    all_to_all x1, blocking collectives, body(): lax.all_to_all(outgoing, 'exp', split_axis=0, concat_axis=0, tiled=True)  144 us
    all_to_all x1, waiting for transfers between devices, body(): lax.all_to_all(jnp.einsum('nlcf,lfd->nlcd', hidden, w_down, preferred_ele...  137 us
    dot_general x1, matrix products, body(): jnp.einsum('nlcf,lfd->nlcd', hidden, w_down, preferred_element_type=jnp.f...  18.4 us
    another operation x3, other arithmetic  18.2 us
    gather x1, local copies, waits for them, and re-layouts, body(): results = returned.reshape(experts_all * CAP, model_width)[dest_pos]  12.4 us
    dot_general x1, matrix products, body(): jnp.einsum('nlcd,ldf->nlcf', arrived, w_up, preferred_element_type=jnp.fl...  10.1 us
  transfers between devices with their start and end apart: 1, of which 1 were waited for; matrix products, arithmetic and copies ran while one was open for 0% of the time, Pallas kernels for 0%

commit v1 on v0

v1 whole, which is shorter than its diff:
```python
import functools

import jax
import jax.numpy as jnp
from jax import lax
from jax.experimental import pallas as pl
from jax.experimental.pallas import tpu as pltpu
from jax.sharding import PartitionSpec as P

CAP = 24
CORES = 2
VMEM_LIMIT = 48 * 1024 * 1024


def params(**kw):
    return pltpu.CompilerParams(vmem_limit_bytes=VMEM_LIMIT, **kw)


def selector(code_ref, local):
    row = jnp.concatenate([code_ref[0, local : local + 1, :], code_ref[1, local : local + 1, :] + CAP], axis=1)
    slots = lax.broadcasted_iota(jnp.int32, (2 * CAP, row.shape[1]), 0)
    return row == slots


def dispatch_kernel(code_ref, wt_ref, x0_ref, x1_ref, rows_ref, weight_ref):
    local_experts = rows_ref.shape[0]
    picks = []
    for local in range(local_experts):
        hit = selector(code_ref, local)
        wt = jnp.concatenate([wt_ref[0, local : local + 1, :], wt_ref[1, local : local + 1, :]], axis=1)
        weight = jnp.sum(jnp.where(hit, wt, 0.0), axis=1, keepdims=True)
        weight_ref[local] = jnp.broadcast_to(weight, weight_ref.shape[1:])
        picks.append(jnp.where(hit, 1.0, 0.0).astype(jnp.bfloat16))
    pick = jnp.concatenate(picks, axis=0)
    x = jnp.concatenate([x0_ref[...], x1_ref[...]], axis=0)
    rows = jnp.dot(pick, x, preferred_element_type=jnp.float32).astype(jnp.bfloat16)
    rows_ref[...] = rows.reshape(rows_ref.shape)


def dispatch(code, wt, x0, x1):
    local_experts = code.shape[1]
    width = x0.shape[1]
    return pl.pallas_call(
        dispatch_kernel,
        out_shape=(
            jax.ShapeDtypeStruct((local_experts, 2 * CAP, width), jnp.bfloat16),
            jax.ShapeDtypeStruct((local_experts, 2 * CAP, 128), jnp.float32),
        ),
        compiler_params=params(),
        cost_estimate=pl.CostEstimate(
            flops=2 * local_experts * 2 * CAP * 2 * x0.shape[0] * width,
            bytes_accessed=2 * width * (2 * x0.shape[0] + local_experts * 2 * CAP),
            transcendentals=0,
        ),
    )(code, wt, x0, x1)


def ffn_kernel(pairs, *refs):
    rows_refs, weight_refs = refs[:pairs], refs[pairs : 2 * pairs]
    gate_w, up_w, down_w, out_ref, total = refs[2 * pairs :]
    step = pl.program_id(1)
    rows = jnp.concatenate([r[0] for r in rows_refs], axis=0)
    weight = jnp.concatenate([r[0, :, :1] for r in weight_refs], axis=0)
    gate = jnp.dot(rows, gate_w[0], preferred_element_type=jnp.float32)
    up = jnp.dot(rows, up_w[0], preferred_element_type=jnp.float32)
    hidden = (gate / (1.0 + jnp.exp(-gate)) * up * weight).astype(jnp.bfloat16)
    part = jnp.dot(hidden, down_w[0], preferred_element_type=jnp.float32)

    @pl.when(step == 0)
    def _():
        total[...] = part

    @pl.when(step > 0)
    def _():
        total[...] += part

    @pl.when(step == pl.num_programs(1) - 1)
    def _():
        out_ref[...] = total[...].astype(jnp.bfloat16).reshape(out_ref.shape)


def ffn(rows, weights, w_gate, w_up, w_down):
    pairs = len(rows)
    local_experts, width, hidden = w_gate.shape
    block = 256 if hidden % 256 == 0 else hidden
    count = pairs * 2 * CAP
    return pl.pallas_call(
        functools.partial(ffn_kernel, pairs),
        grid=(local_experts, hidden // block),
        in_specs=[pl.BlockSpec((1, 2 * CAP, width), lambda l, f: (l, 0, 0))] * pairs
        + [pl.BlockSpec((1, 2 * CAP, 128), lambda l, f: (l, 0, 0))] * pairs
        + [
            pl.BlockSpec((1, width, block), lambda l, f: (l, 0, f)),
            pl.BlockSpec((1, width, block), lambda l, f: (l, 0, f)),
            pl.BlockSpec((1, block, width), lambda l, f: (l, f, 0)),
        ],
        out_specs=pl.BlockSpec((pairs, 1, 2 * CAP, width), lambda l, f: (0, l, 0, 0)),
        out_shape=jax.ShapeDtypeStruct((pairs, local_experts, 2 * CAP, width), jnp.bfloat16),
        scratch_shapes=[pltpu.VMEM((count, width), jnp.float32)],
        compiler_params=params(),
        cost_estimate=pl.CostEstimate(
            flops=6 * local_experts * count * width * hidden,
            bytes_accessed=6 * local_experts * width * hidden + 4 * local_experts * count * width,
            transcendentals=local_experts * count * hidden,
        ),
    )(*rows, *weights, w_gate, w_up, w_down)


def combine_kernel(code_ref, out_ref, y0_ref, y1_ref):
    local_experts = out_ref.shape[1]
    pick = jnp.concatenate(
        [jnp.where(selector(code_ref, l), 1.0, 0.0).astype(jnp.bfloat16) for l in range(local_experts)], axis=0
    )
    out = out_ref[0].reshape(local_experts * 2 * CAP, out_ref.shape[3])
    y = lax.dot_general(pick, out, (((0,), (0,)), ((), ())), preferred_element_type=jnp.float32)
    y = y.astype(jnp.bfloat16)
    y0_ref[...] = y[: y0_ref.shape[0]]
    y1_ref[...] = y[y0_ref.shape[0] :]


def combine(code, results, pair):
    _, local_experts, slots, width = results.shape
    tok = code.shape[2]
    shape = jax.ShapeDtypeStruct((tok, width), jnp.bfloat16)
    return pl.pallas_call(
        combine_kernel,
        grid=(1,),
        in_specs=[
            pl.BlockSpec(code.shape, lambda i: (0, 0, 0)),
            pl.BlockSpec((1, local_experts, slots, width), lambda i: (pair, 0, 0, 0)),
        ],
        out_specs=(pl.BlockSpec((tok, width), lambda i: (0, 0)),) * 2,
        out_shape=(shape, shape),
        compiler_params=params(),
        cost_estimate=pl.CostEstimate(
            flops=4 * local_experts * slots * tok * width,
            bytes_accessed=2 * width * (2 * tok + local_experts * slots),
            transcendentals=0,
        ),
    )(code, results)


def body(depth, lines, tokens, expert_ids, route_weight, w_gate, w_up, w_down):
    tok, width = tokens.shape
    local_experts = w_gate.shape[0]
    index = lax.axis_index("exp")
    z, y, core = index // (lines * CORES), index // CORES % lines, index % CORES

    def place(pz, py, pc):
        return (pz * lines + py) * CORES + pc

    everyone = [(a, b, c) for a in range(depth) for b in range(lines) for c in range(CORES)]

    def send(value, move, who=lambda a: True):
        perm = [(place(a, b, c), place(*move(a, b, c))) for a, b, c in everyone if who(a)]
        return lax.ppermute(value, "exp", perm)

    def swap_core(value):
        return send(value, lambda a, b, c: (a, b, 1 - c))

    def swap_line(value, who=lambda a: True):
        return send(value, lambda a, b, c: (a, 1 - b, c), who)

    def step_up(value, distance):
        return send(value, lambda a, b, c: (a + 1, b, c), lambda a: distance - 1 <= a < depth - 1)

    def step_down(value, distance):
        return send(value, lambda a, b, c: (a - 1, b, c), lambda a: 0 < a <= depth - distance)

    table = jnp.concatenate([expert_ids.T.astype(jnp.float32), route_weight.T], axis=0)
    table = lax.all_gather(table, "exp", axis=0)
    order = [(r, b, c) for r in range(depth) for b in range(lines) for c in range(CORES)]
    source = jnp.stack([place((z + r) % depth, y ^ b, core ^ c) for r, b, c in order])
    table = jnp.take(table, source, axis=0)
    top = expert_ids.shape[1]
    mine = (index * local_experts + jnp.arange(local_experts, dtype=jnp.int32)).astype(jnp.float32)
    hit = table[:, None, :top, :] == mine[None, :, None, None]
    member = jnp.sum(hit.astype(jnp.float32), axis=2)
    wt = jnp.sum(jnp.where(hit, table[:, None, top:, :], 0.0), axis=2)
    before = jnp.triu(jnp.ones((tok, tok), jnp.bfloat16), 1)
    rank = jnp.einsum("nlt,tu->nlu", member.astype(jnp.bfloat16), before, preferred_element_type=jnp.float32)
    code = jnp.where(member > 0.0, rank.astype(jnp.int32), -1024)

    above, below = [tokens], [tokens]
    across_above, across_below = [None], [None]
    if lines > 1:
        across = swap_line(tokens)
    for d in range(1, depth):
        below.append(step_up(below[-1], d))
        above.append(step_down(above[-1], d))
        if lines > 1:
            across_below.append(swap_line(below[-1], lambda a, d=d: a >= d))
            across_above.append(swap_line(above[-1], lambda a, d=d: a + d < depth))
    pieces = []
    for r in range(depth):
        if r == 0:
            pieces.append(tokens)
        else:
            pieces.append(jnp.where(z + r < depth, above[r], below[depth - r]))
        if lines > 1:
            if r == 0:
                pieces.append(across)
            else:
                pieces.append(jnp.where(z + r < depth, across_above[r], across_below[depth - r]))
    rows, weights = [], []
    for p, piece in enumerate(pieces):
        a, w = dispatch(code[2 * p : 2 * p + 2], wt[2 * p : 2 * p + 2], piece, swap_core(piece))
        rows.append(a)
        weights.append(w)

    results = ffn(rows, weights, w_gate, w_up, w_down)

    wide = jnp.float32
    link = jnp.bfloat16 if depth <= 4 else wide
    sums = [None] * depth
    first = []
    for d in range(depth - 1, 0, -1):
        for r in (d, depth - d):
            if r not in first:
                first.append(r)
    for r in first + [0]:
        halves = []
        for b in reversed(range(lines)):
            p = r * lines + b
            y0, y1 = combine(code[2 * p : 2 * p + 2], results, p)
            halves.append(y0.astype(wide) + swap_core(y1).astype(wide))
        own = halves[-1]
        if lines > 1:
            own = own + swap_line(halves[0].astype(jnp.bfloat16)).astype(wide)
        sums[r] = own
    up, down = sums[depth - 1] if depth > 1 else None, sums[1] if depth > 1 else None
    mixed = sums[0]
    for d in range(depth - 1, 0, -1):
        got_up = send(up.astype(link), lambda a, b, c: (a + 1, b, c), lambda a, d=d: a + d < depth).astype(wide)
        got_down = send(down.astype(link), lambda a, b, c: (a - 1, b, c), lambda a, d=d: a - d >= 0).astype(wide)
        if d > 1:
            up, down = sums[d - 1] + got_up, sums[depth - d + 1] + got_down
        else:
            mixed = mixed + got_up + got_down
    return mixed.astype(jnp.bfloat16)


def solution(mesh):
    groups, owners = mesh.shape["grp"], mesh.shape["exp"]
    lines = max(1, 4 // groups)
    depth = owners // (lines * CORES)
    in_specs = (
        P(("grp", "exp"), None),
        P(("grp", "exp"), None),
        P(("grp", "exp"), None),
        P("exp", None, None),
        P("exp", None, None),
        P("exp", None, None),
    )
    out_specs = P(("grp", "exp"), None)
    return jax.shard_map(
        functools.partial(body, depth, lines),
        mesh=mesh,
        in_specs=in_specs,
        out_specs=out_specs,
        check_vma=False,
    )
```

time: 378 us -> 224 us (0.59)
  the two profiles are of different devices: /device:TPU:15 before, /device:TPU:0 now
where the time goes in v1:
time: 224 us; the launch traced here: 223 us
  waiting for transfers between devices  98.6 us (44%)
  starting transfers between devices  47.4 us (21%)
  Pallas kernels  43.4 us (19%)
  blocking collectives  24.6 us (11%)
  other arithmetic  5.47 us (2%)
  local copies, waits for them, and re-layouts  2.39 us (1%)
    ppermute x39, waiting for transfers between devices, send(): return lax.ppermute(value, 'exp', perm)  98.6 us
    ppermute x39, starting transfers between devices, send(): return lax.ppermute(value, 'exp', perm)  47.4 us
    pallas_call x1, Pallas kernels, ffn(): pl.pallas_call(functools.partial(ffn_kernel, pairs), grid=(local_experts,...  27.7 us
    all_gather x1, blocking collectives, body(): table = lax.all_gather(table, 'exp', axis=0)  24.6 us
    pallas_call x8, Pallas kernels, combine(): pl.pallas_call(combine_kernel, grid=(1,), in_specs=[pl.BlockSpec(code.sha...  12.7 us
  transfers between devices with their start and end apart: 39, of which 13 were waited for; matrix products, arithmetic and copies ran while one was open for 2% of the time, Pallas kernels for 6%

profile of v1, /device:TPU:0, one launch (start us, length us, event | category | flops | bytes accessed | tf_op | source)
XLA Modules:
  0.0 222.9 jit_solution(849203772413182338)
XLA Ops:
  0.0 3.0 %collective-permute-start.1 = (bf16[128,2048]{1,0:T(8,128)(2,1)}, bf16[128,2048]{1,0:T(8,128)(2,1)S(1)}, u32[]{:S(2)}, u32[]{:S(2)}) collective-permute-start(bf16[128,2048]{1,0:T(8,128)(2,1)} %x0_ref.1), channel_id=1, source_target_pairs={{0,2},{1,3},{2,0},{3,1},{4,6},{5,7},{6,4},{7,5},{8,10},{9,11},{10,... | collective-permute-start | bytes 1572872 | tf_op jit(solution)/shard_map/ppermute | solution.py:156
  3.0 3.5 %collective-permute-start.4 = (bf16[128,2048]{1,0:T(8,128)(2,1)}, bf16[128,2048]{1,0:T(8,128)(2,1)S(1)}, u32[]{:S(2)}, u32[]{:S(2)}) collective-permute-start(bf16[128,2048]{1,0:T(8,128)(2,1)} %x0_ref.1), channel_id=1, source_target_pairs={{0,4},{1,5},{2,6},{3,7},{4,8},{5,9},{6,10},{7,11},{8,12},{9,13},{1... | collective-permute-start | bytes 1572872 | tf_op jit(solution)/shard_map/ppermute | solution.py:156
  6.5 1.3 collective-permute-start.3
  8.1 0.7 convert_bitcast_fusion
  8.7 0.7 pad_maximum_fusion
  9.4 24.6 %all-gather = f32[256,128]{1,0:T(8,128)S(1)} all-gather(f32[16,128]{1,0:T(8,128)S(1)} %pad_maximum_fusion), channel_id=2, replica_groups=mesh['grp'=2,'exp'=16] {'exp'}, dimensions={0}, use_global_device_ids=true | all-gather | bytes 139264 | tf_op jit(solution)/shard_map/all_gather | solution.py:171
  34.9 1.3 collective-permute-start.11
  36.2 0.7 collective-permute-start.5
  37.3 13.7 %collective-permute-done.11 = bf16[128,2048]{1,0:T(8,128)(2,1)S(1)} collective-permute-done((bf16[128,2048]{1,0:T(8,128)(2,1)S(1)}, bf16[128,2048]{1,0:T(8,128)(2,1)S(1)}, u32[]{:S(2)}, u32[]{:S(2)}) %collective-permute-start.11) | collective-permute-done | bytes 524320 | tf_op jit(solution)/shard_map/ppermute | solution.py:156
  50.9 1.3 collective-permute-start.16
  52.3 0.7 collective-permute-start.19
  53.0 0.7 collective-permute-start.14
  53.7 0.7 collective-permute-start.6
  54.4 11.7 %collective-permute-done.16 = bf16[128,2048]{1,0:T(8,128)(2,1)S(1)} collective-permute-done((bf16[128,2048]{1,0:T(8,128)(2,1)S(1)}, bf16[128,2048]{1,0:T(8,128)(2,1)S(1)}, u32[]{:S(2)}, u32[]{:S(2)}) %collective-permute-start.16) | collective-permute-done | bytes 524320 | tf_op jit(solution)/shard_map/ppermute | solution.py:156
  66.2 4.2 %collective-permute-start.13 = (bf16[128,2048]{1,0:T(8,128)(2,1)S(1)}, bf16[128,2048]{1,0:T(8,128)(2,1)S(1)}, u32[]{:S(2)}, u32[]{:S(2)}) collective-permute-start(bf16[128,2048]{1,0:T(8,128)(2,1)S(1)} %collective-permute-done.11), channel_id=1, source_target_pairs={{0,2},{1,3},{2,0},{3,1},{4,6},{5,7},{6,4},{7,5},{16,18},{17,19},{1... | collective-permute-start | bytes 1572872 | tf_op jit(solution)/shard_map/ppermute | solution.py:156
  70.5 1.9 collective-permute-start.18
  72.5 3.9 %collective-permute-start.8 = (bf16[128,2048]{1,0:T(8,128)(2,1)S(1)}, bf16[128,2048]{1,0:T(8,128)(2,1)S(1)}, u32[]{:S(2)}, u32[]{:S(2)}) collective-permute-start(bf16[128,2048]{1,0:T(8,128)(2,1)S(1)} %collective-permute-done.3), channel_id=1, source_target_pairs={{0,2},{1,3},{2,0},{3,1},{4,6},{5,7},{6,4},{7,5},{8,10},{9,11},{10,... | collective-permute-start | bytes 1572872 | tf_op jit(solution)/shard_map/ppermute | solution.py:156
  76.4 6.8 %collective-permute-done.13 = bf16[128,2048]{1,0:T(8,128)(2,1)S(1)} collective-permute-done((bf16[128,2048]{1,0:T(8,128)(2,1)S(1)}, bf16[128,2048]{1,0:T(8,128)(2,1)S(1)}, u32[]{:S(2)}, u32[]{:S(2)}) %collective-permute-start.13) | collective-permute-done | bytes 524320 | tf_op jit(solution)/shard_map/ppermute | solution.py:156
  83.2 0.7 collective-permute-start.9
  84.6 9.9 %collective-permute-done.18 = bf16[128,2048]{1,0:T(8,128)(2,1)S(1)} collective-permute-done((bf16[128,2048]{1,0:T(8,128)(2,1)S(1)}, bf16[128,2048]{1,0:T(8,128)(2,1)S(1)}, u32[]{:S(2)}, u32[]{:S(2)}) %collective-permute-start.18) | collective-permute-done | bytes 524320 | tf_op jit(solution)/shard_map/ppermute | solution.py:156
  94.5 9.0 %collective-permute-done.8 = bf16[128,2048]{1,0:T(8,128)(2,1)S(1)} collective-permute-done((bf16[128,2048]{1,0:T(8,128)(2,1)S(1)}, bf16[128,2048]{1,0:T(8,128)(2,1)S(1)}, u32[]{:S(2)}, u32[]{:S(2)}) %collective-permute-start.8) | collective-permute-done | bytes 524320 | tf_op jit(solution)/shard_map/ppermute | solution.py:156
  104.8 1.0 copy-done
  109.6 27.7 %shard_map.72.out_ref = bf16[8,4,48,2048]{3,2,1,0:T(8,128)(2,1)} custom-call(bf16[4,48,2048]{2,1,0:T(8,128)(2,1)S(1)} %get-tuple-element.37.refs_0_, bf16[4,48,2048]{2,1,0:T(8,128)(2,1)S(1)} %get-tuple-element.38.refs_1_, bf16[4,48,2048]{2,1,0:T(8,128)(2,1)S(1)} %get-tuple-element.39.refs_2_, bf16[4,48,2048]{2,1,0:T(8,128)(2,1)S(1)} %get-tuple-element.40.refs_3_, ...), custom_call_target="tpu_custom_call" | custom-call | flops 14495514624 | bytes 50331648 | tf_op jit(solution)/shard_map/pallas_call | solution.py:87
  137.3 1.6 shard_map.80
  139.4 1.6 shard_map.79
  141.1 1.6 shard_map.78
  143.3 1.8 collective-permute-start.32
  145.1 1.6 shard_map.77
  146.8 1.6 shard_map.76
  149.5 8.7 %collective-permute-done.32 = bf16[128,2048]{1,0:T(8,128)(2,1)S(1)} collective-permute-done((bf16[128,2048]{1,0:T(8,128)(2,1)S(1)}, bf16[128,2048]{1,0:T(8,128)(2,1)S(1)}, u32[]{:S(2)}, u32[]{:S(2)}) %collective-permute-start.32) | collective-permute-done | bytes 524320 | tf_op jit(solution)/shard_map/ppermute | solution.py:156
  158.4 1.3 collective-permute-start.33
  159.7 1.6 shard_map.75
  161.6 1.8 collective-permute-start.26
  163.4 6.0 %collective-permute-done.29 = bf16[128,2048]{1,0:T(8,128)(2,1)S(1)} collective-permute-done((bf16[128,2048]{1,0:T(8,128)(2,1)S(1)}, bf16[128,2048]{1,0:T(8,128)(2,1)S(1)}, u32[]{:S(2)}, u32[]{:S(2)}) %collective-permute-start.29) | collective-permute-done | bytes 524320 | tf_op jit(solution)/shard_map/ppermute | solution.py:156
  170.1 4.6 %collective-permute-start.34 = (bf16[128,2048]{1,0:T(8,128)(2,1)S(1)}, bf16[128,2048]{1,0:T(8,128)(2,1)S(1)}, u32[]{:S(2)}, u32[]{:S(2)}) collective-permute-start(bf16[128,2048]{1,0:T(8,128)(2,1)S(1)} %add_convert_fusion.4), channel_id=1, source_target_pairs={{0,4},{1,5},{2,6},{3,7},{4,8},{5,9},{6,10},{7,11},{16,20},{17,21},... | collective-permute-start | bytes 1572872 | tf_op jit(solution)/shard_map/ppermute | solution.py:156
  174.7 5.1 %collective-permute-done.26 = bf16[128,2048]{1,0:T(8,128)(2,1)S(1)} collective-permute-done((bf16[128,2048]{1,0:T(8,128)(2,1)S(1)}, bf16[128,2048]{1,0:T(8,128)(2,1)S(1)}, u32[]{:S(2)}, u32[]{:S(2)}) %collective-permute-start.26) | collective-permute-done | bytes 524320 | tf_op jit(solution)/shard_map/ppermute | solution.py:156
  179.8 3.8 %collective-permute-done.34 = bf16[128,2048]{1,0:T(8,128)(2,1)S(1)} collective-permute-done((bf16[128,2048]{1,0:T(8,128)(2,1)S(1)}, bf16[128,2048]{1,0:T(8,128)(2,1)S(1)}, u32[]{:S(2)}, u32[]{:S(2)}) %collective-permute-start.34) | collective-permute-done | bytes 524320 | tf_op jit(solution)/shard_map/ppermute | solution.py:156
  183.9 0.7 collective-permute-start.36
  184.7 1.6 shard_map.74
  186.7 0.7 collective-permute-start.37
  187.4 1.6 shard_map.73
  189.7 1.8 collective-permute-start.23
  191.5 5.0 %collective-permute-start.35 = (bf16[128,2048]{1,0:T(8,128)(2,1)S(1)}, bf16[128,2048]{1,0:T(8,128)(2,1)S(1)}, u32[]{:S(2)}, u32[]{:S(2)}) collective-permute-start(bf16[128,2048]{1,0:T(8,128)(2,1)S(1)} %get-tuple-element.71), channel_id=1, source_target_pairs={{0,4},{1,5},{2,6},{3,7},{4,8},{5,9},{6,10},{7,11},{8,12},{9,13},{1... | collective-permute-start | bytes 1572872 | tf_op jit(solution)/shard_map/ppermute | solution.py:156
  196.8 1.3 collective-permute-start.38
  198.1 5.4 %collective-permute-done.23 = bf16[128,2048]{1,0:T(8,128)(2,1)S(1)} collective-permute-done((bf16[128,2048]{1,0:T(8,128)(2,1)S(1)}, bf16[128,2048]{1,0:T(8,128)(2,1)S(1)}, u32[]{:S(2)}, u32[]{:S(2)}) %collective-permute-start.23) | collective-permute-done | bytes 524320 | tf_op jit(solution)/shard_map/ppermute | solution.py:156
  203.6 3.9 %collective-permute-done.35 = bf16[128,2048]{1,0:T(8,128)(2,1)S(1)} collective-permute-done((bf16[128,2048]{1,0:T(8,128)(2,1)S(1)}, bf16[128,2048]{1,0:T(8,128)(2,1)S(1)}, u32[]{:S(2)}, u32[]{:S(2)}) %collective-permute-start.35) | collective-permute-done | bytes 524320 | tf_op jit(solution)/shard_map/ppermute | solution.py:156
  207.5 14.1 %collective-permute-done.38 = bf16[128,2048]{1,0:T(8,128)(2,1)S(1)} collective-permute-done((bf16[128,2048]{1,0:T(8,128)(2,1)S(1)}, bf16[128,2048]{1,0:T(8,128)(2,1)S(1)}, u32[]{:S(2)}, u32[]{:S(2)}) %collective-permute-start.38) | collective-permute-done | bytes 524320 | tf_op jit(solution)/shard_map/ppermute | solution.py:156
  221.6 1.2 add_convert_fusion
  (87 shorter events, 12.3 us)
Async XLA Ops:
  0.0 84.0 %collective-permute-start.1 = (bf16[128,2048]{1,0:T(8,128)(2,1)}, bf16[128,2048]{1,0:T(8,128)(2,1)S(1)}, u32[]{:S(2)}, u32[]{:S(2)}) collective-permute-start(bf16[128,2048]{1,0:T(8,128)(2,1)} %x0_ref.1), channel_id=1, source_target_pairs={{0,2},{1,3},{2,0},{3,1},{4,6},{5,7},{6,4},{7,5},{8,10},{9,11},{10,... | collective-permute-start | bytes 1572872 | tf_op jit(solution)/shard_map/ppermute | solution.py:156
  3.0 33.2 %collective-permute-start.4 = (bf16[128,2048]{1,0:T(8,128)(2,1)}, bf16[128,2048]{1,0:T(8,128)(2,1)S(1)}, u32[]{:S(2)}, u32[]{:S(2)}) collective-permute-start(bf16[128,2048]{1,0:T(8,128)(2,1)} %x0_ref.1), channel_id=1, source_target_pairs={{0,4},{1,5},{2,6},{3,7},{4,8},{5,9},{6,10},{7,11},{8,12},{9,13},{1... | collective-permute-start | bytes 1572872 | tf_op jit(solution)/shard_map/ppermute | solution.py:156
  6.5 28.4 %collective-permute-start.3 = (bf16[128,2048]{1,0:T(8,128)(2,1)}, bf16[128,2048]{1,0:T(8,128)(2,1)S(1)}, u32[]{:S(2)}, u32[]{:S(2)}) collective-permute-start(bf16[128,2048]{1,0:T(8,128)(2,1)} %x0_ref.1), channel_id=1, source_target_pairs={{4,0},{5,1},{6,2},{7,3},{8,4},{9,5},{10,6},{11,7},{12,8},{13,9},{1... | collective-permute-start | bytes 1572872 | tf_op jit(solution)/shard_map/ppermute | solution.py:156
  34.9 16.1 %collective-permute-start.11 = (bf16[128,2048]{1,0:T(8,128)(2,1)S(1)}, bf16[128,2048]{1,0:T(8,128)(2,1)S(1)}, u32[]{:S(2)}, u32[]{:S(2)}) collective-permute-start(bf16[128,2048]{1,0:T(8,128)(2,1)S(1)} %collective-permute-done.3), channel_id=1, source_target_pairs={{4,0},{5,1},{6,2},{7,3},{8,4},{9,5},{10,6},{11,7},{20,16},{21,17},... | collective-permute-start | bytes 1572872 | tf_op jit(solution)/shard_map/ppermute | solution.py:156
  36.2 16.8 %collective-permute-start.5 = (bf16[128,2048]{1,0:T(8,128)(2,1)S(1)}, bf16[128,2048]{1,0:T(8,128)(2,1)S(1)}, u32[]{:S(2)}, u32[]{:S(2)}) collective-permute-start(bf16[128,2048]{1,0:T(8,128)(2,1)S(1)} %collective-permute-done.4), channel_id=1, source_target_pairs={{4,8},{5,9},{6,10},{7,11},{8,12},{9,13},{10,14},{11,15},{20,24},{2... | collective-permute-start | bytes 1572872 | tf_op jit(solution)/shard_map/ppermute | solution.py:156
  50.9 15.2 %collective-permute-start.16 = (bf16[128,2048]{1,0:T(8,128)(2,1)S(1)}, bf16[128,2048]{1,0:T(8,128)(2,1)S(1)}, u32[]{:S(2)}, u32[]{:S(2)}) collective-permute-start(bf16[128,2048]{1,0:T(8,128)(2,1)S(1)} %collective-permute-done.11), channel_id=1, source_target_pairs={{4,0},{5,1},{6,2},{7,3},{20,16},{21,17},{22,18},{23,19}} | collective-permute-start | bytes 1572872 | tf_op jit(solution)/shard_map/ppermute | solution.py:156
  52.3 31.8 %collective-permute-start.19 = (bf16[128,2048]{1,0:T(8,128)(2,1)S(1)}, bf16[128,2048]{1,0:T(8,128)(2,1)S(1)}, u32[]{:S(2)}, u32[]{:S(2)}) collective-permute-start(bf16[128,2048]{1,0:T(8,128)(2,1)S(1)} %collective-permute-done.4), channel_id=1, source_target_pairs={{4,6},{5,7},{6,4},{7,5},{8,10},{9,11},{10,8},{11,9},{12,14},{13,15... | collective-permute-start | bytes 1572872 | tf_op jit(solution)/shard_map/ppermute | solution.py:156
  53.0 19.5 %collective-permute-start.14 = (bf16[128,2048]{1,0:T(8,128)(2,1)S(1)}, bf16[128,2048]{1,0:T(8,128)(2,1)S(1)}, u32[]{:S(2)}, u32[]{:S(2)}) collective-permute-start(bf16[128,2048]{1,0:T(8,128)(2,1)S(1)} %collective-permute-done.5), channel_id=1, source_target_pairs={{8,10},{9,11},{10,8},{11,9},{12,14},{13,15},{14,12},{15,13},{24,26... | collective-permute-start | bytes 1572872 | tf_op jit(solution)/shard_map/ppermute | solution.py:156
  53.7 16.8 %collective-permute-start.6 = (bf16[128,2048]{1,0:T(8,128)(2,1)S(1)}, bf16[128,2048]{1,0:T(8,128)(2,1)S(1)}, u32[]{:S(2)}, u32[]{:S(2)}) collective-permute-start(bf16[128,2048]{1,0:T(8,128)(2,1)S(1)} %collective-permute-done.5), channel_id=1, source_target_pairs={{8,12},{9,13},{10,14},{11,15},{24,28},{25,29},{26,30},{27,31}} | collective-permute-start | bytes 1572872 | tf_op jit(solution)/shard_map/ppermute | solution.py:156
  66.2 17.0 %collective-permute-start.13 = (bf16[128,2048]{1,0:T(8,128)(2,1)S(1)}, bf16[128,2048]{1,0:T(8,128)(2,1)S(1)}, u32[]{:S(2)}, u32[]{:S(2)}) collective-permute-start(bf16[128,2048]{1,0:T(8,128)(2,1)S(1)} %collective-permute-done.11), channel_id=1, source_target_pairs={{0,2},{1,3},{2,0},{3,1},{4,6},{5,7},{6,4},{7,5},{16,18},{17,19},{1... | collective-permute-start | bytes 1572872 | tf_op jit(solution)/shard_map/ppermute | solution.py:156
  70.5 24.0 %collective-permute-start.18 = (bf16[128,2048]{1,0:T(8,128)(2,1)S(1)}, bf16[128,2048]{1,0:T(8,128)(2,1)S(1)}, u32[]{:S(2)}, u32[]{:S(2)}) collective-permute-start(bf16[128,2048]{1,0:T(8,128)(2,1)S(1)} %collective-permute-done.16), channel_id=1, source_target_pairs={{0,2},{1,3},{2,0},{3,1},{16,18},{17,19},{18,16},{19,17}} | collective-permute-start | bytes 1572872 | tf_op jit(solution)/shard_map/ppermute | solution.py:156
  72.5 31.1 %collective-permute-start.8 = (bf16[128,2048]{1,0:T(8,128)(2,1)S(1)}, bf16[128,2048]{1,0:T(8,128)(2,1)S(1)}, u32[]{:S(2)}, u32[]{:S(2)}) collective-permute-start(bf16[128,2048]{1,0:T(8,128)(2,1)S(1)} %collective-permute-done.3), channel_id=1, source_target_pairs={{0,2},{1,3},{2,0},{3,1},{4,6},{5,7},{6,4},{7,5},{8,10},{9,11},{10,... | collective-permute-start | bytes 1572872 | tf_op jit(solution)/shard_map/ppermute | solution.py:156
  83.2 20.3 %collective-permute-start.9 = (bf16[128,2048]{1,0:T(8,128)(2,1)S(1)}, bf16[128,2048]{1,0:T(8,128)(2,1)S(1)}, u32[]{:S(2)}, u32[]{:S(2)}) collective-permute-start(bf16[128,2048]{1,0:T(8,128)(2,1)S(1)} %collective-permute-done.6), channel_id=1, source_target_pairs={{12,14},{13,15},{14,12},{15,13},{28,30},{29,31},{30,28},{31,29}} | collective-permute-start | bytes 1572872 | tf_op jit(solution)/shard_map/ppermute | solution.py:156
  84.0 20.2 %collective-permute-start = (bf16[128,2048]{1,0:T(8,128)(2,1)}, bf16[128,2048]{1,0:T(8,128)(2,1)S(1)}, u32[]{:S(2)}, u32[]{:S(2)}) collective-permute-start(bf16[128,2048]{1,0:T(8,128)(2,1)} %x0_ref.1), channel_id=1, source_target_pairs={{0,1},{1,0},{2,3},{3,2},{4,5},{5,4},{6,7},{7,6},{8,9},{9,8},{10,11... | collective-permute-start | bytes 1572872 | tf_op jit(solution)/shard_map/ppermute | solution.py:156
  84.1 20.2 %collective-permute-start.2 = (bf16[128,2048]{1,0:T(8,128)(2,1)S(1)}, bf16[128,2048]{1,0:T(8,128)(2,1)S(1)}, u32[]{:S(2)}, u32[]{:S(2)}) collective-permute-start(bf16[128,2048]{1,0:T(8,128)(2,1)S(1)} %collective-permute-done.1.x0_ref), channel_id=1, source_target_pairs={{0,1},{1,0},{2,3},{3,2},{4,5},{5,4},{6,7},{7,6},{8,9},{9,8},{10,11... | collective-permute-start | bytes 1572872 | tf_op jit(solution)/shard_map/ppermute | solution.py:156
  94.4 10.3 %collective-permute-start.12 = (bf16[128,2048]{1,0:T(8,128)(2,1)S(1)}, bf16[128,2048]{1,0:T(8,128)(2,1)S(1)}, u32[]{:S(2)}, u32[]{:S(2)}) collective-permute-start(bf16[128,2048]{1,0:T(8,128)(2,1)S(1)} %broadcast_select_fusion.3.x0_ref), channel_id=1, source_target_pairs={{0,1},{1,0},{2,3},{3,2},{4,5},{5,4},{6,7},{7,6},{8,9},{9,8},{10,11... | collective-permute-start | bytes 1572872 | tf_op jit(solution)/shard_map/ppermute | solution.py:156
  103.5 3.5 %collective-permute-start.7 = (bf16[128,2048]{1,0:T(8,128)(2,1)S(1)}, bf16[128,2048]{1,0:T(8,128)(2,1)S(1)}, u32[]{:S(2)}, u32[]{:S(2)}) collective-permute-start(bf16[128,2048]{1,0:T(8,128)(2,1)S(1)} %broadcast_select_fusion.5.x0_ref), channel_id=1, source_target_pairs={{0,1},{1,0},{2,3},{3,2},{4,5},{5,4},{6,7},{7,6},{8,9},{9,8},{10,11... | collective-permute-start | bytes 1572872 | tf_op jit(solution)/shard_map/ppermute | solution.py:156
  103.6 3.9 %collective-permute-start.17 = (bf16[128,2048]{1,0:T(8,128)(2,1)S(1)}, bf16[128,2048]{1,0:T(8,128)(2,1)S(1)}, u32[]{:S(2)}, u32[]{:S(2)}) collective-permute-start(bf16[128,2048]{1,0:T(8,128)(2,1)S(1)} %broadcast_select_fusion.1.x0_ref), channel_id=1, source_target_pairs={{0,1},{1,0},{2,3},{3,2},{4,5},{5,4},{6,7},{7,6},{8,9},{9,8},{10,11... | collective-permute-start | bytes 1572872 | tf_op jit(solution)/shard_map/ppermute | solution.py:156
  104.1 3.7 %collective-permute-start.15 = (bf16[128,2048]{1,0:T(8,128)(2,1)S(1)}, bf16[128,2048]{1,0:T(8,128)(2,1)S(1)}, u32[]{:S(2)}, u32[]{:S(2)}) collective-permute-start(bf16[128,2048]{1,0:T(8,128)(2,1)S(1)} %broadcast_select_fusion.2.x0_ref), channel_id=1, source_target_pairs={{0,1},{1,0},{2,3},{3,2},{4,5},{5,4},{6,7},{7,6},{8,9},{9,8},{10,11... | collective-permute-start | bytes 1572872 | tf_op jit(solution)/shard_map/ppermute | solution.py:156
  104.2 4.0 %collective-permute-start.20 = (bf16[128,2048]{1,0:T(8,128)(2,1)S(1)}, bf16[128,2048]{1,0:T(8,128)(2,1)S(1)}, u32[]{:S(2)}, u32[]{:S(2)}) collective-permute-start(bf16[128,2048]{1,0:T(8,128)(2,1)S(1)} %broadcast_select_fusion.x0_ref), channel_id=1, source_target_pairs={{0,1},{1,0},{2,3},{3,2},{4,5},{5,4},{6,7},{7,6},{8,9},{9,8},{10,11... | collective-permute-start | bytes 1572872 | tf_op jit(solution)/shard_map/ppermute | solution.py:156
  104.7 3.9 %collective-permute-start.10 = (bf16[128,2048]{1,0:T(8,128)(2,1)S(1)}, bf16[128,2048]{1,0:T(8,128)(2,1)S(1)}, u32[]{:S(2)}, u32[]{:S(2)}) collective-permute-start(bf16[128,2048]{1,0:T(8,128)(2,1)S(1)} %broadcast_select_fusion.4.x0_ref), channel_id=1, source_target_pairs={{0,1},{1,0},{2,3},{3,2},{4,5},{5,4},{6,7},{7,6},{8,9},{9,8},{10,11... | collective-permute-start | bytes 1572872 | tf_op jit(solution)/shard_map/ppermute | solution.py:156
  104.8 1.0 copy-start
  107.8 1.2 copy-start.1
  108.6 1.0 copy-start.2
  138.9 4.3 %collective-permute-start.31 = (bf16[128,2048]{1,0:T(8,128)(2,1)S(1)}, bf16[128,2048]{1,0:T(8,128)(2,1)S(1)}, u32[]{:S(2)}, u32[]{:S(2)}) collective-permute-start(bf16[128,2048]{1,0:T(8,128)(2,1)S(1)} %get-tuple-element.68), channel_id=1, source_target_pairs={{0,1},{1,0},{2,3},{3,2},{4,5},{5,4},{6,7},{7,6},{8,9},{9,8},{10,11... | collective-permute-start | bytes 1572872 | tf_op jit(solution)/shard_map/ppermute | solution.py:156
  141.0 8.5 %collective-permute-start.30 = (bf16[128,2048]{1,0:T(8,128)(2,1)S(1)}, bf16[128,2048]{1,0:T(8,128)(2,1)S(1)}, u32[]{:S(2)}, u32[]{:S(2)}) collective-permute-start(bf16[128,2048]{1,0:T(8,128)(2,1)S(1)} %get-tuple-element.66), channel_id=1, source_target_pairs={{0,1},{1,0},{2,3},{3,2},{4,5},{5,4},{6,7},{7,6},{8,9},{9,8},{10,11... | collective-permute-start | bytes 1572872 | tf_op jit(solution)/shard_map/ppermute | solution.py:156
  142.7 6.3 %collective-permute-start.28 = (bf16[128,2048]{1,0:T(8,128)(2,1)S(1)}, bf16[128,2048]{1,0:T(8,128)(2,1)S(1)}, u32[]{:S(2)}, u32[]{:S(2)}) collective-permute-start(bf16[128,2048]{1,0:T(8,128)(2,1)S(1)} %get-tuple-element.64), channel_id=1, source_target_pairs={{0,1},{1,0},{2,3},{3,2},{4,5},{5,4},{6,7},{7,6},{8,9},{9,8},{10,11... | collective-permute-start | bytes 1572872 | tf_op jit(solution)/shard_map/ppermute | solution.py:156
  143.3 14.8 %collective-permute-start.32 = (bf16[128,2048]{1,0:T(8,128)(2,1)S(1)}, bf16[128,2048]{1,0:T(8,128)(2,1)S(1)}, u32[]{:S(2)}, u32[]{:S(2)}) collective-permute-start(bf16[128,2048]{1,0:T(8,128)(2,1)S(1)} %add_convert_fusion.5), channel_id=1, source_target_pairs={{0,2},{1,3},{2,0},{3,1},{4,6},{5,7},{6,4},{7,5},{8,10},{9,11},{10,... | collective-permute-start | bytes 1572872 | tf_op jit(solution)/shard_map/ppermute | solution.py:156
  146.7 16.6 %collective-permute-start.27 = (bf16[128,2048]{1,0:T(8,128)(2,1)S(1)}, bf16[128,2048]{1,0:T(8,128)(2,1)S(1)}, u32[]{:S(2)}, u32[]{:S(2)}) collective-permute-start(bf16[128,2048]{1,0:T(8,128)(2,1)S(1)} %get-tuple-element.62), channel_id=1, source_target_pairs={{0,1},{1,0},{2,3},{3,2},{4,5},{5,4},{6,7},{7,6},{8,9},{9,8},{10,11... | collective-permute-start | bytes 1572872 | tf_op jit(solution)/shard_map/ppermute | solution.py:156
  148.4 13.0 %collective-permute-start.25 = (bf16[128,2048]{1,0:T(8,128)(2,1)S(1)}, bf16[128,2048]{1,0:T(8,128)(2,1)S(1)}, u32[]{:S(2)}, u32[]{:S(2)}) collective-permute-start(bf16[128,2048]{1,0:T(8,128)(2,1)S(1)} %get-tuple-element.60), channel_id=1, source_target_pairs={{0,1},{1,0},{2,3},{3,2},{4,5},{5,4},{6,7},{7,6},{8,9},{9,8},{10,11... | collective-permute-start | bytes 1572872 | tf_op jit(solution)/shard_map/ppermute | solution.py:156
  149.1 20.3 %collective-permute-start.29 = (bf16[128,2048]{1,0:T(8,128)(2,1)S(1)}, bf16[128,2048]{1,0:T(8,128)(2,1)S(1)}, u32[]{:S(2)}, u32[]{:S(2)}) collective-permute-start(bf16[128,2048]{1,0:T(8,128)(2,1)S(1)} %add_convert_fusion.6), channel_id=1, source_target_pairs={{0,2},{1,3},{2,0},{3,1},{4,6},{5,7},{6,4},{7,5},{8,10},{9,11},{10,... | collective-permute-start | bytes 1572872 | tf_op jit(solution)/shard_map/ppermute | solution.py:156
  158.4 11.3 %collective-permute-start.33 = (bf16[128,2048]{1,0:T(8,128)(2,1)S(1)}, bf16[128,2048]{1,0:T(8,128)(2,1)S(1)}, u32[]{:S(2)}, u32[]{:S(2)}) collective-permute-start(bf16[128,2048]{1,0:T(8,128)(2,1)S(1)} %fusion.1), channel_id=1, source_target_pairs={{0,4},{1,5},{2,6},{3,7},{16,20},{17,21},{18,22},{19,23}} | collective-permute-start | bytes 1572872 | tf_op jit(solution)/shard_map/ppermute | solution.py:156
  161.3 13.3 %collective-permute-start.24 = (bf16[128,2048]{1,0:T(8,128)(2,1)S(1)}, bf16[128,2048]{1,0:T(8,128)(2,1)S(1)}, u32[]{:S(2)}, u32[]{:S(2)}) collective-permute-start(bf16[128,2048]{1,0:T(8,128)(2,1)S(1)} %get-tuple-element.58), channel_id=1, source_target_pairs={{0,1},{1,0},{2,3},{3,2},{4,5},{5,4},{6,7},{7,6},{8,9},{9,8},{10,11... | collective-permute-start | bytes 1572872 | tf_op jit(solution)/shard_map/ppermute | solution.py:156
  161.6 18.2 %collective-permute-start.26 = (bf16[128,2048]{1,0:T(8,128)(2,1)S(1)}, bf16[128,2048]{1,0:T(8,128)(2,1)S(1)}, u32[]{:S(2)}, u32[]{:S(2)}) collective-permute-start(bf16[128,2048]{1,0:T(8,128)(2,1)S(1)} %add_convert_fusion.7), channel_id=1, source_target_pairs={{0,2},{1,3},{2,0},{3,1},{4,6},{5,7},{6,4},{7,5},{8,10},{9,11},{10,... | collective-permute-start | bytes 1572872 | tf_op jit(solution)/shard_map/ppermute | solution.py:156
  170.1 13.5 %collective-permute-start.34 = (bf16[128,2048]{1,0:T(8,128)(2,1)S(1)}, bf16[128,2048]{1,0:T(8,128)(2,1)S(1)}, u32[]{:S(2)}, u32[]{:S(2)}) collective-permute-start(bf16[128,2048]{1,0:T(8,128)(2,1)S(1)} %add_convert_fusion.4), channel_id=1, source_target_pairs={{0,4},{1,5},{2,6},{3,7},{4,8},{5,9},{6,10},{7,11},{16,20},{17,21},... | collective-permute-start | bytes 1572872 | tf_op jit(solution)/shard_map/ppermute | solution.py:156
  183.9 2.4 %collective-permute-start.36 = (bf16[128,2048]{1,0:T(8,128)(2,1)S(1)}, bf16[128,2048]{1,0:T(8,128)(2,1)S(1)}, u32[]{:S(2)}, u32[]{:S(2)}) collective-permute-start(bf16[128,2048]{1,0:T(8,128)(2,1)S(1)} %get-tuple-element.72), channel_id=1, source_target_pairs={{12,8},{13,9},{14,10},{15,11},{28,24},{29,25},{30,26},{31,27}} | collective-permute-start | bytes 1572872 | tf_op jit(solution)/shard_map/ppermute | solution.py:156
  186.2 3.3 %collective-permute-start.22 = (bf16[128,2048]{1,0:T(8,128)(2,1)S(1)}, bf16[128,2048]{1,0:T(8,128)(2,1)S(1)}, u32[]{:S(2)}, u32[]{:S(2)}) collective-permute-start(bf16[128,2048]{1,0:T(8,128)(2,1)S(1)} %get-tuple-element.56), channel_id=1, source_target_pairs={{0,1},{1,0},{2,3},{3,2},{4,5},{5,4},{6,7},{7,6},{8,9},{9,8},{10,11... | collective-permute-start | bytes 1572872 | tf_op jit(solution)/shard_map/ppermute | solution.py:156
  186.7 9.8 %collective-permute-start.37 = (bf16[128,2048]{1,0:T(8,128)(2,1)S(1)}, bf16[128,2048]{1,0:T(8,128)(2,1)S(1)}, u32[]{:S(2)}, u32[]{:S(2)}) collective-permute-start(bf16[128,2048]{1,0:T(8,128)(2,1)S(1)} %add_convert_fusion.2), channel_id=1, source_target_pairs={{8,4},{9,5},{10,6},{11,7},{12,8},{13,9},{14,10},{15,11},{24,20},{2... | collective-permute-start | bytes 1572872 | tf_op jit(solution)/shard_map/ppermute | solution.py:156
  189.0 9.2 %collective-permute-start.21 = (bf16[128,2048]{1,0:T(8,128)(2,1)S(1)}, bf16[128,2048]{1,0:T(8,128)(2,1)S(1)}, u32[]{:S(2)}, u32[]{:S(2)}) collective-permute-start(bf16[128,2048]{1,0:T(8,128)(2,1)S(1)} %get-tuple-element.54), channel_id=1, source_target_pairs={{0,1},{1,0},{2,3},{3,2},{4,5},{5,4},{6,7},{7,6},{8,9},{9,8},{10,11... | collective-permute-start | bytes 1572872 | tf_op jit(solution)/shard_map/ppermute | solution.py:156
  189.7 13.9 %collective-permute-start.23 = (bf16[128,2048]{1,0:T(8,128)(2,1)S(1)}, bf16[128,2048]{1,0:T(8,128)(2,1)S(1)}, u32[]{:S(2)}, u32[]{:S(2)}) collective-permute-start(bf16[128,2048]{1,0:T(8,128)(2,1)S(1)} %add_convert_fusion.8), channel_id=1, source_target_pairs={{0,2},{1,3},{2,0},{3,1},{4,6},{5,7},{6,4},{7,5},{8,10},{9,11},{10,... | collective-permute-start | bytes 1572872 | tf_op jit(solution)/shard_map/ppermute | solution.py:156
  191.5 16.1 %collective-permute-start.35 = (bf16[128,2048]{1,0:T(8,128)(2,1)S(1)}, bf16[128,2048]{1,0:T(8,128)(2,1)S(1)}, u32[]{:S(2)}, u32[]{:S(2)}) collective-permute-start(bf16[128,2048]{1,0:T(8,128)(2,1)S(1)} %get-tuple-element.71), channel_id=1, source_target_pairs={{0,4},{1,5},{2,6},{3,7},{4,8},{5,9},{6,10},{7,11},{8,12},{9,13},{1... | collective-permute-start | bytes 1572872 | tf_op jit(solution)/shard_map/ppermute | solution.py:156
  196.8 24.8 %collective-permute-start.38 = (bf16[128,2048]{1,0:T(8,128)(2,1)S(1)}, bf16[128,2048]{1,0:T(8,128)(2,1)S(1)}, u32[]{:S(2)}, u32[]{:S(2)}) collective-permute-start(bf16[128,2048]{1,0:T(8,128)(2,1)S(1)} %add_convert_fusion.1), channel_id=1, source_target_pairs={{4,0},{5,1},{6,2},{7,3},{8,4},{9,5},{10,6},{11,7},{12,8},{13,9},{1... | collective-permute-start | bytes 1572872 | tf_op jit(solution)/shard_map/ppermute | solution.py:156

commit v2 on v1

v2 whole, which is shorter than its diff:
```python
import functools

import jax
import jax.numpy as jnp
from jax import lax
from jax.experimental import pallas as pl
from jax.experimental.pallas import tpu as pltpu
from jax.sharding import PartitionSpec as P

CAP = 24
CORES = 2
CHUNKS = 2
VMEM_LIMIT = 40 * 1024 * 1024


def params(**kw):
    return pltpu.CompilerParams(vmem_limit_bytes=VMEM_LIMIT, **kw)


def selector(code_ref, local):
    row = jnp.concatenate([code_ref[0, local : local + 1, :], code_ref[1, local : local + 1, :] + CAP], axis=1)
    slots = lax.broadcasted_iota(jnp.int32, (2 * CAP, row.shape[1]), 0)
    return row == slots


def dispatch_kernel(code_ref, wt_ref, x0_ref, x1_ref, rows_ref, weight_ref):
    local_experts = rows_ref.shape[0]
    picks = []
    for local in range(local_experts):
        hit = selector(code_ref, local)
        wt = jnp.concatenate([wt_ref[0, local : local + 1, :], wt_ref[1, local : local + 1, :]], axis=1)
        weight = jnp.sum(jnp.where(hit, wt, 0.0), axis=1, keepdims=True)
        weight_ref[local] = jnp.broadcast_to(weight, weight_ref.shape[1:])
        picks.append(jnp.where(hit, 1.0, 0.0).astype(jnp.bfloat16))
    pick = jnp.concatenate(picks, axis=0)
    x = jnp.concatenate([x0_ref[...], x1_ref[...]], axis=0)
    rows = jnp.dot(pick, x, preferred_element_type=jnp.float32).astype(jnp.bfloat16)
    rows_ref[...] = rows.reshape(rows_ref.shape)


def dispatch(code, wt, x0, x1):
    local_experts = code.shape[1]
    width = x0.shape[1]
    return pl.pallas_call(
        dispatch_kernel,
        out_shape=(
            jax.ShapeDtypeStruct((local_experts, 2 * CAP, width), jnp.bfloat16),
            jax.ShapeDtypeStruct((local_experts, 2 * CAP, 128), jnp.float32),
        ),
        compiler_params=params(),
        cost_estimate=pl.CostEstimate(
            flops=2 * local_experts * 2 * CAP * 2 * x0.shape[0] * width,
            bytes_accessed=2 * width * (2 * x0.shape[0] + local_experts * 2 * CAP),
            transcendentals=0,
        ),
    )(code, wt, x0, x1)


def rows_specs(rows):
    return [pl.BlockSpec((1,) + r.shape[1:], lambda l: (l, 0, 0)) for r in rows]


def joined(refs):
    return jnp.concatenate([r[0] for r in refs], axis=0)


def begin_kernel(pairs, *refs):
    rows = joined(refs[:pairs])
    gate_w, up_w, gate_ref, up_ref = refs[pairs:]
    gate_ref[0] = jnp.dot(rows, gate_w[0], preferred_element_type=jnp.float32)
    up_ref[0] = jnp.dot(rows, up_w[0], preferred_element_type=jnp.float32)


def begin(rows, w_gate, w_up):
    pairs = len(rows)
    local_experts, _, hidden = w_gate.shape
    count, width = pairs * rows[0].shape[1], rows[0].shape[2]
    weight_spec = pl.BlockSpec((1, width, hidden), lambda l: (l, 0, 0))
    sum_spec = pl.BlockSpec((1, count, hidden), lambda l: (l, 0, 0))
    shape = jax.ShapeDtypeStruct((local_experts, count, hidden), jnp.float32)
    return pl.pallas_call(
        functools.partial(begin_kernel, pairs),
        grid=(local_experts,),
        in_specs=rows_specs(rows) + [weight_spec] * 2,
        out_specs=(sum_spec, sum_spec),
        out_shape=(shape, shape),
        compiler_params=params(),
        cost_estimate=pl.CostEstimate(
            flops=4 * local_experts * count * width * hidden,
            bytes_accessed=4 * local_experts * width * hidden + 8 * local_experts * count * hidden,
            transcendentals=0,
        ),
    )(*rows, w_gate, w_up)


def middle_kernel(pairs, *refs):
    rows, weight = joined(refs[:pairs]), jnp.concatenate([r[0, :, :1] for r in refs[pairs : 2 * pairs]], axis=0)
    gate_sum, up_sum, gate_w, up_w, down_w, hidden_ref = refs[2 * pairs : 2 * pairs + 6]
    out_refs = refs[2 * pairs + 6 :]
    gate = gate_sum[0] + jnp.dot(rows, gate_w[0], preferred_element_type=jnp.float32)
    up = up_sum[0] + jnp.dot(rows, up_w[0], preferred_element_type=jnp.float32)
    hidden = (gate / (1.0 + jnp.exp(-gate)) * up * weight).astype(jnp.bfloat16)
    hidden_ref[0] = hidden
    write_out(out_refs, jnp.dot(hidden, down_w[0], preferred_element_type=jnp.float32))


def write_out(out_refs, out):
    out = out.astype(jnp.bfloat16)
    for p, ref in enumerate(out_refs):
        ref[0] = out[p * 2 * CAP : (p + 1) * 2 * CAP]


def middle(rows, weights, gate_sum, up_sum, w_gate, w_up, w_down):
    pairs = len(rows)
    local_experts, _, hidden = w_gate.shape
    count, width = pairs * rows[0].shape[1], rows[0].shape[2]
    weight_spec = pl.BlockSpec((1, width, hidden), lambda l: (l, 1, 0))
    sum_spec = pl.BlockSpec((1, count, hidden), lambda l: (l, 0, 0))
    out_shapes = [jax.ShapeDtypeStruct((local_experts, 2 * CAP, width), jnp.bfloat16)] * pairs
    got = pl.pallas_call(
        functools.partial(middle_kernel, pairs),
        grid=(local_experts,),
        in_specs=rows_specs(rows)
        + rows_specs(weights)
        + [sum_spec] * 2
        + [weight_spec] * 2
        + [pl.BlockSpec((1, hidden, width), lambda l: (l, 0, 0))],
        out_specs=[sum_spec] + rows_specs(out_shapes),
        out_shape=[jax.ShapeDtypeStruct((local_experts, count, hidden), jnp.bfloat16)] + out_shapes,
        compiler_params=params(),
        cost_estimate=pl.CostEstimate(
            flops=6 * local_experts * count * width * hidden,
            bytes_accessed=6 * local_experts * width * hidden + 8 * local_experts * count * hidden,
            transcendentals=local_experts * count * hidden,
        ),
    )(*rows, *weights, gate_sum, up_sum, w_gate, w_up, w_down)
    return got[0], got[1:]


def finish_kernel(hidden_ref, down_w, *out_refs):
    write_out(out_refs, jnp.dot(hidden_ref[0], down_w[0], preferred_element_type=jnp.float32))


def finish(hidden, w_down, width, pairs):
    local_experts, count, depth = hidden.shape
    out_shapes = [jax.ShapeDtypeStruct((local_experts, 2 * CAP, width), jnp.bfloat16)] * pairs
    return pl.pallas_call(
        finish_kernel,
        grid=(local_experts,),
        in_specs=[
            pl.BlockSpec((1, count, depth), lambda l: (l, 0, 0)),
            pl.BlockSpec((1, depth, width), lambda l: (l, 0, 1)),
        ],
        out_specs=rows_specs(out_shapes),
        out_shape=out_shapes,
        compiler_params=params(),
        cost_estimate=pl.CostEstimate(
            flops=2 * local_experts * count * width * depth,
            bytes_accessed=2 * local_experts * (width * depth + count * depth + count * width),
            transcendentals=0,
        ),
    )(hidden, w_down)


def combine_kernel(code_ref, out_ref, y0_ref, y1_ref):
    local_experts, slots, width = out_ref.shape
    pick = jnp.concatenate(
        [jnp.where(selector(code_ref, l), 1.0, 0.0).astype(jnp.bfloat16) for l in range(local_experts)], axis=0
    )
    out = out_ref[...].reshape(local_experts * slots, width)
    y = lax.dot_general(pick, out, (((0,), (0,)), ((), ())), preferred_element_type=jnp.float32)
    y0_ref[...] = y[: y0_ref.shape[0]]
    y1_ref[...] = y[y0_ref.shape[0] :].astype(jnp.bfloat16)


def combine(code, results):
    local_experts, slots, width = results.shape
    tok = code.shape[2]
    return pl.pallas_call(
        combine_kernel,
        out_shape=(
            jax.ShapeDtypeStruct((tok, width), jnp.float32),
            jax.ShapeDtypeStruct((tok, width), jnp.bfloat16),
        ),
        compiler_params=params(),
        cost_estimate=pl.CostEstimate(
            flops=4 * local_experts * slots * tok * width,
            bytes_accessed=2 * width * (3 * tok + local_experts * slots),
            transcendentals=0,
        ),
    )(code, results)


def body(depth, lines, tokens, expert_ids, route_weight, w_gate, w_up, w_down):
    tok, width = tokens.shape
    local_experts = w_gate.shape[0]
    index = lax.axis_index("exp")
    owners = depth * lines * CORES
    part = width // CHUNKS

    def place(pz, py, pc):
        return (pz % depth * lines + py) * CORES + pc

    everyone = [(a, b, c) for a in range(depth) for b in range(lines) for c in range(CORES)]

    def send(value, move):
        return lax.ppermute(value, "exp", [(place(*who), place(*move(*who))) for who in everyone])

    def swap_core(value):
        return send(value, lambda a, b, c: (a, b, 1 - c))

    def swap_line(value):
        return send(value, lambda a, b, c: (a, 1 - b, c))

    def to_above(value):
        return send(value, lambda a, b, c: (a + 1, b, c))

    def to_below(value):
        return send(value, lambda a, b, c: (a - 1, b, c))

    table = jnp.concatenate([expert_ids.T.astype(jnp.float32), route_weight.T], axis=0)[None]
    bit = 1
    while bit < owners:
        table = jnp.concatenate(
            [table, lax.ppermute(table, "exp", [(i, i ^ bit) for i in range(owners)])], axis=0
        )
        bit *= 2
    z, y, core = index // (lines * CORES), index // CORES % lines, index % CORES
    source = jnp.stack([place(z + r, y ^ b, core ^ c) ^ index for r, b, c in everyone])
    table = jnp.take(table, source, axis=0)
    top = expert_ids.shape[1]
    mine = (index * local_experts + jnp.arange(local_experts, dtype=jnp.int32)).astype(jnp.float32)
    hit = table[:, None, :top, :] == mine[None, :, None, None]
    member = jnp.sum(hit.astype(jnp.float32), axis=2)
    wt = jnp.sum(jnp.where(hit, table[:, None, top:, :], 0.0), axis=2)
    before = jnp.triu(jnp.ones((tok, tok), jnp.bfloat16), 1)
    rank = jnp.einsum("nlt,tu->nlu", member.astype(jnp.bfloat16), before, preferred_element_type=jnp.float32)
    code = jnp.where(member > 0.0, rank.astype(jnp.int32), -1024)

    nearer = depth // 2
    line = [[tokens[:, c * part : (c + 1) * part] for c in range(CHUNKS)]] + [None] * (depth - 1)
    far = [None] * depth

    def chunked(move, values):
        return [move(v) for v in values]

    turns = []
    for d in range(1, nearer + 1):
        turns.append((d, d - 1, to_below))
        if depth - d > nearer:
            turns.append((depth - d, (depth - d + 1) % depth, to_above))
    if lines > 1:
        far[0] = chunked(swap_line, line[0])
    for r, before_r, move in turns:
        line[r] = chunked(move, line[before_r])
        if lines > 1:
            far[r] = chunked(swap_line, line[r])
    rows, weights = [[] for _ in range(CHUNKS)], []
    codes = [code[2 * p : 2 * p + 2] for p in range(owners // CORES)]
    wts = [wt[2 * p : 2 * p + 2] for p in range(owners // CORES)]
    for p in range(owners // CORES):
        piece = line[p // lines] if p % lines == 0 else far[p // lines]
        for c in range(CHUNKS):
            a, w = dispatch(codes[p], wts[p], piece[c], swap_core(piece[c]))
            rows[c].append(a)
            if c == 0:
                weights.append(w)

    gate_sum, up_sum = begin(rows[0], w_gate, w_up)
    hidden, out0 = middle(rows[1], weights, gate_sum, up_sum, w_gate, w_up, w_down)
    results = [out0, finish(hidden, w_down, part, len(weights))]

    wide = jnp.float32
    link = jnp.bfloat16 if depth <= 4 else wide
    mixed = []
    for c in range(CHUNKS):

        def across(r):
            halves = []
            for b in reversed(range(lines)):
                p = r * lines + b
                y0, y1 = combine(codes[p], results[c][p])
                halves.append(y0 + swap_core(y1).astype(wide))
            if lines > 1:
                return halves[1] + swap_line(halves[0].astype(jnp.bfloat16)).astype(wide)
            return halves[0]

        got_up = got_down = 0.0
        for d in range(nearer, 0, -1):
            got_up = to_above((across(d) + got_up).astype(link)).astype(wide)
            if depth - d > nearer:
                got_down = to_below((across(depth - d) + got_down).astype(link)).astype(wide)
        mixed.append((across(0) + got_up + got_down).astype(jnp.bfloat16))
    return jnp.concatenate(mixed, axis=1)


def solution(mesh):
    groups, owners = mesh.shape["grp"], mesh.shape["exp"]
    lines = max(1, 4 // groups)
    depth = owners // (lines * CORES)
    in_specs = (
        P(("grp", "exp"), None),
        P(("grp", "exp"), None),
        P(("grp", "exp"), None),
        P("exp", None, None),
        P("exp", None, None),
        P("exp", None, None),
    )
    out_specs = P(("grp", "exp"), None)
    return jax.shard_map(
        functools.partial(body, depth, lines),
        mesh=mesh,
        in_specs=in_specs,
        out_specs=out_specs,
        check_vma=False,
    )
```

time: 224 us -> 177 us (0.79)
  blocking collectives: 24.6 us -> 0 us
  waiting for transfers between devices: 98.6 us -> 83.8 us
  Pallas kernels: 43.4 us -> 39.4 us
  starting transfers between devices: 47.4 us -> 44.4 us
    all_gather x1 -> x0, blocking collectives: 24.6 us -> none  [body(): table = lax.all_gather(table, 'exp', axis=0)]
    ppermute x39 -> x64, waiting for transfers between devices: 98.6 us -> 83.8 us  [the longest x60 72 us: send(): lax.ppermute(value, 'exp', [(place(*who), place(*move(*who))) for who in...]
    pallas_call x9 -> x19, Pallas kernels: 40.4 us -> 30.4 us  [the longest x1 11.8 us: middle(): pl.pallas_call(functools.partial(middle_kernel, pairs), grid=(local_exper...]
    pallas_call x8 -> x16, Pallas kernels: 3.07 us -> 9 us  [dispatch(): pl.pallas_call(dispatch_kernel, out_shape=(jax.ShapeDtypeStruct((local_ex...]
    ppermute x39 -> x64, starting transfers between devices: 47.4 us -> 44.4 us  [the longest x60 42.5 us: send(): lax.ppermute(value, 'exp', [(place(*who), place(*move(*who))) for who in...]
  transfers between devices with their start and end apart: 39 -> 64, of which waited for: 13 -> 26; matrix products, arithmetic and copies ran while one was open for 2% -> 3% of each run, Pallas kernels for 6% -> 15%
where the time goes in v2:
time: 177 us
  waiting for transfers between devices  83.8 us (47%)
  starting transfers between devices  44.4 us (25%)
  Pallas kernels  39.4 us (22%)
  other arithmetic  4.87 us (3%)
  local copies, waits for them, and re-layouts  4.03 us (2%)
    ppermute x60, waiting for transfers between devices, send(): lax.ppermute(value, 'exp', [(place(*who), place(*move(*who))) for who in...  72 us
    ppermute x60, starting transfers between devices, send(): lax.ppermute(value, 'exp', [(place(*who), place(*move(*who))) for who in...  42.5 us
    ppermute x4, waiting for transfers between devices, body(): lax.ppermute(table, 'exp', [(i, i ^ bit) for i in range(owners)])  11.8 us
    pallas_call x1, Pallas kernels, middle(): pl.pallas_call(functools.partial(middle_kernel, pairs), grid=(local_exper...  11.8 us
    pallas_call x16, Pallas kernels, dispatch(): pl.pallas_call(dispatch_kernel, out_shape=(jax.ShapeDtypeStruct((local_ex...  9 us
    pallas_call x1, Pallas kernels, begin(): pl.pallas_call(functools.partial(begin_kernel, pairs), grid=(local_expert...  8.28 us
    pallas_call x1, Pallas kernels, finish(): pl.pallas_call(finish_kernel, grid=(local_experts,), in_specs=[pl.BlockSp...  5.31 us
    pallas_call x16, Pallas kernels, combine(): pl.pallas_call(combine_kernel, out_shape=(jax.ShapeDtypeStruct((tok, widt...  5.08 us
  transfers between devices with their start and end apart: 64, of which 26 were waited for; matrix products, arithmetic and copies ran while one was open for 3% of the time, Pallas kernels for 15%

profile of v2, /device:TPU:0, one launch (start us, length us, event | category | flops | bytes accessed | tf_op | source)
XLA Modules:
  0.0 177.2 jit_solution(2484328691505126664)
XLA Ops:
  0.0 1.1 fusion.13
  1.1 3.1 %collective-permute-start.30 = (bf16[128,1024]{1,0:T(8,128)(2,1)S(1)}, bf16[128,1024]{1,0:T(8,128)(2,1)S(1)}, u32[]{:S(2)}, u32[]{:S(2)}) collective-permute-start(bf16[128,1024]{1,0:T(8,128)(2,1)S(1)} %get-tuple-element.157.x0_ref), channel_id=1, source_target_pairs={{0,4},{1,5},{2,6},{3,7},{4,8},{5,9},{6,10},{7,11},{8,12},{9,13},{1... | collective-permute-start | bytes 786440 | tf_op jit(solution)/shard_map/ppermute | solution.py:207
  4.1 2.1 %collective-permute-start.22 = (bf16[128,1024]{1,0:T(8,128)(2,1)S(1)}, bf16[128,1024]{1,0:T(8,128)(2,1)S(1)}, u32[]{:S(2)}, u32[]{:S(2)}) collective-permute-start(bf16[128,1024]{1,0:T(8,128)(2,1)S(1)} %get-tuple-element.157.x0_ref), channel_id=1, source_target_pairs={{0,12},{1,13},{2,14},{3,15},{4,0},{5,1},{6,2},{7,3},{8,4},{9,5},{1... | collective-permute-start | bytes 786440 | tf_op jit(solution)/shard_map/ppermute | solution.py:207
  6.2 1.7 collective-permute-start.20
  11.1 3.4 %collective-permute-done.1 = f32[2,16,128]{2,1,0:T(8,128)S(1)} collective-permute-done((f32[2,16,128]{2,1,0:T(8,128)S(1)}, f32[2,16,128]{2,1,0:T(8,128)S(1)}, u32[]{:S(2)}, u32[]{:S(2)}) %collective-permute-start.1) | collective-permute-done | bytes 16416 | tf_op jit(solution)/shard_map/ppermute | solution.py:225
  14.5 3.9 %collective-permute-done.2 = f32[4,16,128]{2,1,0:T(8,128)S(1)} collective-permute-done((f32[4,16,128]{2,1,0:T(8,128)S(1)}, f32[4,16,128]{2,1,0:T(8,128)S(1)}, u32[]{:S(2)}, u32[]{:S(2)}) %collective-permute-start.2) | collective-permute-done | bytes 32800 | tf_op jit(solution)/shard_map/ppermute | solution.py:225
  18.4 1.0 collective-permute-start.3
  19.4 4.5 %collective-permute-done.3 = f32[8,16,128]{2,1,0:T(8,128)S(1)} collective-permute-done((f32[8,16,128]{2,1,0:T(8,128)S(1)}, f32[8,16,128]{2,1,0:T(8,128)S(1)}, u32[]{:S(2)}, u32[]{:S(2)}) %collective-permute-start.3) | collective-permute-done | bytes 65568 | tf_op jit(solution)/shard_map/ppermute | solution.py:225
  23.9 3.8 %collective-permute-start.7 = (bf16[128,1024]{1,0:T(8,128)(2,1)S(1)}, bf16[128,1024]{1,0:T(8,128)(2,1)S(1)}, u32[]{:S(2)}, u32[]{:S(2)}) collective-permute-start(bf16[128,1024]{1,0:T(8,128)(2,1)S(1)} %get-tuple-element.158.x0_ref), channel_id=1, source_target_pairs={{0,12},{1,13},{2,14},{3,15},{4,0},{5,1},{6,2},{7,3},{8,4},{9,5},{1... | collective-permute-start | bytes 786440 | tf_op jit(solution)/shard_map/ppermute | solution.py:207
  27.8 1.5 collective-permute-start.5
  30.5 4.5 %collective-permute-done.15.x0_ref = bf16[128,1024]{1,0:T(8,128)(2,1)S(1)} collective-permute-done((bf16[128,1024]{1,0:T(8,128)(2,1)S(1)}, bf16[128,1024]{1,0:T(8,128)(2,1)S(1)}, u32[]{:S(2)}, u32[]{:S(2)}) %collective-permute-start.15) | collective-permute-done | bytes 262176 | tf_op jit(solution)/shard_map/ppermute | solution.py:207
  35.0 1.9 %collective-permute-done.7.x0_ref = bf16[128,1024]{1,0:T(8,128)(2,1)S(1)} collective-permute-done((bf16[128,1024]{1,0:T(8,128)(2,1)S(1)}, bf16[128,1024]{1,0:T(8,128)(2,1)S(1)}, u32[]{:S(2)}, u32[]{:S(2)}) %collective-permute-start.7) | collective-permute-done | bytes 262176 | tf_op jit(solution)/shard_map/ppermute | solution.py:207
  36.9 2.1 %collective-permute-start.26 = (bf16[128,1024]{1,0:T(8,128)(2,1)S(1)}, bf16[128,1024]{1,0:T(8,128)(2,1)S(1)}, u32[]{:S(2)}, u32[]{:S(2)}) collective-permute-start(bf16[128,1024]{1,0:T(8,128)(2,1)S(1)} %collective-permute-done.22.x0_ref), channel_id=1, source_target_pairs={{0,12},{1,13},{2,14},{3,15},{4,0},{5,1},{6,2},{7,3},{8,4},{9,5},{1... | collective-permute-start | bytes 786440 | tf_op jit(solution)/shard_map/ppermute | solution.py:207
  39.0 1.5 collective-permute-start.24
  41.1 1.1 collective-permute-start.17
  42.2 1.5 collective-permute-done.26.x0_ref
  43.7 3.9 %collective-permute-done.24.x0_ref = bf16[128,1024]{1,0:T(8,128)(2,1)S(1)} collective-permute-done((bf16[128,1024]{1,0:T(8,128)(2,1)S(1)}, bf16[128,1024]{1,0:T(8,128)(2,1)S(1)}, u32[]{:S(2)}, u32[]{:S(2)}) %collective-permute-start.24) | collective-permute-done | bytes 262176 | tf_op jit(solution)/shard_map/ppermute | solution.py:207
  47.6 1.0 collective-permute-start.11
  48.7 2.5 %collective-permute-start.9 = (bf16[128,1024]{1,0:T(8,128)(2,1)S(1)}, bf16[128,1024]{1,0:T(8,128)(2,1)S(1)}, u32[]{:S(2)}, u32[]{:S(2)}) collective-permute-start(bf16[128,1024]{1,0:T(8,128)(2,1)S(1)} %collective-permute-done.7.x0_ref), channel_id=1, source_target_pairs={{0,2},{1,3},{2,0},{3,1},{4,6},{5,7},{6,4},{7,5},{8,10},{9,11},{10,... | collective-permute-start | bytes 786440 | tf_op jit(solution)/shard_map/ppermute | solution.py:207
  51.5 0.9 collective-permute-done.17.x0_ref
  52.4 1.5 collective-permute-start.28
  54.2 4.2 %collective-permute-done.9.x0_ref = bf16[128,1024]{1,0:T(8,128)(2,1)S(1)} collective-permute-done((bf16[128,1024]{1,0:T(8,128)(2,1)S(1)}, bf16[128,1024]{1,0:T(8,128)(2,1)S(1)}, u32[]{:S(2)}, u32[]{:S(2)}) %collective-permute-start.9) | collective-permute-done | bytes 262176 | tf_op jit(solution)/shard_map/ppermute | solution.py:207
  58.9 1.6 collective-permute-start.13
  60.6 3.0 %collective-permute-done.28.x0_ref = bf16[128,1024]{1,0:T(8,128)(2,1)S(1)} collective-permute-done((bf16[128,1024]{1,0:T(8,128)(2,1)S(1)}, bf16[128,1024]{1,0:T(8,128)(2,1)S(1)}, u32[]{:S(2)}, u32[]{:S(2)}) %collective-permute-start.28) | collective-permute-done | bytes 262176 | tf_op jit(solution)/shard_map/ppermute | solution.py:207
  64.5 0.9 shard_map.64
  67.9 0.9 shard_map.65
  72.9 8.3 %shard_map.80 = (f32[4,384,768]{2,1,0:T(8,128)S(1)}, f32[4,384,768]{2,1,0:T(8,128)S(1)}) custom-call(bf16[4,48,1024]{2,1,0:T(8,128)(2,1)S(1)} %get-tuple-element.96.refs_0_, bf16[4,48,1024]{2,1,0:T(8,128)(2,1)S(1)} %get-tuple-element.97.refs_1_, bf16[4,48,1024]{2,1,0:T(8,128)(2,1)S(1)} %get-tuple-element.98.refs_2_, ...), custom_call_target="tpu_custom_call" | custom-call | flops 4831838208 | bytes 22020096 | tf_op jit(solution)/shard_map/pallas_call | solution.py:81
  81.2 2.2 %copy-done = f32[4,384,768]{2,1,0:T(8,128)} copy-done((f32[4,384,768]{2,1,0:T(8,128)}, f32[4,384,768]{2,1,0:T(8,128)S(1)}, u32[]{:S(2)}) %copy-start) | copy-done | bytes 4718616
  84.2 11.8 %shard_map.81 = (bf16[4,384,768]{2,1,0:T(8,128)(2,1)S(1)}, bf16[4,48,1024]{2,1,0:T(8,128)(2,1)S(1)}, bf16[4,48,1024]{2,1,0:T(8,128)(2,1)S(1)}, bf16[4,48,1024]{2...) custom-call(bf16[4,48,1024]{2,1,0:T(8,128)(2,1)S(1)} %get-tuple-elem, ...), custom_call_target="tpu_custom_call" | custom-call | flops 7247757312 | bytes 28311552 | tf_op jit(solution)/shard_map/pallas_call | solution.py:120
  100.0 5.3 %shard_map.90 = (bf16[4,48,1024]{2,1,0:T(8,128)(2,1)S(1)}, bf16[4,48,1024]{2,1,0:T(8,128)(2,1)S(1)}, bf16[4,48,1024]{2,1,0:T(8,128)(2,1)S(1)}, bf16[4,48,1024]{2...) custom-call(bf16[4,384,768]{2,1,0:T(8,128)(2,1)S(1)} %get-tuple-elem, ...), custom_call_target="tpu_custom_call" | custom-call | flops 2415919104 | bytes 11796480 | tf_op jit(solution)/shard_map/pallas_call | solution.py:147
  112.0 1.5 collective-permute-start.42
  113.6 1.1 collective-permute-start.47
  114.8 6.3 %collective-permute-done.42 = bf16[128,1024]{1,0:T(8,128)(2,1)S(1)} collective-permute-done((bf16[128,1024]{1,0:T(8,128)(2,1)S(1)}, bf16[128,1024]{1,0:T(8,128)(2,1)S(1)}, u32[]{:S(2)}, u32[]{:S(2)}) %collective-permute-start.42) | collective-permute-done | bytes 262176 | tf_op jit(solution)/shard_map/ppermute | solution.py:207
  121.1 1.5 collective-permute-start.57
  122.8 3.9 %collective-permute-done.47 = bf16[128,1024]{1,0:T(8,128)(2,1)S(1)} collective-permute-done((bf16[128,1024]{1,0:T(8,128)(2,1)S(1)}, bf16[128,1024]{1,0:T(8,128)(2,1)S(1)}, u32[]{:S(2)}, u32[]{:S(2)}) %collective-permute-start.47) | collective-permute-done | bytes 262176 | tf_op jit(solution)/shard_map/ppermute | solution.py:207
  126.7 1.5 collective-permute-start.62
  129.0 3.4 %collective-permute-done.57 = bf16[128,1024]{1,0:T(8,128)(2,1)S(1)} collective-permute-done((bf16[128,1024]{1,0:T(8,128)(2,1)S(1)}, bf16[128,1024]{1,0:T(8,128)(2,1)S(1)}, u32[]{:S(2)}, u32[]{:S(2)}) %collective-permute-start.57) | collective-permute-done | bytes 262176 | tf_op jit(solution)/shard_map/ppermute | solution.py:207
  132.6 5.4 %collective-permute-done.62 = bf16[128,1024]{1,0:T(8,128)(2,1)S(1)} collective-permute-done((bf16[128,1024]{1,0:T(8,128)(2,1)S(1)}, bf16[128,1024]{1,0:T(8,128)(2,1)S(1)}, u32[]{:S(2)}, u32[]{:S(2)}) %collective-permute-start.62) | collective-permute-done | bytes 262176 | tf_op jit(solution)/shard_map/ppermute | solution.py:207
  138.7 4.3 %collective-permute-done.39 = bf16[128,1024]{1,0:T(8,128)(2,1)S(1)} collective-permute-done((bf16[128,1024]{1,0:T(8,128)(2,1)S(1)}, bf16[128,1024]{1,0:T(8,128)(2,1)S(1)}, u32[]{:S(2)}, u32[]{:S(2)}) %collective-permute-start.39) | collective-permute-done | bytes 262176 | tf_op jit(solution)/shard_map/ppermute | solution.py:207
  142.9 1.5 collective-permute-start.54
  145.2 7.0 %collective-permute-done.54 = bf16[128,1024]{1,0:T(8,128)(2,1)S(1)} collective-permute-done((bf16[128,1024]{1,0:T(8,128)(2,1)S(1)}, bf16[128,1024]{1,0:T(8,128)(2,1)S(1)}, u32[]{:S(2)}, u32[]{:S(2)}) %collective-permute-start.54) | collective-permute-done | bytes 262176 | tf_op jit(solution)/shard_map/ppermute | solution.py:207
  152.2 1.0 collective-permute-start.48
  153.2 2.3 %collective-permute-done.58 = bf16[128,1024]{1,0:T(8,128)(2,1)S(1)} collective-permute-done((bf16[128,1024]{1,0:T(8,128)(2,1)S(1)}, bf16[128,1024]{1,0:T(8,128)(2,1)S(1)}, u32[]{:S(2)}, u32[]{:S(2)}) %collective-permute-start.58) | collective-permute-done | bytes 262176 | tf_op jit(solution)/shard_map/ppermute | solution.py:207
  156.2 1.5 collective-permute-done.36
  157.7 2.3 %collective-permute-start.63 = (bf16[128,1024]{1,0:T(8,128)(2,1)S(1)}, bf16[128,1024]{1,0:T(8,128)(2,1)S(1)}, u32[]{:S(2)}, u32[]{:S(2)}) collective-permute-start(bf16[128,1024]{1,0:T(8,128)(2,1)S(1)} %add_convert_fusion.1), channel_id=1, source_target_pairs={{0,12},{1,13},{2,14},{3,15},{4,0},{5,1},{6,2},{7,3},{8,4},{9,5},{1... | collective-permute-start | bytes 786440 | tf_op jit(solution)/shard_map/ppermute | solution.py:207
  160.0 6.8 %collective-permute-done.48 = bf16[128,1024]{1,0:T(8,128)(2,1)S(1)} collective-permute-done((bf16[128,1024]{1,0:T(8,128)(2,1)S(1)}, bf16[128,1024]{1,0:T(8,128)(2,1)S(1)}, u32[]{:S(2)}, u32[]{:S(2)}) %collective-permute-start.48) | collective-permute-done | bytes 262176 | tf_op jit(solution)/shard_map/ppermute | solution.py:207
  167.1 5.3 %collective-permute-done.63 = bf16[128,1024]{1,0:T(8,128)(2,1)S(1)} collective-permute-done((bf16[128,1024]{1,0:T(8,128)(2,1)S(1)}, bf16[128,1024]{1,0:T(8,128)(2,1)S(1)}, u32[]{:S(2)}, u32[]{:S(2)}) %collective-permute-start.63) | collective-permute-done | bytes 262176 | tf_op jit(solution)/shard_map/ppermute | solution.py:207
  172.4 3.8 %collective-permute-done.59 = bf16[128,1024]{1,0:T(8,128)(2,1)S(1)} collective-permute-done((bf16[128,1024]{1,0:T(8,128)(2,1)S(1)}, bf16[128,1024]{1,0:T(8,128)(2,1)S(1)}, u32[]{:S(2)}, u32[]{:S(2)}) %collective-permute-start.59) | collective-permute-done | bytes 262176 | tf_op jit(solution)/shard_map/ppermute | solution.py:207
  (160 shorter events, 29.6 us)
Async XLA Ops:
  1.1 22.9 %collective-permute-start.30 = (bf16[128,1024]{1,0:T(8,128)(2,1)S(1)}, bf16[128,1024]{1,0:T(8,128)(2,1)S(1)}, u32[]{:S(2)}, u32[]{:S(2)}) collective-permute-start(bf16[128,1024]{1,0:T(8,128)(2,1)S(1)} %get-tuple-element.157.x0_ref), channel_id=1, source_target_pairs={{0,4},{1,5},{2,6},{3,7},{4,8},{5,9},{6,10},{7,11},{8,12},{9,13},{1... | collective-permute-start | bytes 786440 | tf_op jit(solution)/shard_map/ppermute | solution.py:207
  4.1 23.6 %collective-permute-start.22 = (bf16[128,1024]{1,0:T(8,128)(2,1)S(1)}, bf16[128,1024]{1,0:T(8,128)(2,1)S(1)}, u32[]{:S(2)}, u32[]{:S(2)}) collective-permute-start(bf16[128,1024]{1,0:T(8,128)(2,1)S(1)} %get-tuple-element.157.x0_ref), channel_id=1, source_target_pairs={{0,12},{1,13},{2,14},{3,15},{4,0},{5,1},{6,2},{7,3},{8,4},{9,5},{1... | collective-permute-start | bytes 786440 | tf_op jit(solution)/shard_map/ppermute | solution.py:207
  6.2 23.1 %collective-permute-start.20 = (bf16[128,1024]{1,0:T(8,128)(2,1)S(1)}, bf16[128,1024]{1,0:T(8,128)(2,1)S(1)}, u32[]{:S(2)}, u32[]{:S(2)}) collective-permute-start(bf16[128,1024]{1,0:T(8,128)(2,1)S(1)} %get-tuple-element.157.x0_ref), channel_id=1, source_target_pairs={{0,2},{1,3},{2,0},{3,1},{4,6},{5,7},{6,4},{7,5},{8,10},{9,11},{10,... | collective-permute-start | bytes 786440 | tf_op jit(solution)/shard_map/ppermute | solution.py:207
  7.9 21.4 %collective-permute-start.19 = (bf16[128,1024]{1,0:T(8,128)(2,1)S(1)}, bf16[128,1024]{1,0:T(8,128)(2,1)S(1)}, u32[]{:S(2)}, u32[]{:S(2)}) collective-permute-start(bf16[128,1024]{1,0:T(8,128)(2,1)S(1)} %get-tuple-element.157.x0_ref), channel_id=1, source_target_pairs={{0,1},{1,0},{2,3},{3,2},{4,5},{5,4},{6,7},{7,6},{8,9},{9,8},{10,11... | collective-permute-start | bytes 786440 | tf_op jit(solution)/shard_map/ppermute | solution.py:207
  23.9 11.0 %collective-permute-start.15 = (bf16[128,1024]{1,0:T(8,128)(2,1)S(1)}, bf16[128,1024]{1,0:T(8,128)(2,1)S(1)}, u32[]{:S(2)}, u32[]{:S(2)}) collective-permute-start(bf16[128,1024]{1,0:T(8,128)(2,1)S(1)} %get-tuple-element.158.x0_ref), channel_id=1, source_target_pairs={{0,4},{1,5},{2,6},{3,7},{4,8},{5,9},{6,10},{7,11},{8,12},{9,13},{1... | collective-permute-start | bytes 786440 | tf_op jit(solution)/shard_map/ppermute | solution.py:207
  23.9 12.9 %collective-permute-start.7 = (bf16[128,1024]{1,0:T(8,128)(2,1)S(1)}, bf16[128,1024]{1,0:T(8,128)(2,1)S(1)}, u32[]{:S(2)}, u32[]{:S(2)}) collective-permute-start(bf16[128,1024]{1,0:T(8,128)(2,1)S(1)} %get-tuple-element.158.x0_ref), channel_id=1, source_target_pairs={{0,12},{1,13},{2,14},{3,15},{4,0},{5,1},{6,2},{7,3},{8,4},{9,5},{1... | collective-permute-start | bytes 786440 | tf_op jit(solution)/shard_map/ppermute | solution.py:207
  27.8 11.2 %collective-permute-start.5 = (bf16[128,1024]{1,0:T(8,128)(2,1)S(1)}, bf16[128,1024]{1,0:T(8,128)(2,1)S(1)}, u32[]{:S(2)}, u32[]{:S(2)}) collective-permute-start(bf16[128,1024]{1,0:T(8,128)(2,1)S(1)} %get-tuple-element.158.x0_ref), channel_id=1, source_target_pairs={{0,2},{1,3},{2,0},{3,1},{4,6},{5,7},{6,4},{7,5},{8,10},{9,11},{10,... | collective-permute-start | bytes 786440 | tf_op jit(solution)/shard_map/ppermute | solution.py:207
  29.3 11.2 %collective-permute-start.4 = (bf16[128,1024]{1,0:T(8,128)(2,1)S(1)}, bf16[128,1024]{1,0:T(8,128)(2,1)S(1)}, u32[]{:S(2)}, u32[]{:S(2)}) collective-permute-start(bf16[128,1024]{1,0:T(8,128)(2,1)S(1)} %get-tuple-element.158.x0_ref), channel_id=1, source_target_pairs={{0,1},{1,0},{2,3},{3,2},{4,5},{5,4},{6,7},{7,6},{8,9},{9,8},{10,11... | collective-permute-start | bytes 786440 | tf_op jit(solution)/shard_map/ppermute | solution.py:207
  29.3 11.2 %collective-permute-start.32 = (bf16[128,1024]{1,0:T(8,128)(2,1)S(1)}, bf16[128,1024]{1,0:T(8,128)(2,1)S(1)}, u32[]{:S(2)}, u32[]{:S(2)}) collective-permute-start(bf16[128,1024]{1,0:T(8,128)(2,1)S(1)} %collective-permute-done.30.x0_ref), channel_id=1, source_target_pairs={{0,2},{1,3},{2,0},{3,1},{4,6},{5,7},{6,4},{7,5},{8,10},{9,11},{10,... | collective-permute-start | bytes 786440 | tf_op jit(solution)/shard_map/ppermute | solution.py:207
  39.0 8.7 %collective-permute-start.24 = (bf16[128,1024]{1,0:T(8,128)(2,1)S(1)}, bf16[128,1024]{1,0:T(8,128)(2,1)S(1)}, u32[]{:S(2)}, u32[]{:S(2)}) collective-permute-start(bf16[128,1024]{1,0:T(8,128)(2,1)S(1)} %collective-permute-done.22.x0_ref), channel_id=1, source_target_pairs={{0,2},{1,3},{2,0},{3,1},{4,6},{5,7},{6,4},{7,5},{8,10},{9,11},{10,... | collective-permute-start | bytes 786440 | tf_op jit(solution)/shard_map/ppermute | solution.py:207
  40.5 8.2 %collective-permute-start.23 = (bf16[128,1024]{1,0:T(8,128)(2,1)S(1)}, bf16[128,1024]{1,0:T(8,128)(2,1)S(1)}, u32[]{:S(2)}, u32[]{:S(2)}) collective-permute-start(bf16[128,1024]{1,0:T(8,128)(2,1)S(1)} %collective-permute-done.22.x0_ref), channel_id=1, source_target_pairs={{0,1},{1,0},{2,3},{3,2},{4,5},{5,4},{6,7},{7,6},{8,9},{9,8},{10,11... | collective-permute-start | bytes 786440 | tf_op jit(solution)/shard_map/ppermute | solution.py:207
  40.5 10.7 %collective-permute-start.21 = (bf16[128,1024]{1,0:T(8,128)(2,1)S(1)}, bf16[128,1024]{1,0:T(8,128)(2,1)S(1)}, u32[]{:S(2)}, u32[]{:S(2)}) collective-permute-start(bf16[128,1024]{1,0:T(8,128)(2,1)S(1)} %collective-permute-done.20.x0_ref), channel_id=1, source_target_pairs={{0,1},{1,0},{2,3},{3,2},{4,5},{5,4},{6,7},{7,6},{8,9},{9,8},{10,11... | collective-permute-start | bytes 786440 | tf_op jit(solution)/shard_map/ppermute | solution.py:207
  41.1 11.3 %collective-permute-start.17 = (bf16[128,1024]{1,0:T(8,128)(2,1)S(1)}, bf16[128,1024]{1,0:T(8,128)(2,1)S(1)}, u32[]{:S(2)}, u32[]{:S(2)}) collective-permute-start(bf16[128,1024]{1,0:T(8,128)(2,1)S(1)} %collective-permute-done.15.x0_ref), channel_id=1, source_target_pairs={{0,2},{1,3},{2,0},{3,1},{4,6},{5,7},{6,4},{7,5},{8,10},{9,11},{10,... | collective-permute-start | bytes 786440 | tf_op jit(solution)/shard_map/ppermute | solution.py:207
  43.7 8.7 %collective-permute-start.16 = (bf16[128,1024]{1,0:T(8,128)(2,1)S(1)}, bf16[128,1024]{1,0:T(8,128)(2,1)S(1)}, u32[]{:S(2)}, u32[]{:S(2)}) collective-permute-start(bf16[128,1024]{1,0:T(8,128)(2,1)S(1)} %collective-permute-done.15.x0_ref), channel_id=1, source_target_pairs={{0,1},{1,0},{2,3},{3,2},{4,5},{5,4},{6,7},{7,6},{8,9},{9,8},{10,11... | collective-permute-start | bytes 786440 | tf_op jit(solution)/shard_map/ppermute | solution.py:207
  48.7 9.7 %collective-permute-start.9 = (bf16[128,1024]{1,0:T(8,128)(2,1)S(1)}, bf16[128,1024]{1,0:T(8,128)(2,1)S(1)}, u32[]{:S(2)}, u32[]{:S(2)}) collective-permute-start(bf16[128,1024]{1,0:T(8,128)(2,1)S(1)} %collective-permute-done.7.x0_ref), channel_id=1, source_target_pairs={{0,2},{1,3},{2,0},{3,1},{4,6},{5,7},{6,4},{7,5},{8,10},{9,11},{10,... | collective-permute-start | bytes 786440 | tf_op jit(solution)/shard_map/ppermute | solution.py:207
  51.2 7.2 %collective-permute-start.8 = (bf16[128,1024]{1,0:T(8,128)(2,1)S(1)}, bf16[128,1024]{1,0:T(8,128)(2,1)S(1)}, u32[]{:S(2)}, u32[]{:S(2)}) collective-permute-start(bf16[128,1024]{1,0:T(8,128)(2,1)S(1)} %collective-permute-done.7.x0_ref), channel_id=1, source_target_pairs={{0,1},{1,0},{2,3},{3,2},{4,5},{5,4},{6,7},{7,6},{8,9},{9,8},{10,11... | collective-permute-start | bytes 786440 | tf_op jit(solution)/shard_map/ppermute | solution.py:207
  52.4 11.2 %collective-permute-start.28 = (bf16[128,1024]{1,0:T(8,128)(2,1)S(1)}, bf16[128,1024]{1,0:T(8,128)(2,1)S(1)}, u32[]{:S(2)}, u32[]{:S(2)}) collective-permute-start(bf16[128,1024]{1,0:T(8,128)(2,1)S(1)} %collective-permute-done.26.x0_ref), channel_id=1, source_target_pairs={{0,2},{1,3},{2,0},{3,1},{4,6},{5,7},{6,4},{7,5},{8,10},{9,11},{10,... | collective-permute-start | bytes 786440 | tf_op jit(solution)/shard_map/ppermute | solution.py:207
  54.0 9.6 %collective-permute-start.27 = (bf16[128,1024]{1,0:T(8,128)(2,1)S(1)}, bf16[128,1024]{1,0:T(8,128)(2,1)S(1)}, u32[]{:S(2)}, u32[]{:S(2)}) collective-permute-start(bf16[128,1024]{1,0:T(8,128)(2,1)S(1)} %collective-permute-done.26.x0_ref), channel_id=1, source_target_pairs={{0,1},{1,0},{2,3},{3,2},{4,5},{5,4},{6,7},{7,6},{8,9},{9,8},{10,11... | collective-permute-start | bytes 786440 | tf_op jit(solution)/shard_map/ppermute | solution.py:207
  58.9 10.9 %collective-permute-start.13 = (bf16[128,1024]{1,0:T(8,128)(2,1)S(1)}, bf16[128,1024]{1,0:T(8,128)(2,1)S(1)}, u32[]{:S(2)}, u32[]{:S(2)}) collective-permute-start(bf16[128,1024]{1,0:T(8,128)(2,1)S(1)} %collective-permute-done.11.x0_ref), channel_id=1, source_target_pairs={{0,2},{1,3},{2,0},{3,1},{4,6},{5,7},{6,4},{7,5},{8,10},{9,11},{10,... | collective-permute-start | bytes 786440 | tf_op jit(solution)/shard_map/ppermute | solution.py:207
  60.5 10.0 %collective-permute-start.12 = (bf16[128,1024]{1,0:T(8,128)(2,1)S(1)}, bf16[128,1024]{1,0:T(8,128)(2,1)S(1)}, u32[]{:S(2)}, u32[]{:S(2)}) collective-permute-start(bf16[128,1024]{1,0:T(8,128)(2,1)S(1)} %collective-permute-done.11.x0_ref), channel_id=1, source_target_pairs={{0,1},{1,0},{2,3},{3,2},{4,5},{5,4},{6,7},{7,6},{8,9},{9,8},{10,11... | collective-permute-start | bytes 786440 | tf_op jit(solution)/shard_map/ppermute | solution.py:207
  63.6 7.8 %collective-permute-start.25 = (bf16[128,1024]{1,0:T(8,128)(2,1)S(1)}, bf16[128,1024]{1,0:T(8,128)(2,1)S(1)}, u32[]{:S(2)}, u32[]{:S(2)}) collective-permute-start(bf16[128,1024]{1,0:T(8,128)(2,1)S(1)} %collective-permute-done.24.x0_ref), channel_id=1, source_target_pairs={{0,1},{1,0},{2,3},{3,2},{4,5},{5,4},{6,7},{7,6},{8,9},{9,8},{10,11... | collective-permute-start | bytes 786440 | tf_op jit(solution)/shard_map/ppermute | solution.py:207
  63.6 8.1 %collective-permute-start.10 = (bf16[128,1024]{1,0:T(8,128)(2,1)S(1)}, bf16[128,1024]{1,0:T(8,128)(2,1)S(1)}, u32[]{:S(2)}, u32[]{:S(2)}) collective-permute-start(bf16[128,1024]{1,0:T(8,128)(2,1)S(1)} %collective-permute-done.9.x0_ref), channel_id=1, source_target_pairs={{0,1},{1,0},{2,3},{3,2},{4,5},{5,4},{6,7},{7,6},{8,9},{9,8},{10,11... | collective-permute-start | bytes 786440 | tf_op jit(solution)/shard_map/ppermute | solution.py:207
  64.1 8.5 %collective-permute-start.29 = (bf16[128,1024]{1,0:T(8,128)(2,1)S(1)}, bf16[128,1024]{1,0:T(8,128)(2,1)S(1)}, u32[]{:S(2)}, u32[]{:S(2)}) collective-permute-start(bf16[128,1024]{1,0:T(8,128)(2,1)S(1)} %collective-permute-done.28.x0_ref), channel_id=1, source_target_pairs={{0,1},{1,0},{2,3},{3,2},{4,5},{5,4},{6,7},{7,6},{8,9},{9,8},{10,11... | collective-permute-start | bytes 786440 | tf_op jit(solution)/shard_map/ppermute | solution.py:207
  69.9 13.5 %collective-permute-start.14 = (bf16[128,1024]{1,0:T(8,128)(2,1)S(1)}, bf16[128,1024]{1,0:T(8,128)(2,1)S(1)}, u32[]{:S(2)}, u32[]{:S(2)}) collective-permute-start(bf16[128,1024]{1,0:T(8,128)(2,1)S(1)} %collective-permute-done.13.x0_ref), channel_id=1, source_target_pairs={{0,1},{1,0},{2,3},{3,2},{4,5},{5,4},{6,7},{7,6},{8,9},{9,8},{10,11... | collective-permute-start | bytes 786440 | tf_op jit(solution)/shard_map/ppermute | solution.py:207
  96.6 11.3 %collective-permute-start.35 = (bf16[128,1024]{1,0:T(8,128)(2,1)S(1)}, bf16[128,1024]{1,0:T(8,128)(2,1)S(1)}, u32[]{:S(2)}, u32[]{:S(2)}) collective-permute-start(bf16[128,1024]{1,0:T(8,128)(2,1)S(1)} %get-tuple-element.111), channel_id=1, source_target_pairs={{0,1},{1,0},{2,3},{3,2},{4,5},{5,4},{6,7},{7,6},{8,9},{9,8},{10,11... | collective-permute-start | bytes 786440 | tf_op jit(solution)/shard_map/ppermute | solution.py:207
  97.1 41.0 %collective-permute-start.37 = (bf16[128,1024]{1,0:T(8,128)(2,1)S(1)}, bf16[128,1024]{1,0:T(8,128)(2,1)S(1)}, u32[]{:S(2)}, u32[]{:S(2)}) collective-permute-start(bf16[128,1024]{1,0:T(8,128)(2,1)S(1)} %get-tuple-element.114), channel_id=1, source_target_pairs={{0,1},{1,0},{2,3},{3,2},{4,5},{5,4},{6,7},{7,6},{8,9},{9,8},{10,11... | collective-permute-start | bytes 786440 | tf_op jit(solution)/shard_map/ppermute | solution.py:207
  97.9 10.6 %collective-permute-start.38 = (bf16[128,1024]{1,0:T(8,128)(2,1)S(1)}, bf16[128,1024]{1,0:T(8,128)(2,1)S(1)}, u32[]{:S(2)}, u32[]{:S(2)}) collective-permute-start(bf16[128,1024]{1,0:T(8,128)(2,1)S(1)} %get-tuple-element.117), channel_id=1, source_target_pairs={{0,1},{1,0},{2,3},{3,2},{4,5},{5,4},{6,7},{7,6},{8,9},{9,8},{10,11... | collective-permute-start | bytes 786440 | tf_op jit(solution)/shard_map/ppermute | solution.py:207
  98.3 16.4 %collective-permute-start.40 = (bf16[128,1024]{1,0:T(8,128)(2,1)S(1)}, bf16[128,1024]{1,0:T(8,128)(2,1)S(1)}, u32[]{:S(2)}, u32[]{:S(2)}) collective-permute-start(bf16[128,1024]{1,0:T(8,128)(2,1)S(1)} %get-tuple-element.120), channel_id=1, source_target_pairs={{0,1},{1,0},{2,3},{3,2},{4,5},{5,4},{6,7},{7,6},{8,9},{9,8},{10,11... | collective-permute-start | bytes 786440 | tf_op jit(solution)/shard_map/ppermute | solution.py:207
  99.2 9.5 %collective-permute-start.41 = (bf16[128,1024]{1,0:T(8,128)(2,1)S(1)}, bf16[128,1024]{1,0:T(8,128)(2,1)S(1)}, u32[]{:S(2)}, u32[]{:S(2)}) collective-permute-start(bf16[128,1024]{1,0:T(8,128)(2,1)S(1)} %get-tuple-element.123), channel_id=1, source_target_pairs={{0,1},{1,0},{2,3},{3,2},{4,5},{5,4},{6,7},{7,6},{8,9},{9,8},{10,11... | collective-permute-start | bytes 786440 | tf_op jit(solution)/shard_map/ppermute | solution.py:207
  107.9 14.8 %collective-permute-start.45 = (bf16[128,1024]{1,0:T(8,128)(2,1)S(1)}, bf16[128,1024]{1,0:T(8,128)(2,1)S(1)}, u32[]{:S(2)}, u32[]{:S(2)}) collective-permute-start(bf16[128,1024]{1,0:T(8,128)(2,1)S(1)} %get-tuple-element.126), channel_id=1, source_target_pairs={{0,1},{1,0},{2,3},{3,2},{4,5},{5,4},{6,7},{7,6},{8,9},{9,8},{10,11... | collective-permute-start | bytes 786440 | tf_op jit(solution)/shard_map/ppermute | solution.py:207
  112.0 9.1 %collective-permute-start.42 = (bf16[128,1024]{1,0:T(8,128)(2,1)S(1)}, bf16[128,1024]{1,0:T(8,128)(2,1)S(1)}, u32[]{:S(2)}, u32[]{:S(2)}) collective-permute-start(bf16[128,1024]{1,0:T(8,128)(2,1)S(1)} %add_convert_fusion.13), channel_id=1, source_target_pairs={{0,2},{1,3},{2,0},{3,1},{4,6},{5,7},{6,4},{7,5},{8,10},{9,11},{10,... | collective-permute-start | bytes 786440 | tf_op jit(solution)/shard_map/ppermute | solution.py:207
  113.6 13.2 %collective-permute-start.47 = (bf16[128,1024]{1,0:T(8,128)(2,1)S(1)}, bf16[128,1024]{1,0:T(8,128)(2,1)S(1)}, u32[]{:S(2)}, u32[]{:S(2)}) collective-permute-start(bf16[128,1024]{1,0:T(8,128)(2,1)S(1)} %add_convert_fusion.10), channel_id=1, source_target_pairs={{0,2},{1,3},{2,0},{3,1},{4,6},{5,7},{6,4},{7,5},{8,10},{9,11},{10,... | collective-permute-start | bytes 786440 | tf_op jit(solution)/shard_map/ppermute | solution.py:207
  114.7 13.6 %collective-permute-start.55 = (bf16[128,1024]{1,0:T(8,128)(2,1)S(1)}, bf16[128,1024]{1,0:T(8,128)(2,1)S(1)}, u32[]{:S(2)}, u32[]{:S(2)}) collective-permute-start(bf16[128,1024]{1,0:T(8,128)(2,1)S(1)} %get-tuple-element.145), channel_id=1, source_target_pairs={{0,1},{1,0},{2,3},{3,2},{4,5},{5,4},{6,7},{7,6},{8,9},{9,8},{10,11... | collective-permute-start | bytes 786440 | tf_op jit(solution)/shard_map/ppermute | solution.py:207
  121.1 11.2 %collective-permute-start.57 = (bf16[128,1024]{1,0:T(8,128)(2,1)S(1)}, bf16[128,1024]{1,0:T(8,128)(2,1)S(1)}, u32[]{:S(2)}, u32[]{:S(2)}) collective-permute-start(bf16[128,1024]{1,0:T(8,128)(2,1)S(1)} %add_convert_fusion.5), channel_id=1, source_target_pairs={{0,2},{1,3},{2,0},{3,1},{4,6},{5,7},{6,4},{7,5},{8,10},{9,11},{10,... | collective-permute-start | bytes 786440 | tf_op jit(solution)/shard_map/ppermute | solution.py:207
  122.7 9.8 %collective-permute-start.60 = (bf16[128,1024]{1,0:T(8,128)(2,1)S(1)}, bf16[128,1024]{1,0:T(8,128)(2,1)S(1)}, u32[]{:S(2)}, u32[]{:S(2)}) collective-permute-start(bf16[128,1024]{1,0:T(8,128)(2,1)S(1)} %get-tuple-element.151), channel_id=1, source_target_pairs={{0,1},{1,0},{2,3},{3,2},{4,5},{5,4},{6,7},{7,6},{8,9},{9,8},{10,11... | collective-permute-start | bytes 786440 | tf_op jit(solution)/shard_map/ppermute | solution.py:207
  126.7 11.2 %collective-permute-start.62 = (bf16[128,1024]{1,0:T(8,128)(2,1)S(1)}, bf16[128,1024]{1,0:T(8,128)(2,1)S(1)}, u32[]{:S(2)}, u32[]{:S(2)}) collective-permute-start(bf16[128,1024]{1,0:T(8,128)(2,1)S(1)} %add_convert_fusion.2), channel_id=1, source_target_pairs={{0,2},{1,3},{2,0},{3,1},{4,6},{5,7},{6,4},{7,5},{8,10},{9,11},{10,... | collective-permute-start | bytes 786440 | tf_op jit(solution)/shard_map/ppermute | solution.py:207
  128.3 14.6 %collective-permute-start.39 = (bf16[128,1024]{1,0:T(8,128)(2,1)S(1)}, bf16[128,1024]{1,0:T(8,128)(2,1)S(1)}, u32[]{:S(2)}, u32[]{:S(2)}) collective-permute-start(bf16[128,1024]{1,0:T(8,128)(2,1)S(1)} %add_convert_fusion.14), channel_id=1, source_target_pairs={{0,2},{1,3},{2,0},{3,1},{4,6},{5,7},{6,4},{7,5},{8,10},{9,11},{10,... | collective-permute-start | bytes 786440 | tf_op jit(solution)/shard_map/ppermute | solution.py:207
  132.4 12.1 %collective-permute-start.43 = (bf16[128,1024]{1,0:T(8,128)(2,1)S(1)}, bf16[128,1024]{1,0:T(8,128)(2,1)S(1)}, u32[]{:S(2)}, u32[]{:S(2)}) collective-permute-start(bf16[128,1024]{1,0:T(8,128)(2,1)S(1)} %add_convert_fusion.12), channel_id=1, source_target_pairs={{0,4},{1,5},{2,6},{3,7},{4,8},{5,9},{6,10},{7,11},{8,12},{9,13},{1... | collective-permute-start | bytes 786440 | tf_op jit(solution)/shard_map/ppermute | solution.py:207
  132.5 23.2 %collective-permute-start.34 = (bf16[128,1024]{1,0:T(8,128)(2,1)S(1)}, bf16[128,1024]{1,0:T(8,128)(2,1)S(1)}, u32[]{:S(2)}, u32[]{:S(2)}) collective-permute-start(bf16[128,1024]{1,0:T(8,128)(2,1)S(1)} %get-tuple-element.108), channel_id=1, source_target_pairs={{0,1},{1,0},{2,3},{3,2},{4,5},{5,4},{6,7},{7,6},{8,9},{9,8},{10,11... | collective-permute-start | bytes 786440 | tf_op jit(solution)/shard_map/ppermute | solution.py:207
  138.0 29.1 %collective-permute-start.49 = (bf16[128,1024]{1,0:T(8,128)(2,1)S(1)}, bf16[128,1024]{1,0:T(8,128)(2,1)S(1)}, u32[]{:S(2)}, u32[]{:S(2)}) collective-permute-start(bf16[128,1024]{1,0:T(8,128)(2,1)S(1)} %get-tuple-element.133), channel_id=1, source_target_pairs={{0,1},{1,0},{2,3},{3,2},{4,5},{5,4},{6,7},{7,6},{8,9},{9,8},{10,11... | collective-permute-start | bytes 786440 | tf_op jit(solution)/shard_map/ppermute | solution.py:207
  142.9 9.2 %collective-permute-start.54 = (bf16[128,1024]{1,0:T(8,128)(2,1)S(1)}, bf16[128,1024]{1,0:T(8,128)(2,1)S(1)}, u32[]{:S(2)}, u32[]{:S(2)}) collective-permute-start(bf16[128,1024]{1,0:T(8,128)(2,1)S(1)} %add_convert_fusion.6), channel_id=1, source_target_pairs={{0,2},{1,3},{2,0},{3,1},{4,6},{5,7},{6,4},{7,5},{8,10},{9,11},{10,... | collective-permute-start | bytes 786440 | tf_op jit(solution)/shard_map/ppermute | solution.py:207
  144.4 11.1 %collective-permute-start.58 = (bf16[128,1024]{1,0:T(8,128)(2,1)S(1)}, bf16[128,1024]{1,0:T(8,128)(2,1)S(1)}, u32[]{:S(2)}, u32[]{:S(2)}) collective-permute-start(bf16[128,1024]{1,0:T(8,128)(2,1)S(1)} %add_convert_fusion.4), channel_id=1, source_target_pairs={{0,4},{1,5},{2,6},{3,7},{4,8},{5,9},{6,10},{7,11},{8,12},{9,13},{1... | collective-permute-start | bytes 786440 | tf_op jit(solution)/shard_map/ppermute | solution.py:207
  144.6 13.1 %collective-permute-start.36 = (bf16[128,1024]{1,0:T(8,128)(2,1)S(1)}, bf16[128,1024]{1,0:T(8,128)(2,1)S(1)}, u32[]{:S(2)}, u32[]{:S(2)}) collective-permute-start(bf16[128,1024]{1,0:T(8,128)(2,1)S(1)} %add_convert_fusion.15), channel_id=1, source_target_pairs={{0,2},{1,3},{2,0},{3,1},{4,6},{5,7},{6,4},{7,5},{8,10},{9,11},{10,... | collective-permute-start | bytes 786440 | tf_op jit(solution)/shard_map/ppermute | solution.py:207
  152.2 14.7 %collective-permute-start.48 = (bf16[128,1024]{1,0:T(8,128)(2,1)S(1)}, bf16[128,1024]{1,0:T(8,128)(2,1)S(1)}, u32[]{:S(2)}, u32[]{:S(2)}) collective-permute-start(bf16[128,1024]{1,0:T(8,128)(2,1)S(1)} %add_convert_fusion.9), channel_id=1, source_target_pairs={{0,12},{1,13},{2,14},{3,15},{4,0},{5,1},{6,2},{7,3},{8,4},{9,5},{1... | collective-permute-start | bytes 786440 | tf_op jit(solution)/shard_map/ppermute | solution.py:207
  155.5 11.4 %collective-permute-start.44 = (bf16[128,1024]{1,0:T(8,128)(2,1)S(1)}, bf16[128,1024]{1,0:T(8,128)(2,1)S(1)}, u32[]{:S(2)}, u32[]{:S(2)}) collective-permute-start(bf16[128,1024]{1,0:T(8,128)(2,1)S(1)} %add_convert_fusion.11), channel_id=1, source_target_pairs={{0,4},{1,5},{2,6},{3,7},{4,8},{5,9},{6,10},{7,11},{8,12},{9,13},{1... | collective-permute-start | bytes 786440 | tf_op jit(solution)/shard_map/ppermute | solution.py:207
  155.7 11.4 %collective-permute-start.51 = (bf16[128,1024]{1,0:T(8,128)(2,1)S(1)}, bf16[128,1024]{1,0:T(8,128)(2,1)S(1)}, u32[]{:S(2)}, u32[]{:S(2)}) collective-permute-start(bf16[128,1024]{1,0:T(8,128)(2,1)S(1)} %add_convert_fusion.7), channel_id=1, source_target_pairs={{0,2},{1,3},{2,0},{3,1},{4,6},{5,7},{6,4},{7,5},{8,10},{9,11},{10,... | collective-permute-start | bytes 786440 | tf_op jit(solution)/shard_map/ppermute | solution.py:207
  157.7 14.8 %collective-permute-start.63 = (bf16[128,1024]{1,0:T(8,128)(2,1)S(1)}, bf16[128,1024]{1,0:T(8,128)(2,1)S(1)}, u32[]{:S(2)}, u32[]{:S(2)}) collective-permute-start(bf16[128,1024]{1,0:T(8,128)(2,1)S(1)} %add_convert_fusion.1), channel_id=1, source_target_pairs={{0,12},{1,13},{2,14},{3,15},{4,0},{5,1},{6,2},{7,3},{8,4},{9,5},{1... | collective-permute-start | bytes 786440 | tf_op jit(solution)/shard_map/ppermute | solution.py:207
  166.9 9.3 %collective-permute-start.59 = (bf16[128,1024]{1,0:T(8,128)(2,1)S(1)}, bf16[128,1024]{1,0:T(8,128)(2,1)S(1)}, u32[]{:S(2)}, u32[]{:S(2)}) collective-permute-start(bf16[128,1024]{1,0:T(8,128)(2,1)S(1)} %add_convert_fusion.3), channel_id=1, source_target_pairs={{0,4},{1,5},{2,6},{3,7},{4,8},{5,9},{6,10},{7,11},{8,12},{9,13},{1... | collective-permute-start | bytes 786440 | tf_op jit(solution)/shard_map/ppermute | solution.py:207
  (17 other events, 65.4 us)

commit v3 on v2

v3 whole, which is shorter than its diff:
```python
import functools

import jax
import jax.numpy as jnp
from jax import lax
from jax.experimental import pallas as pl
from jax.experimental.pallas import tpu as pltpu
from jax.sharding import PartitionSpec as P

CAP = 24
CORES = 2
LANES = 128
VMEM_LIMIT = 40 * 1024 * 1024


def params(**kw):
    return pltpu.CompilerParams(vmem_limit_bytes=VMEM_LIMIT, **kw)


def selector(code_ref, local):
    row = jnp.concatenate([code_ref[0, local : local + 1, :], code_ref[1, local : local + 1, :] + CAP], axis=1)
    slots = lax.broadcasted_iota(jnp.int32, (2 * CAP, row.shape[1]), 0)
    return row == slots


def picks(code_ref):
    hits = [selector(code_ref, local) for local in range(code_ref.shape[1])]
    return jnp.concatenate([jnp.where(hit, 1.0, 0.0).astype(jnp.bfloat16) for hit in hits], axis=0)


def with_routes(tokens, expert_ids, route_weight):
    high = route_weight.astype(jnp.bfloat16)
    rest = route_weight - high.astype(jnp.float32)
    middle = rest.astype(jnp.bfloat16)
    low = (rest - middle.astype(jnp.float32)).astype(jnp.bfloat16)
    routes = jnp.concatenate([expert_ids.astype(jnp.bfloat16), high, middle, low], axis=1)
    return jnp.concatenate([jnp.pad(routes, ((0, 0), (0, LANES - routes.shape[1]))), tokens], axis=1)


def dispatch_kernel(top, first_ref, x0_ref, x1_ref, rows_ref, code_ref, weight_ref):
    local_experts = rows_ref.shape[0]
    tok = x0_ref.shape[0]
    first = first_ref[0]
    members, wts = [], []
    for x_ref in (x0_ref, x1_ref):
        routes = x_ref[:, :LANES].astype(jnp.float32).T
        ids = routes[:top].astype(jnp.int32)
        wt = routes[top : 2 * top] + (routes[2 * top : 3 * top] + routes[3 * top : 4 * top])
        for local in range(local_experts):
            hit = ids == first + local
            members.append(jnp.sum(jnp.where(hit, 1.0, 0.0), axis=0, keepdims=True))
            wts.append(jnp.sum(jnp.where(hit, wt, 0.0), axis=0, keepdims=True))
    pad = -len(members) % 16
    member = jnp.concatenate(members + [jnp.zeros((pad, tok), jnp.float32)] * (pad > 0), axis=0)
    before = lax.broadcasted_iota(jnp.int32, (tok, tok), 0) < lax.broadcasted_iota(jnp.int32, (tok, tok), 1)
    rank = jnp.dot(
        member.astype(jnp.bfloat16),
        jnp.where(before, 1.0, 0.0).astype(jnp.bfloat16),
        preferred_element_type=jnp.float32,
    )
    code = jnp.where(member > 0.0, rank.astype(jnp.int32), -1024)
    for i in range(2):
        for local in range(local_experts):
            n = i * local_experts + local
            code_ref[i, local : local + 1, :] = code[n : n + 1]
    for local in range(local_experts):
        wt = jnp.concatenate([wts[local], wts[local_experts + local]], axis=1)
        weight = jnp.sum(jnp.where(selector(code_ref, local), wt, 0.0), axis=1, keepdims=True)
        weight_ref[local] = jnp.broadcast_to(weight, weight_ref.shape[1:])
    pick_rows(code_ref, x0_ref[:, LANES:], x1_ref[:, LANES:], rows_ref)


def pick_rows(code_ref, x0, x1, rows_ref):
    x = jnp.concatenate([x0, x1], axis=0)
    rows = jnp.dot(picks(code_ref), x, preferred_element_type=jnp.float32).astype(jnp.bfloat16)
    rows_ref[...] = rows.reshape(rows_ref.shape)


def more_kernel(code_ref, x0_ref, x1_ref, rows_ref):
    pick_rows(code_ref, x0_ref[...], x1_ref[...], rows_ref)


def pick_cost(local_experts, tok, width):
    return pl.CostEstimate(
        flops=8 * local_experts * CAP * tok * width,
        bytes_accessed=4 * width * (tok + local_experts * CAP),
        transcendentals=0,
    )


def dispatch(first, top, local_experts, x0, x1):
    tok, width = x0.shape[0], x0.shape[1] - LANES
    whole = pl.BlockSpec(memory_space=pltpu.VMEM)
    return pl.pallas_call(
        functools.partial(dispatch_kernel, top),
        in_specs=[pl.BlockSpec(memory_space=pltpu.SMEM), whole, whole],
        out_specs=(whole,) * 3,
        out_shape=(
            jax.ShapeDtypeStruct((local_experts, 2 * CAP, width), jnp.bfloat16),
            jax.ShapeDtypeStruct((2, local_experts, tok), jnp.int32),
            jax.ShapeDtypeStruct((local_experts, 2 * CAP, LANES), jnp.float32),
        ),
        compiler_params=params(),
        cost_estimate=pick_cost(local_experts, tok, width),
    )(first, x0, x1)


def dispatch_more(code, x0, x1):
    local_experts, width = code.shape[1], x0.shape[1]
    return pl.pallas_call(
        more_kernel,
        out_shape=jax.ShapeDtypeStruct((local_experts, 2 * CAP, width), jnp.bfloat16),
        compiler_params=params(),
        cost_estimate=pick_cost(local_experts, x0.shape[0], width),
    )(code, x0, x1)


def column_specs(rows, part, chunk):
    def spec(r):
        at = chunk if r.shape[2] > part else 0
        return pl.BlockSpec((1, r.shape[1], part), lambda l: (l, 0, at))

    return [spec(r) for r in rows]


def rows_specs(rows):
    return [pl.BlockSpec((1,) + r.shape[1:], lambda l: (l, 0, 0)) for r in rows]


def joined(refs):
    return jnp.concatenate([r[0] for r in refs], axis=0)


def begin_kernel(pairs, *refs):
    rows = joined(refs[:pairs])
    gate_w, up_w, gate_ref, up_ref = refs[pairs:]
    gate_ref[0] = jnp.dot(rows, gate_w[0], preferred_element_type=jnp.float32)
    up_ref[0] = jnp.dot(rows, up_w[0], preferred_element_type=jnp.float32)


def begin(rows, width, w_gate, w_up):
    pairs = len(rows)
    local_experts, _, hidden = w_gate.shape
    count = pairs * rows[0].shape[1]
    weight_spec = pl.BlockSpec((1, width, hidden), lambda l: (l, 0, 0))
    sum_spec = pl.BlockSpec((1, count, hidden), lambda l: (l, 0, 0))
    shape = jax.ShapeDtypeStruct((local_experts, count, hidden), jnp.float32)
    return pl.pallas_call(
        functools.partial(begin_kernel, pairs),
        grid=(local_experts,),
        in_specs=column_specs(rows, width, 0) + [weight_spec] * 2,
        out_specs=(sum_spec, sum_spec),
        out_shape=(shape, shape),
        compiler_params=params(),
        cost_estimate=pl.CostEstimate(
            flops=4 * local_experts * count * width * hidden,
            bytes_accessed=4 * local_experts * width * hidden + 8 * local_experts * count * hidden,
            transcendentals=0,
        ),
    )(*rows, w_gate, w_up)


def middle_kernel(pairs, *refs):
    rows, weight = joined(refs[:pairs]), jnp.concatenate([r[0, :, :1] for r in refs[pairs : 2 * pairs]], axis=0)
    gate_sum, up_sum, gate_w, up_w, down_w, hidden_ref = refs[2 * pairs : 2 * pairs + 6]
    out_refs = refs[2 * pairs + 6 :]
    gate = gate_sum[0] + jnp.dot(rows, gate_w[0], preferred_element_type=jnp.float32)
    up = up_sum[0] + jnp.dot(rows, up_w[0], preferred_element_type=jnp.float32)
    hidden = (gate / (1.0 + jnp.exp(-gate)) * up * weight).astype(jnp.bfloat16)
    hidden_ref[0] = hidden
    write_out(out_refs, jnp.dot(hidden, down_w[0], preferred_element_type=jnp.float32))


def write_out(out_refs, out):
    out = out.astype(jnp.bfloat16)
    for p, ref in enumerate(out_refs):
        ref[0] = out[p * 2 * CAP : (p + 1) * 2 * CAP]


def middle(rows, width, weights, gate_sum, up_sum, w_gate, w_up, w_down):
    pairs = len(rows)
    local_experts, _, hidden = w_gate.shape
    count = pairs * rows[0].shape[1]
    weight_spec = pl.BlockSpec((1, width, hidden), lambda l: (l, 1, 0))
    sum_spec = pl.BlockSpec((1, count, hidden), lambda l: (l, 0, 0))
    out_shapes = [jax.ShapeDtypeStruct((local_experts, 2 * CAP, width), jnp.bfloat16)] * pairs
    got = pl.pallas_call(
        functools.partial(middle_kernel, pairs),
        grid=(local_experts,),
        in_specs=column_specs(rows, width, 1)
        + rows_specs(weights)
        + [sum_spec] * 2
        + [weight_spec] * 2
        + [pl.BlockSpec((1, hidden, width), lambda l: (l, 0, 0))],
        out_specs=[sum_spec] + rows_specs(out_shapes),
        out_shape=[jax.ShapeDtypeStruct((local_experts, count, hidden), jnp.bfloat16)] + out_shapes,
        compiler_params=params(),
        cost_estimate=pl.CostEstimate(
            flops=6 * local_experts * count * width * hidden,
            bytes_accessed=6 * local_experts * width * hidden + 8 * local_experts * count * hidden,
            transcendentals=local_experts * count * hidden,
        ),
    )(*rows, *weights, gate_sum, up_sum, w_gate, w_up, w_down)
    return got[0], got[1:]


def finish_kernel(hidden_ref, down_w, *out_refs):
    write_out(out_refs, jnp.dot(hidden_ref[0], down_w[0], preferred_element_type=jnp.float32))


def finish(hidden, w_down, width, pairs):
    local_experts, count, depth = hidden.shape
    out_shapes = [jax.ShapeDtypeStruct((local_experts, 2 * CAP, width), jnp.bfloat16)] * pairs
    return pl.pallas_call(
        finish_kernel,
        grid=(local_experts,),
        in_specs=[
            pl.BlockSpec((1, count, depth), lambda l: (l, 0, 0)),
            pl.BlockSpec((1, depth, width), lambda l: (l, 0, 1)),
        ],
        out_specs=rows_specs(out_shapes),
        out_shape=out_shapes,
        compiler_params=params(),
        cost_estimate=pl.CostEstimate(
            flops=2 * local_experts * count * width * depth,
            bytes_accessed=2 * local_experts * (width * depth + count * depth + count * width),
            transcendentals=0,
        ),
    )(hidden, w_down)


def combine_kernel(code_ref, *refs):
    out_refs, (y0_ref, y1_ref) = refs[:-2], refs[-2:]
    pick = picks(code_ref)
    for i, out_ref in enumerate(out_refs):
        local_experts, slots, width = out_ref.shape
        out = out_ref[...].reshape(local_experts * slots, width)
        y = lax.dot_general(pick, out, (((0,), (0,)), ((), ())), preferred_element_type=jnp.float32)
        tok = y0_ref.shape[0]
        y0_ref[:, i * width : (i + 1) * width] = y[:tok]
        y1_ref[:, i * width : (i + 1) * width] = y[tok:].astype(jnp.bfloat16)


def combine(code, *results):
    local_experts, slots, _ = results[0].shape
    width = sum(r.shape[2] for r in results)
    tok = code.shape[2]
    return pl.pallas_call(
        combine_kernel,
        out_shape=(
            jax.ShapeDtypeStruct((tok, width), jnp.float32),
            jax.ShapeDtypeStruct((tok, width), jnp.bfloat16),
        ),
        compiler_params=params(),
        cost_estimate=pl.CostEstimate(
            flops=4 * local_experts * slots * tok * width,
            bytes_accessed=2 * width * (3 * tok + local_experts * slots),
            transcendentals=0,
        ),
    )(code, *results)


def body(depth, lines, tokens, expert_ids, route_weight, w_gate, w_up, w_down):
    width = tokens.shape[1]
    top = expert_ids.shape[1]
    local_experts = w_gate.shape[0]
    index = lax.axis_index("exp")
    part = width // 2

    def place(pz, py, pc):
        return (pz % depth * lines + py) * CORES + pc

    everyone = [(a, b, c) for a in range(depth) for b in range(lines) for c in range(CORES)]

    def send(value, move):
        return lax.ppermute(value, "exp", [(place(*who), place(*move(*who))) for who in everyone])

    def swap_core(value):
        return send(value, lambda a, b, c: (a, b, 1 - c))

    def swap_line(value):
        return send(value, lambda a, b, c: (a, 1 - b, c))

    def to_above(value):
        return send(value, lambda a, b, c: (a + 1, b, c))

    def to_below(value):
        return send(value, lambda a, b, c: (a - 1, b, c))

    nearer = depth // 2
    line = [with_routes(tokens, expert_ids, route_weight)] + [None] * (depth - 1)
    turns = []
    for d in range(1, nearer + 1):
        turns.append((d, d - 1, to_below))
        if depth - d > nearer:
            turns.append((depth - d, (depth - d + 1) % depth, to_above))
    for r, source, move in turns:
        line[r] = move(line[source])
    pieces = {(r, 0): line[r] for r in range(depth)}
    if lines > 1:
        for r in [0] + [t[0] for t in turns[:-1]]:
            pieces[r, 1] = swap_line(line[r])
        pieces[nearer, 1] = [swap_line(v) for v in (line[nearer][:, : LANES + part], line[nearer][:, LANES + part :])]

    first = (index * local_experts).astype(jnp.int32).reshape(1)
    rows, codes, weights = {}, {}, {}
    for key, piece in pieces.items():
        halves = piece if isinstance(piece, list) else [piece]
        a, codes[key], weights[key] = dispatch(first, top, local_experts, halves[0], swap_core(halves[0]))
        rows[key] = [a, a]
        if len(halves) > 1:
            rows[key][1] = dispatch_more(codes[key], halves[1], swap_core(halves[1]))
    keys = list(rows)

    gate_sum, up_sum = begin([rows[k][0] for k in keys], part, w_gate, w_up)
    hidden, out0 = middle(
        [rows[k][1] for k in keys], part, [weights[k] for k in keys], gate_sum, up_sum, w_gate, w_up, w_down
    )
    out1 = finish(hidden, w_down, part, len(keys))
    results = {k: (out0[i], out1[i]) for i, k in enumerate(keys)}

    wide = jnp.float32
    link = jnp.bfloat16 if depth <= 4 else wide

    def across(r, parts=(0, 1)):
        halves = []
        for b in reversed(range(lines)):
            y0, y1 = combine(codes[r, b], *[results[r, b][i] for i in parts])
            halves.append(y0 + swap_core(y1).astype(wide))
        if lines > 1:
            return halves[1] + swap_line(halves[0].astype(jnp.bfloat16)).astype(wide)
        return halves[0]

    got_up = got_down = 0.0
    for d in range(nearer, 0, -1):
        if d == nearer:
            got_up = [to_above(across(d, (i,)).astype(link)).astype(wide) for i in range(2)]
            got_up = jnp.concatenate(got_up, axis=1)
        else:
            got_up = to_above((across(d) + got_up).astype(link)).astype(wide)
        if depth - d > nearer:
            got_down = to_below((across(depth - d) + got_down).astype(link)).astype(wide)
    return (across(0) + got_up + got_down).astype(jnp.bfloat16)


def solution(mesh):
    groups, owners = mesh.shape["grp"], mesh.shape["exp"]
    lines = max(1, 4 // groups)
    depth = owners // (lines * CORES)
    in_specs = (
        P(("grp", "exp"), None),
        P(("grp", "exp"), None),
        P(("grp", "exp"), None),
        P("exp", None, None),
        P("exp", None, None),
        P("exp", None, None),
    )
    out_specs = P(("grp", "exp"), None)
    return jax.shard_map(
        functools.partial(body, depth, lines),
        mesh=mesh,
        in_specs=in_specs,
        out_specs=out_specs,
        check_vma=False,
    )
```

time: 177 us -> 171 us (0.966)
  waiting for transfers between devices: 83.8 us -> 75 us
  starting transfers between devices: 44.4 us -> 38.8 us
  local copies, waits for them, and re-layouts: 4.03 us -> 9.48 us
  Pallas kernels: 39.4 us -> 41.8 us
    ppermute x4 -> x0, waiting for transfers between devices: 11.8 us -> none  [body(): lax.ppermute(table, 'exp', [(i, i ^ bit) for i in range(owners)])]
    unnamed x5 -> x22, local copies, waits for them, and re-layouts: 2.17 us -> 8.61 us
    ppermute x60 -> x36, starting transfers between devices: 42.5 us -> 38.8 us  [send(): lax.ppermute(value, 'exp', [(place(*who), place(*move(*who))) for who in...]
    ppermute x60 -> x36, waiting for transfers between devices: 72 us -> 75 us  [send(): lax.ppermute(value, 'exp', [(place(*who), place(*move(*who))) for who in...]
    ppermute x4 -> x0, starting transfers between devices: 1.87 us -> none  [body(): lax.ppermute(table, 'exp', [(i, i ^ bit) for i in range(owners)])]
    pallas_call x16 -> x10, Pallas kernels: 5.08 us -> 4 us  [combine(): pl.pallas_call(combine_kernel, out_shape=(jax.ShapeDtypeStruct((tok, widt...]
    pallas_call x16 -> x9, Pallas kernels: 9 us -> 9.93 us  [the longest x8 8.72 us: dispatch(): pl.pallas_call(functools.partial(dispatch_kernel, top), in_specs=[pl.Bloc...]
  transfers between devices with their start and end apart: 64 -> 36, of which waited for: 26 -> 12; matrix products, arithmetic and copies ran while one was open for 3% -> 1% of each run, Pallas kernels for 15% -> 16%
where the time goes in v3:
time: 171 us; the launch traced here: 170 us
  waiting for transfers between devices  75 us (44%)
  Pallas kernels  41.8 us (24%)
  starting transfers between devices  38.8 us (23%)
  local copies, waits for them, and re-layouts  9.48 us (6%)
  other arithmetic  4.97 us (3%)
    ppermute x36, waiting for transfers between devices, send(): lax.ppermute(value, 'exp', [(place(*who), place(*move(*who))) for who in...  75 us
    ppermute x36, starting transfers between devices, send(): lax.ppermute(value, 'exp', [(place(*who), place(*move(*who))) for who in...  38.8 us
    pallas_call x1, Pallas kernels, middle(): pl.pallas_call(functools.partial(middle_kernel, pairs), grid=(local_exper...  12.8 us
    pallas_call x1, Pallas kernels, begin(): pl.pallas_call(functools.partial(begin_kernel, pairs), grid=(local_expert...  9.81 us
    pallas_call x8, Pallas kernels, dispatch(): pl.pallas_call(functools.partial(dispatch_kernel, top), in_specs=[pl.Bloc...  8.72 us
    unnamed x22, local copies, waits for them, and re-layouts  8.61 us
    pallas_call x1, Pallas kernels, finish(): pl.pallas_call(finish_kernel, grid=(local_experts,), in_specs=[pl.BlockSp...  5.3 us
    pallas_call x10, Pallas kernels, combine(): pl.pallas_call(combine_kernel, out_shape=(jax.ShapeDtypeStruct((tok, widt...  4 us
  transfers between devices with their start and end apart: 36, of which 12 were waited for; matrix products, arithmetic and copies ran while one was open for 1% of the time, Pallas kernels for 16%

profile of v3, /device:TPU:0, one launch (start us, length us, event | category | flops | bytes accessed | tf_op | source)
XLA Modules:
  0.0 170.4 jit_solution(3226206062236435211)
XLA Ops:
  0.7 0.8 fusion.3
  1.6 1.1 fusion.1.x0_ref
  2.7 3.1 %collective-permute-start.5 = (bf16[128,2176]{1,0:T(8,128)(2,1)S(1)}, bf16[128,2176]{1,0:T(8,128)(2,1)S(1)}, u32[]{:S(2)}, u32[]{:S(2)}) collective-permute-start(bf16[128,2176]{1,0:T(8,128)(2,1)S(1)} %fusion.1.x0_ref), channel_id=1, source_target_pairs={{0,4},{1,5},{2,6},{3,7},{4,8},{5,9},{6,10},{7,11},{8,12},{9,13},{1... | collective-permute-start | bytes 1671176 | tf_op jit(solution)/shard_map/ppermute | solution.py:276
  5.8 2.1 %collective-permute-start.1 = (bf16[128,2176]{1,0:T(8,128)(2,1)S(1)}, bf16[128,2176]{1,0:T(8,128)(2,1)S(1)}, u32[]{:S(2)}, u32[]{:S(2)}) collective-permute-start(bf16[128,2176]{1,0:T(8,128)(2,1)S(1)} %fusion.1.x0_ref), channel_id=1, source_target_pairs={{0,12},{1,13},{2,14},{3,15},{4,0},{5,1},{6,2},{7,3},{8,4},{9,5},{1... | collective-permute-start | bytes 1671176 | tf_op jit(solution)/shard_map/ppermute | solution.py:276
  7.8 1.7 collective-permute-start.7
  9.5 11.8 %collective-permute-done.5.x0_ref = bf16[128,2176]{1,0:T(8,128)(2,1)S(1)} collective-permute-done((bf16[128,2176]{1,0:T(8,128)(2,1)S(1)}, bf16[128,2176]{1,0:T(8,128)(2,1)S(1)}, u32[]{:S(2)}, u32[]{:S(2)}) %collective-permute-start.5) | collective-permute-done | bytes 557088 | tf_op jit(solution)/shard_map/ppermute | solution.py:276
  21.3 1.8 %collective-permute-start.11 = (bf16[128,2176]{1,0:T(8,128)(2,1)S(1)}, bf16[128,2176]{1,0:T(8,128)(2,1)S(1)}, u32[]{:S(2)}, u32[]{:S(2)}) collective-permute-start(bf16[128,2176]{1,0:T(8,128)(2,1)S(1)} %collective-permute-done.5.x0_ref), channel_id=1, source_target_pairs={{0,2},{1,3},{2,0},{3,1},{4,6},{5,7},{6,4},{7,5},{8,10},{9,11},{10,... | collective-permute-start | bytes 1671176 | tf_op jit(solution)/shard_map/ppermute | solution.py:276
  23.0 8.7 %collective-permute-done.1.x0_ref = bf16[128,2176]{1,0:T(8,128)(2,1)S(1)} collective-permute-done((bf16[128,2176]{1,0:T(8,128)(2,1)S(1)}, bf16[128,2176]{1,0:T(8,128)(2,1)S(1)}, u32[]{:S(2)}, u32[]{:S(2)}) %collective-permute-start.1) | collective-permute-done | bytes 557088 | tf_op jit(solution)/shard_map/ppermute | solution.py:276
  31.8 1.5 collective-permute-start.9
  33.3 2.8 %collective-permute-start.3 = (bf16[128,2176]{1,0:T(8,128)(2,1)S(1)}, bf16[128,2176]{1,0:T(8,128)(2,1)S(1)}, u32[]{:S(2)}, u32[]{:S(2)}) collective-permute-start(bf16[128,2176]{1,0:T(8,128)(2,1)S(1)} %collective-permute-done.1.x0_ref), channel_id=1, source_target_pairs={{0,12},{1,13},{2,14},{3,15},{4,0},{5,1},{6,2},{7,3},{8,4},{9,5},{1... | collective-permute-start | bytes 1671176 | tf_op jit(solution)/shard_map/ppermute | solution.py:276
  36.1 0.8 copy-done.3
  37.5 8.7 %collective-permute-done.9.x0_ref = bf16[128,2176]{1,0:T(8,128)(2,1)S(1)} collective-permute-done((bf16[128,2176]{1,0:T(8,128)(2,1)S(1)}, bf16[128,2176]{1,0:T(8,128)(2,1)S(1)}, u32[]{:S(2)}, u32[]{:S(2)}) %collective-permute-start.9) | collective-permute-done | bytes 557088 | tf_op jit(solution)/shard_map/ppermute | solution.py:276
  46.2 0.7 collective-permute-done.3.x0_ref
  47.0 0.8 copy-done.5
  47.8 1.0 collective-permute-start.13
  48.8 0.8 copy-done.7
  50.4 0.8 copy-done.9
  51.2 1.2 collective-permute-start.15
  52.4 5.3 %collective-permute-done.13.x0_ref = bf16[128,1152]{1,0:T(8,128)(2,1)} collective-permute-done((bf16[128,1152]{1,0:T(8,128)(2,1)S(1)}, bf16[128,1152]{1,0:T(8,128)(2,1)}, u32[]{:S(2)}, u32[]{:S(2)}) %collective-permute-start.13) | collective-permute-done | bytes 294944 | tf_op jit(solution)/shard_map/ppermute | solution.py:276
  57.7 1.1 copy-done.4
  59.4 1.0 copy-done.2
  60.4 1.1 copy-done.6
  63.8 1.6 shard_map.70
  65.5 1.6 shard_map.69
  67.1 1.6 shard_map.66
  68.8 1.5 shard_map.71
  70.3 9.8 %shard_map.73 = (f32[4,384,768]{2,1,0:T(8,128)S(1)}, f32[4,384,768]{2,1,0:T(8,128)}) custom-call(bf16[4,48,2048]{2,1,0:T(8,128)(2,1)S(1)} %get-tuple-element.69.refs_0_, bf16[4,48,2048]{2,1,0:T(8,128)(2,1)S(1)} %get-tuple-element.70.refs_1_, bf16[4,48,2048]{2,1,0:T(8,128)(2,1)S(1)} %get-tuple-element.71.refs_2_, ...), custom_call_target="tpu_custom_call" | custom-call | flops 4831838208 | bytes 22020096 | tf_op jit(solution)/shard_map/pallas_call | solution.py:148
  80.1 2.2 %copy-done = f32[4,384,768]{2,1,0:T(8,128)} copy-done((f32[4,384,768]{2,1,0:T(8,128)}, f32[4,384,768]{2,1,0:T(8,128)S(1)}, u32[]{:S(2)}) %copy-start) | copy-done | bytes 4718616
  82.3 1.2 shard_map.72.refs_7_
  83.5 12.8 %shard_map.74 = (bf16[4,384,768]{2,1,0:T(8,128)(2,1)S(1)}, bf16[4,48,1024]{2,1,0:T(8,128)(2,1)S(1)}, bf16[4,48,1024]{2,1,0:T(8,128)(2,1)S(1)}, bf16[4,48,1024]{2...) custom-call(bf16[4,48,2048]{2,1,0:T(8,128)(2,1)S(1)} %get-tuple-elem, ...), custom_call_target="tpu_custom_call" | custom-call | flops 7247757312 | bytes 28311552 | tf_op jit(solution)/shard_map/pallas_call | solution.py:187
  97.6 5.3 %shard_map.75 = (bf16[4,48,1024]{2,1,0:T(8,128)(2,1)S(1)}, bf16[4,48,1024]{2,1,0:T(8,128)(2,1)S(1)}, bf16[4,48,1024]{2,1,0:T(8,128)(2,1)S(1)}, bf16[4,48,1024]{2...) custom-call(bf16[4,384,768]{2,1,0:T(8,128)(2,1)S(1)} %get-tuple-elem, ...), custom_call_target="tpu_custom_call" | custom-call | flops 2415919104 | bytes 11796480 | tf_op jit(solution)/shard_map/pallas_call | solution.py:214
  106.7 1.2 collective-permute-start.25
  107.9 1.0 collective-permute-start.29
  109.5 6.4 %collective-permute-done.25 = bf16[128,1024]{1,0:T(8,128)(2,1)S(1)} collective-permute-done((bf16[128,1024]{1,0:T(8,128)(2,1)S(1)}, bf16[128,1024]{1,0:T(8,128)(2,1)S(1)}, u32[]{:S(2)}, u32[]{:S(2)}) %collective-permute-start.25) | collective-permute-done | bytes 262176 | tf_op jit(solution)/shard_map/ppermute | solution.py:276
  116.5 4.5 %collective-permute-done.29 = bf16[128,1024]{1,0:T(8,128)(2,1)S(1)} collective-permute-done((bf16[128,1024]{1,0:T(8,128)(2,1)S(1)}, bf16[128,1024]{1,0:T(8,128)(2,1)S(1)}, u32[]{:S(2)}, u32[]{:S(2)}) %collective-permute-start.29) | collective-permute-done | bytes 262176 | tf_op jit(solution)/shard_map/ppermute | solution.py:276
  121.2 1.8 %collective-permute-start.26 = (bf16[128,1024]{1,0:T(8,128)(2,1)S(1)}, bf16[128,1024]{1,0:T(8,128)(2,1)S(1)}, u32[]{:S(2)}, u32[]{:S(2)}) collective-permute-start(bf16[128,1024]{1,0:T(8,128)(2,1)S(1)} %add_convert_fusion.8), channel_id=1, source_target_pairs={{0,4},{1,5},{2,6},{3,7},{4,8},{5,9},{6,10},{7,11},{8,12},{9,13},{1... | collective-permute-start | bytes 786440 | tf_op jit(solution)/shard_map/ppermute | solution.py:276
  123.1 1.0 collective-permute-start.22
  124.2 5.6 %collective-permute-start.30 = (bf16[128,1024]{1,0:T(8,128)(2,1)S(1)}, bf16[128,1024]{1,0:T(8,128)(2,1)S(1)}, u32[]{:S(2)}, u32[]{:S(2)}) collective-permute-start(bf16[128,1024]{1,0:T(8,128)(2,1)S(1)} %add_convert_fusion.6), channel_id=1, source_target_pairs={{0,4},{1,5},{2,6},{3,7},{4,8},{5,9},{6,10},{7,11},{8,12},{9,13},{1... | collective-permute-start | bytes 786440 | tf_op jit(solution)/shard_map/ppermute | solution.py:276
  129.8 0.8 collective-permute-start.34
  130.7 4.7 %collective-permute-done.26 = bf16[128,1024]{1,0:T(8,128)(2,1)S(1)} collective-permute-done((bf16[128,1024]{1,0:T(8,128)(2,1)S(1)}, bf16[128,1024]{1,0:T(8,128)(2,1)S(1)}, u32[]{:S(2)}, u32[]{:S(2)}) %collective-permute-start.26) | collective-permute-done | bytes 262176 | tf_op jit(solution)/shard_map/ppermute | solution.py:276
  135.4 5.4 %collective-permute-done.30 = bf16[128,1024]{1,0:T(8,128)(2,1)S(1)} collective-permute-done((bf16[128,1024]{1,0:T(8,128)(2,1)S(1)}, bf16[128,1024]{1,0:T(8,128)(2,1)S(1)}, u32[]{:S(2)}, u32[]{:S(2)}) %collective-permute-start.30) | collective-permute-done | bytes 262176 | tf_op jit(solution)/shard_map/ppermute | solution.py:276
  140.8 1.5 collective-permute-start.19
  142.7 0.8 collective-permute-start.31
  143.5 5.7 %collective-permute-done.34 = bf16[128,2048]{1,0:T(8,128)(2,1)S(1)} collective-permute-done((bf16[128,2048]{1,0:T(8,128)(2,1)S(1)}, bf16[128,2048]{1,0:T(8,128)(2,1)S(1)}, u32[]{:S(2)}, u32[]{:S(2)}) %collective-permute-start.34) | collective-permute-done | bytes 524320 | tf_op jit(solution)/shard_map/ppermute | solution.py:276
  149.4 6.8 %collective-permute-start.35 = (bf16[128,2048]{1,0:T(8,128)(2,1)S(1)}, bf16[128,2048]{1,0:T(8,128)(2,1)S(1)}, u32[]{:S(2)}, u32[]{:S(2)}) collective-permute-start(bf16[128,2048]{1,0:T(8,128)(2,1)S(1)} %add_convert_fusion.1), channel_id=1, source_target_pairs={{0,12},{1,13},{2,14},{3,15},{4,0},{5,1},{6,2},{7,3},{8,4},{9,5},{1... | collective-permute-start | bytes 1572872 | tf_op jit(solution)/shard_map/ppermute | solution.py:276
  156.2 3.5 %collective-permute-done.19 = bf16[128,2048]{1,0:T(8,128)(2,1)S(1)} collective-permute-done((bf16[128,2048]{1,0:T(8,128)(2,1)S(1)}, bf16[128,2048]{1,0:T(8,128)(2,1)S(1)}, u32[]{:S(2)}, u32[]{:S(2)}) %collective-permute-start.19) | collective-permute-done | bytes 524320 | tf_op jit(solution)/shard_map/ppermute | solution.py:276
  159.7 9.5 %collective-permute-done.35 = bf16[128,2048]{1,0:T(8,128)(2,1)S(1)} collective-permute-done((bf16[128,2048]{1,0:T(8,128)(2,1)S(1)}, bf16[128,2048]{1,0:T(8,128)(2,1)S(1)}, u32[]{:S(2)}, u32[]{:S(2)}) %collective-permute-start.35) | collective-permute-done | bytes 524320 | tf_op jit(solution)/shard_map/ppermute | solution.py:276
  169.2 1.2 add_convert_fusion
  (85 shorter events, 12.3 us)
Async XLA Ops:
  2.7 18.6 %collective-permute-start.5 = (bf16[128,2176]{1,0:T(8,128)(2,1)S(1)}, bf16[128,2176]{1,0:T(8,128)(2,1)S(1)}, u32[]{:S(2)}, u32[]{:S(2)}) collective-permute-start(bf16[128,2176]{1,0:T(8,128)(2,1)S(1)} %fusion.1.x0_ref), channel_id=1, source_target_pairs={{0,4},{1,5},{2,6},{3,7},{4,8},{5,9},{6,10},{7,11},{8,12},{9,13},{1... | collective-permute-start | bytes 1671176 | tf_op jit(solution)/shard_map/ppermute | solution.py:276
  5.8 26.0 %collective-permute-start.1 = (bf16[128,2176]{1,0:T(8,128)(2,1)S(1)}, bf16[128,2176]{1,0:T(8,128)(2,1)S(1)}, u32[]{:S(2)}, u32[]{:S(2)}) collective-permute-start(bf16[128,2176]{1,0:T(8,128)(2,1)S(1)} %fusion.1.x0_ref), channel_id=1, source_target_pairs={{0,12},{1,13},{2,14},{3,15},{4,0},{5,1},{6,2},{7,3},{8,4},{9,5},{1... | collective-permute-start | bytes 1671176 | tf_op jit(solution)/shard_map/ppermute | solution.py:276
  7.8 28.3 %collective-permute-start.7 = (bf16[128,2176]{1,0:T(8,128)(2,1)S(1)}, bf16[128,2176]{1,0:T(8,128)(2,1)S(1)}, u32[]{:S(2)}, u32[]{:S(2)}) collective-permute-start(bf16[128,2176]{1,0:T(8,128)(2,1)S(1)} %fusion.1.x0_ref), channel_id=1, source_target_pairs={{0,2},{1,3},{2,0},{3,1},{4,6},{5,7},{6,4},{7,5},{8,10},{9,11},{10,... | collective-permute-start | bytes 1671176 | tf_op jit(solution)/shard_map/ppermute | solution.py:276
  9.5 26.6 %collective-permute-start = (bf16[128,2176]{1,0:T(8,128)(2,1)S(1)}, bf16[128,2176]{1,0:T(8,128)(2,1)S(1)}, u32[]{:S(2)}, u32[]{:S(2)}) collective-permute-start(bf16[128,2176]{1,0:T(8,128)(2,1)S(1)} %fusion.1.x0_ref), channel_id=1, source_target_pairs={{0,1},{1,0},{2,3},{3,2},{4,5},{5,4},{6,7},{7,6},{8,9},{9,8},{10,11... | collective-permute-start | bytes 1671176 | tf_op jit(solution)/shard_map/ppermute | solution.py:276
  21.3 16.2 %collective-permute-start.11 = (bf16[128,2176]{1,0:T(8,128)(2,1)S(1)}, bf16[128,2176]{1,0:T(8,128)(2,1)S(1)}, u32[]{:S(2)}, u32[]{:S(2)}) collective-permute-start(bf16[128,2176]{1,0:T(8,128)(2,1)S(1)} %collective-permute-done.5.x0_ref), channel_id=1, source_target_pairs={{0,2},{1,3},{2,0},{3,1},{4,6},{5,7},{6,4},{7,5},{8,10},{9,11},{10,... | collective-permute-start | bytes 1671176 | tf_op jit(solution)/shard_map/ppermute | solution.py:276
  31.8 14.4 %collective-permute-start.9 = (bf16[128,2176]{1,0:T(8,128)(2,1)S(1)}, bf16[128,2176]{1,0:T(8,128)(2,1)S(1)}, u32[]{:S(2)}, u32[]{:S(2)}) collective-permute-start(bf16[128,2176]{1,0:T(8,128)(2,1)S(1)} %collective-permute-done.1.x0_ref), channel_id=1, source_target_pairs={{0,2},{1,3},{2,0},{3,1},{4,6},{5,7},{6,4},{7,5},{8,10},{9,11},{10,... | collective-permute-start | bytes 1671176 | tf_op jit(solution)/shard_map/ppermute | solution.py:276
  33.3 13.7 %collective-permute-start.3 = (bf16[128,2176]{1,0:T(8,128)(2,1)S(1)}, bf16[128,2176]{1,0:T(8,128)(2,1)S(1)}, u32[]{:S(2)}, u32[]{:S(2)}) collective-permute-start(bf16[128,2176]{1,0:T(8,128)(2,1)S(1)} %collective-permute-done.1.x0_ref), channel_id=1, source_target_pairs={{0,12},{1,13},{2,14},{3,15},{4,0},{5,1},{6,2},{7,3},{8,4},{9,5},{1... | collective-permute-start | bytes 1671176 | tf_op jit(solution)/shard_map/ppermute | solution.py:276
  36.1 14.3 %copy-start.1 = (bf16[128,2176]{1,0:T(8,128)(2,1)}, bf16[128,2176]{1,0:T(8,128)(2,1)S(1)}, u32[]{:S(2)}) copy-start(bf16[128,2176]{1,0:T(8,128)(2,1)S(1)} %collective-permute-done.7.x0_ref) | copy-start | bytes 1671172
  36.1 10.9 %collective-permute-start.8 = (bf16[128,2176]{1,0:T(8,128)(2,1)S(1)}, bf16[128,2176]{1,0:T(8,128)(2,1)S(1)}, u32[]{:S(2)}, u32[]{:S(2)}) collective-permute-start(bf16[128,2176]{1,0:T(8,128)(2,1)S(1)} %collective-permute-done.7.x0_ref), channel_id=1, source_target_pairs={{0,1},{1,0},{2,3},{3,2},{4,5},{5,4},{6,7},{7,6},{8,9},{9,8},{10,11... | collective-permute-start | bytes 1671176 | tf_op jit(solution)/shard_map/ppermute | solution.py:276
  36.1 0.9 copy-start.3
  37.0 11.9 %collective-permute-start.6 = (bf16[128,2176]{1,0:T(8,128)(2,1)S(1)}, bf16[128,2176]{1,0:T(8,128)(2,1)S(1)}, u32[]{:S(2)}, u32[]{:S(2)}) collective-permute-start(bf16[128,2176]{1,0:T(8,128)(2,1)S(1)} %collective-permute-done.5.x0_ref), channel_id=1, source_target_pairs={{0,1},{1,0},{2,3},{3,2},{4,5},{5,4},{6,7},{7,6},{8,9},{9,8},{10,11... | collective-permute-start | bytes 1671176 | tf_op jit(solution)/shard_map/ppermute | solution.py:276
  37.5 12.9 %collective-permute-start.2 = (bf16[128,2176]{1,0:T(8,128)(2,1)S(1)}, bf16[128,2176]{1,0:T(8,128)(2,1)S(1)}, u32[]{:S(2)}, u32[]{:S(2)}) collective-permute-start(bf16[128,2176]{1,0:T(8,128)(2,1)S(1)} %collective-permute-done.1.x0_ref), channel_id=1, source_target_pairs={{0,1},{1,0},{2,3},{3,2},{4,5},{5,4},{6,7},{7,6},{8,9},{9,8},{10,11... | collective-permute-start | bytes 1671176 | tf_op jit(solution)/shard_map/ppermute | solution.py:276
  46.2 17.6 %collective-permute-start.12 = (bf16[128,2176]{1,0:T(8,128)(2,1)S(1)}, bf16[128,2176]{1,0:T(8,128)(2,1)}, u32[]{:S(2)}, u32[]{:S(2)}) collective-permute-start(bf16[128,2176]{1,0:T(8,128)(2,1)S(1)} %collective-permute-done.11.x0_ref), channel_id=1, source_target_pairs={{0,1},{1,0},{2,3},{3,2},{4,5},{5,4},{6,7},{7,6},{8,9},{9,8},{10,11... | collective-permute-start | bytes 1671176 | tf_op jit(solution)/shard_map/ppermute | solution.py:276
  47.0 18.5 %collective-permute-start.10 = (bf16[128,2176]{1,0:T(8,128)(2,1)S(1)}, bf16[128,2176]{1,0:T(8,128)(2,1)}, u32[]{:S(2)}, u32[]{:S(2)}) collective-permute-start(bf16[128,2176]{1,0:T(8,128)(2,1)S(1)} %collective-permute-done.9.x0_ref), channel_id=1, source_target_pairs={{0,1},{1,0},{2,3},{3,2},{4,5},{5,4},{6,7},{7,6},{8,9},{9,8},{10,11... | collective-permute-start | bytes 1671176 | tf_op jit(solution)/shard_map/ppermute | solution.py:276
  47.0 0.8 copy-start.5
  47.8 9.9 %collective-permute-start.13 = (bf16[128,1152]{1,0:T(8,128)(2,1)S(1)}, bf16[128,1152]{1,0:T(8,128)(2,1)}, u32[]{:S(2)}, u32[]{:S(2)}) collective-permute-start(bf16[128,1152]{1,0:T(8,128)(2,1)S(1)} %slice.8), channel_id=1, source_target_pairs={{0,2},{1,3},{2,0},{3,1},{4,6},{5,7},{6,4},{7,5},{8,10},{9,11},{10,... | collective-permute-start | bytes 884744 | tf_op jit(solution)/shard_map/ppermute | solution.py:276
  48.8 0.8 copy-start.7
  49.7 17.5 %collective-permute-start.4 = (bf16[128,2176]{1,0:T(8,128)(2,1)S(1)}, bf16[128,2176]{1,0:T(8,128)(2,1)}, u32[]{:S(2)}, u32[]{:S(2)}) collective-permute-start(bf16[128,2176]{1,0:T(8,128)(2,1)S(1)} %collective-permute-done.3.x0_ref), channel_id=1, source_target_pairs={{0,1},{1,0},{2,3},{3,2},{4,5},{5,4},{6,7},{7,6},{8,9},{9,8},{10,11... | collective-permute-start | bytes 1671176 | tf_op jit(solution)/shard_map/ppermute | solution.py:276
  50.4 0.8 copy-start.9
  51.2 12.0 %collective-permute-start.15 = (bf16[128,1024]{1,0:T(8,128)(2,1)}, bf16[128,1024]{1,0:T(8,128)(2,1)}, u32[]{:S(2)}, u32[]{:S(2)}) collective-permute-start(bf16[128,1024]{1,0:T(8,128)(2,1)} %slice.9), channel_id=1, source_target_pairs={{0,2},{1,3},{2,0},{3,1},{4,6},{5,7},{6,4},{7,5},{8,10},{9,11},{10,... | collective-permute-start | bytes 786440 | tf_op jit(solution)/shard_map/ppermute | solution.py:276
  57.7 11.1 %collective-permute-start.14 = (bf16[128,1152]{1,0:T(8,128)(2,1)}, bf16[128,1152]{1,0:T(8,128)(2,1)}, u32[]{:S(2)}, u32[]{:S(2)}) collective-permute-start(bf16[128,1152]{1,0:T(8,128)(2,1)} %collective-permute-done.13.x0_ref), channel_id=1, source_target_pairs={{0,1},{1,0},{2,3},{3,2},{4,5},{5,4},{6,7},{7,6},{8,9},{9,8},{10,11... | collective-permute-start | bytes 884744 | tf_op jit(solution)/shard_map/ppermute | solution.py:276
  57.7 1.1 copy-start.4
  58.8 3.3 %copy-start.8 = (bf16[128,2176]{1,0:T(8,128)(2,1)S(1)}, bf16[128,2176]{1,0:T(8,128)(2,1)}, u32[]{:S(2)}) copy-start(bf16[128,2176]{1,0:T(8,128)(2,1)} %copy-done.7) | copy-start | bytes 1671172
  58.8 3.9 %copy-start.10 = (bf16[128,2176]{1,0:T(8,128)(2,1)S(1)}, bf16[128,2176]{1,0:T(8,128)(2,1)}, u32[]{:S(2)}) copy-start(bf16[128,2176]{1,0:T(8,128)(2,1)} %copy-done.9) | copy-start | bytes 1671172
  59.4 1.1 copy-start.2
  60.4 1.1 copy-start.6
  63.3 19.0 %collective-permute-start.16 = (bf16[128,1024]{1,0:T(8,128)(2,1)}, bf16[128,1024]{1,0:T(8,128)(2,1)S(1)}, u32[]{:S(2)}, u32[]{:S(2)}) collective-permute-start(bf16[128,1024]{1,0:T(8,128)(2,1)} %collective-permute-done.15.x0_ref), channel_id=1, source_target_pairs={{0,1},{1,0},{2,3},{3,2},{4,5},{5,4},{6,7},{7,6},{8,9},{9,8},{10,11... | collective-permute-start | bytes 786440 | tf_op jit(solution)/shard_map/ppermute | solution.py:276
  80.1 2.2 %copy-start = (f32[4,384,768]{2,1,0:T(8,128)}, f32[4,384,768]{2,1,0:T(8,128)S(1)}, u32[]{:S(2)}) copy-start(f32[4,384,768]{2,1,0:T(8,128)S(1)} %get-tuple-element.86.refs_16_) | copy-start | bytes 14155780
  96.6 12.7 %collective-permute-start.23 = (bf16[128,1024]{1,0:T(8,128)(2,1)S(1)}, bf16[128,1024]{1,0:T(8,128)(2,1)S(1)}, u32[]{:S(2)}, u32[]{:S(2)}) collective-permute-start(bf16[128,1024]{1,0:T(8,128)(2,1)S(1)} %get-tuple-element.111), channel_id=1, source_target_pairs={{0,1},{1,0},{2,3},{3,2},{4,5},{5,4},{6,7},{7,6},{8,9},{9,8},{10,11... | collective-permute-start | bytes 786440 | tf_op jit(solution)/shard_map/ppermute | solution.py:276
  97.1 9.5 %collective-permute-start.24 = (bf16[128,1024]{1,0:T(8,128)(2,1)S(1)}, bf16[128,1024]{1,0:T(8,128)(2,1)S(1)}, u32[]{:S(2)}, u32[]{:S(2)}) collective-permute-start(bf16[128,1024]{1,0:T(8,128)(2,1)S(1)} %get-tuple-element.114), channel_id=1, source_target_pairs={{0,1},{1,0},{2,3},{3,2},{4,5},{5,4},{6,7},{7,6},{8,9},{9,8},{10,11... | collective-permute-start | bytes 786440 | tf_op jit(solution)/shard_map/ppermute | solution.py:276
  103.2 12.7 %collective-permute-start.27 = (bf16[128,1024]{1,0:T(8,128)(2,1)S(1)}, bf16[128,1024]{1,0:T(8,128)(2,1)S(1)}, u32[]{:S(2)}, u32[]{:S(2)}) collective-permute-start(bf16[128,1024]{1,0:T(8,128)(2,1)S(1)} %get-tuple-element.117), channel_id=1, source_target_pairs={{0,1},{1,0},{2,3},{3,2},{4,5},{5,4},{6,7},{7,6},{8,9},{9,8},{10,11... | collective-permute-start | bytes 786440 | tf_op jit(solution)/shard_map/ppermute | solution.py:276
  103.7 4.2 %collective-permute-start.28 = (bf16[128,1024]{1,0:T(8,128)(2,1)S(1)}, bf16[128,1024]{1,0:T(8,128)(2,1)S(1)}, u32[]{:S(2)}, u32[]{:S(2)}) collective-permute-start(bf16[128,1024]{1,0:T(8,128)(2,1)S(1)} %get-tuple-element.120), channel_id=1, source_target_pairs={{0,1},{1,0},{2,3},{3,2},{4,5},{5,4},{6,7},{7,6},{8,9},{9,8},{10,11... | collective-permute-start | bytes 786440 | tf_op jit(solution)/shard_map/ppermute | solution.py:276
  104.7 16.5 %collective-permute-start.21 = (bf16[128,2048]{1,0:T(8,128)(2,1)S(1)}, bf16[128,2048]{1,0:T(8,128)(2,1)S(1)}, u32[]{:S(2)}, u32[]{:S(2)}) collective-permute-start(bf16[128,2048]{1,0:T(8,128)(2,1)S(1)} %get-tuple-element.107), channel_id=1, source_target_pairs={{0,1},{1,0},{2,3},{3,2},{4,5},{5,4},{6,7},{7,6},{8,9},{9,8},{10,11... | collective-permute-start | bytes 1572872 | tf_op jit(solution)/shard_map/ppermute | solution.py:276
  106.7 9.2 %collective-permute-start.25 = (bf16[128,1024]{1,0:T(8,128)(2,1)S(1)}, bf16[128,1024]{1,0:T(8,128)(2,1)S(1)}, u32[]{:S(2)}, u32[]{:S(2)}) collective-permute-start(bf16[128,1024]{1,0:T(8,128)(2,1)S(1)} %add_convert_fusion.9), channel_id=1, source_target_pairs={{0,2},{1,3},{2,0},{3,1},{4,6},{5,7},{6,4},{7,5},{8,10},{9,11},{10,... | collective-permute-start | bytes 786440 | tf_op jit(solution)/shard_map/ppermute | solution.py:276
  107.9 13.1 %collective-permute-start.29 = (bf16[128,1024]{1,0:T(8,128)(2,1)S(1)}, bf16[128,1024]{1,0:T(8,128)(2,1)S(1)}, u32[]{:S(2)}, u32[]{:S(2)}) collective-permute-start(bf16[128,1024]{1,0:T(8,128)(2,1)S(1)} %add_convert_fusion.7), channel_id=1, source_target_pairs={{0,2},{1,3},{2,0},{3,1},{4,6},{5,7},{6,4},{7,5},{8,10},{9,11},{10,... | collective-permute-start | bytes 786440 | tf_op jit(solution)/shard_map/ppermute | solution.py:276
  109.4 14.9 %collective-permute-start.18 = (bf16[128,2048]{1,0:T(8,128)(2,1)S(1)}, bf16[128,2048]{1,0:T(8,128)(2,1)S(1)}, u32[]{:S(2)}, u32[]{:S(2)}) collective-permute-start(bf16[128,2048]{1,0:T(8,128)(2,1)S(1)} %get-tuple-element.97), channel_id=1, source_target_pairs={{0,1},{1,0},{2,3},{3,2},{4,5},{5,4},{6,7},{7,6},{8,9},{9,8},{10,11... | collective-permute-start | bytes 1572872 | tf_op jit(solution)/shard_map/ppermute | solution.py:276
  115.9 14.0 %collective-permute-start.20 = (bf16[128,2048]{1,0:T(8,128)(2,1)S(1)}, bf16[128,2048]{1,0:T(8,128)(2,1)S(1)}, u32[]{:S(2)}, u32[]{:S(2)}) collective-permute-start(bf16[128,2048]{1,0:T(8,128)(2,1)S(1)} %get-tuple-element.102), channel_id=1, source_target_pairs={{0,1},{1,0},{2,3},{3,2},{4,5},{5,4},{6,7},{7,6},{8,9},{9,8},{10,11... | collective-permute-start | bytes 1572872 | tf_op jit(solution)/shard_map/ppermute | solution.py:276
  116.0 27.5 %collective-permute-start.32 = (bf16[128,2048]{1,0:T(8,128)(2,1)S(1)}, bf16[128,2048]{1,0:T(8,128)(2,1)S(1)}, u32[]{:S(2)}, u32[]{:S(2)}) collective-permute-start(bf16[128,2048]{1,0:T(8,128)(2,1)S(1)} %get-tuple-element.125), channel_id=1, source_target_pairs={{0,1},{1,0},{2,3},{3,2},{4,5},{5,4},{6,7},{7,6},{8,9},{9,8},{10,11... | collective-permute-start | bytes 1572872 | tf_op jit(solution)/shard_map/ppermute | solution.py:276
  121.1 2.1 %collective-permute-start.33 = (bf16[128,2048]{1,0:T(8,128)(2,1)S(1)}, bf16[128,2048]{1,0:T(8,128)(2,1)S(1)}, u32[]{:S(2)}, u32[]{:S(2)}) collective-permute-start(bf16[128,2048]{1,0:T(8,128)(2,1)S(1)} %get-tuple-element.130), channel_id=1, source_target_pairs={{0,1},{1,0},{2,3},{3,2},{4,5},{5,4},{6,7},{7,6},{8,9},{9,8},{10,11... | collective-permute-start | bytes 1572872 | tf_op jit(solution)/shard_map/ppermute | solution.py:276
  121.2 14.2 %collective-permute-start.26 = (bf16[128,1024]{1,0:T(8,128)(2,1)S(1)}, bf16[128,1024]{1,0:T(8,128)(2,1)S(1)}, u32[]{:S(2)}, u32[]{:S(2)}) collective-permute-start(bf16[128,1024]{1,0:T(8,128)(2,1)S(1)} %add_convert_fusion.8), channel_id=1, source_target_pairs={{0,4},{1,5},{2,6},{3,7},{4,8},{5,9},{6,10},{7,11},{8,12},{9,13},{1... | collective-permute-start | bytes 786440 | tf_op jit(solution)/shard_map/ppermute | solution.py:276
  123.1 19.2 %collective-permute-start.22 = (bf16[128,2048]{1,0:T(8,128)(2,1)S(1)}, bf16[128,2048]{1,0:T(8,128)(2,1)S(1)}, u32[]{:S(2)}, u32[]{:S(2)}) collective-permute-start(bf16[128,2048]{1,0:T(8,128)(2,1)S(1)} %add_convert_fusion.4), channel_id=1, source_target_pairs={{0,2},{1,3},{2,0},{3,1},{4,6},{5,7},{6,4},{7,5},{8,10},{9,11},{10,... | collective-permute-start | bytes 1572872 | tf_op jit(solution)/shard_map/ppermute | solution.py:276
  124.2 16.6 %collective-permute-start.30 = (bf16[128,1024]{1,0:T(8,128)(2,1)S(1)}, bf16[128,1024]{1,0:T(8,128)(2,1)S(1)}, u32[]{:S(2)}, u32[]{:S(2)}) collective-permute-start(bf16[128,1024]{1,0:T(8,128)(2,1)S(1)} %add_convert_fusion.6), channel_id=1, source_target_pairs={{0,4},{1,5},{2,6},{3,7},{4,8},{5,9},{6,10},{7,11},{8,12},{9,13},{1... | collective-permute-start | bytes 786440 | tf_op jit(solution)/shard_map/ppermute | solution.py:276
  129.8 19.4 %collective-permute-start.34 = (bf16[128,2048]{1,0:T(8,128)(2,1)S(1)}, bf16[128,2048]{1,0:T(8,128)(2,1)S(1)}, u32[]{:S(2)}, u32[]{:S(2)}) collective-permute-start(bf16[128,2048]{1,0:T(8,128)(2,1)S(1)} %add_convert_fusion.2), channel_id=1, source_target_pairs={{0,2},{1,3},{2,0},{3,1},{4,6},{5,7},{6,4},{7,5},{8,10},{9,11},{10,... | collective-permute-start | bytes 1572872 | tf_op jit(solution)/shard_map/ppermute | solution.py:276
  135.4 20.8 %collective-permute-start.17 = (bf16[128,2048]{1,0:T(8,128)(2,1)S(1)}, bf16[128,2048]{1,0:T(8,128)(2,1)S(1)}, u32[]{:S(2)}, u32[]{:S(2)}) collective-permute-start(bf16[128,2048]{1,0:T(8,128)(2,1)S(1)} %get-tuple-element.92), channel_id=1, source_target_pairs={{0,1},{1,0},{2,3},{3,2},{4,5},{5,4},{6,7},{7,6},{8,9},{9,8},{10,11... | collective-permute-start | bytes 1572872 | tf_op jit(solution)/shard_map/ppermute | solution.py:276
  140.8 18.9 %collective-permute-start.19 = (bf16[128,2048]{1,0:T(8,128)(2,1)S(1)}, bf16[128,2048]{1,0:T(8,128)(2,1)S(1)}, u32[]{:S(2)}, u32[]{:S(2)}) collective-permute-start(bf16[128,2048]{1,0:T(8,128)(2,1)S(1)} %add_convert_fusion.5), channel_id=1, source_target_pairs={{0,2},{1,3},{2,0},{3,1},{4,6},{5,7},{6,4},{7,5},{8,10},{9,11},{10,... | collective-permute-start | bytes 1572872 | tf_op jit(solution)/shard_map/ppermute | solution.py:276
  142.7 17.1 %collective-permute-start.31 = (bf16[128,2048]{1,0:T(8,128)(2,1)S(1)}, bf16[128,2048]{1,0:T(8,128)(2,1)S(1)}, u32[]{:S(2)}, u32[]{:S(2)}) collective-permute-start(bf16[128,2048]{1,0:T(8,128)(2,1)S(1)} %add_convert_fusion.3), channel_id=1, source_target_pairs={{0,4},{1,5},{2,6},{3,7},{4,8},{5,9},{6,10},{7,11},{8,12},{9,13},{1... | collective-permute-start | bytes 1572872 | tf_op jit(solution)/shard_map/ppermute | solution.py:276
  149.4 19.8 %collective-permute-start.35 = (bf16[128,2048]{1,0:T(8,128)(2,1)S(1)}, bf16[128,2048]{1,0:T(8,128)(2,1)S(1)}, u32[]{:S(2)}, u32[]{:S(2)}) collective-permute-start(bf16[128,2048]{1,0:T(8,128)(2,1)S(1)} %add_convert_fusion.1), channel_id=1, source_target_pairs={{0,12},{1,13},{2,14},{3,15},{4,0},{5,1},{6,2},{7,3},{8,4},{9,5},{1... | collective-permute-start | bytes 1572872 | tf_op jit(solution)/shard_map/ppermute | solution.py:276

commit v4 on v3

--- a/solution.py
+++ b/solution.py
@@ -10,11 +10,12 @@
 CAP = 24
 CORES = 2
 LANES = 128
-VMEM_LIMIT = 40 * 1024 * 1024
-
-
-def params(**kw):
-    return pltpu.CompilerParams(vmem_limit_bytes=VMEM_LIMIT, **kw)
+MIB = 1024 * 1024
+SMALL_LIMIT = 6 * MIB
+
+
+def params(limit=SMALL_LIMIT):
+    return pltpu.CompilerParams(vmem_limit_bytes=limit)
 
 
 def selector(code_ref, local):
@@ -101,7 +102,7 @@
             jax.ShapeDtypeStruct((local_experts, 2 * CAP, LANES), jnp.float32),
         ),
         compiler_params=params(),
-        cost_estimate=pick_cost(local_experts, tok, width),
+        cost_estimate=pl.CostEstimate(flops=0, bytes_accessed=0, transcendentals=0),
     )(first, x0, x1)
 
 
@@ -111,121 +112,171 @@
         more_kernel,
         out_shape=jax.ShapeDtypeStruct((local_experts, 2 * CAP, width), jnp.bfloat16),
         compiler_params=params(),
-        cost_estimate=pick_cost(local_experts, x0.shape[0], width),
+        cost_estimate=pl.CostEstimate(flops=0, bytes_accessed=0, transcendentals=0),
     )(code, x0, x1)
 
 
-def column_specs(rows, part, chunk):
-    def spec(r):
-        at = chunk if r.shape[2] > part else 0
-        return pl.BlockSpec((1, r.shape[1], part), lambda l: (l, 0, at))
-
-    return [spec(r) for r in rows]
-
-
-def rows_specs(rows):
-    return [pl.BlockSpec((1,) + r.shape[1:], lambda l: (l, 0, 0)) for r in rows]
-
-
-def joined(refs):
-    return jnp.concatenate([r[0] for r in refs], axis=0)
-
-
-def begin_kernel(pairs, *refs):
-    rows = joined(refs[:pairs])
-    gate_w, up_w, gate_ref, up_ref = refs[pairs:]
-    gate_ref[0] = jnp.dot(rows, gate_w[0], preferred_element_type=jnp.float32)
-    up_ref[0] = jnp.dot(rows, up_w[0], preferred_element_type=jnp.float32)
-
-
-def begin(rows, width, w_gate, w_up):
+def row_blocks(pairs):
+    return [range(p, min(p + 8, pairs)) for p in range(0, pairs, 8)]
+
+
+def columns_of(refs, part, chunk):
+    return [slice(chunk * part, (chunk + 1) * part) if r.shape[2] > part else slice(None) for r in refs]
+
+
+def rows_of(refs, local, part, chunk, block):
+    where = columns_of(refs, part, chunk)
+    return jnp.concatenate([refs[p][local, :, where[p]] for p in block], axis=0)
+
+
+def span(block):
+    return slice(block[0] * 2 * CAP, (block[-1] + 1) * 2 * CAP)
+
+
+class Stream:
+    def __init__(self, hbm, buffer, sems, rows, columns):
+        self.hbm, self.buffer, self.sems, self.where = hbm, buffer, sems, (rows, columns)
+
+    def copy(self, local):
+        slot = local % 2
+        return pltpu.make_async_copy(self.hbm.at[(local,) + self.where], self.buffer.at[slot], self.sems.at[slot])
+
+    def start(self, local):
+        self.copy(local).start()
+
+    def get(self, local):
+        self.copy(local).wait()
+        return self.buffer[local % 2]
+
+
+def over_experts(count, streams, work):
+    for stream in streams:
+        stream.start(0)
+
+    @pl.loop(0, count)
+    def _(local):
+        @pl.when(local + 1 < count)
+        def _():
+            for stream in streams:
+                stream.start(local + 1)
+
+        work(local)
+
+
+def stream_scratch(*shapes):
+    buffers = [pltpu.VMEM((2,) + shape, jnp.bfloat16) for shape in shapes]
+    return buffers + [pltpu.SemaphoreType.DMA((2,)) for _ in shapes]
+
+
+def begin_kernel(pairs, part, *refs):
+    rows_refs = refs[:pairs]
+    gate_hbm, up_hbm, gate_ref, up_ref, gate_buf, up_buf, gate_sem, up_sem = refs[pairs:]
+    head, full = slice(0, part), slice(None)
+    gate_w = Stream(gate_hbm, gate_buf, gate_sem, head, full)
+    up_w = Stream(up_hbm, up_buf, up_sem, head, full)
+
+    def work(local):
+        blocks = row_blocks(pairs)
+        for stream, out_ref in ((gate_w, gate_ref), (up_w, up_ref)):
+            weight = stream.get(local)
+            for block in blocks:
+                rows = rows_of(rows_refs, local, part, 0, block)
+                out_ref[local, span(block)] = jnp.dot(rows, weight, preferred_element_type=jnp.float32)
+
+    over_experts(gate_ref.shape[0], (gate_w, up_w), work)
+
+
+VMEM_SPEC = pl.BlockSpec(memory_space=pltpu.VMEM)
+HBM_SPEC = pl.BlockSpec(memory_space=pltpu.HBM)
+
+
+def begin(rows, part, w_gate, w_up):
     pairs = len(rows)
     local_experts, _, hidden = w_gate.shape
-    count = pairs * rows[0].shape[1]
-    weight_spec = pl.BlockSpec((1, width, hidden), lambda l: (l, 0, 0))
-    sum_spec = pl.BlockSpec((1, count, hidden), lambda l: (l, 0, 0))
+    count = pairs * 2 * CAP
     shape = jax.ShapeDtypeStruct((local_experts, count, hidden), jnp.float32)
     return pl.pallas_call(
-        functools.partial(begin_kernel, pairs),
-        grid=(local_experts,),
-        in_specs=column_specs(rows, width, 0) + [weight_spec] * 2,
-        out_specs=(sum_spec, sum_spec),
+        functools.partial(begin_kernel, pairs, part),
+        in_specs=[VMEM_SPEC] * pairs + [HBM_SPEC] * 2,
+        out_specs=(VMEM_SPEC,) * 2,
         out_shape=(shape, shape),
-        compiler_params=params(),
-        cost_estimate=pl.CostEstimate(
-            flops=4 * local_experts * count * width * hidden,
-            bytes_accessed=4 * local_experts * width * hidden + 8 * local_experts * count * hidden,
-            transcendentals=0,
-        ),
+        scratch_shapes=stream_scratch((part, hidden), (part, hidden)),
+        compiler_params=params(32 * MIB),
+        cost_estimate=pl.CostEstimate(flops=0, bytes_accessed=0, transcendentals=0),
     )(*rows, w_gate, w_up)
 
 
-def middle_kernel(pairs, *refs):
-    rows, weight = joined(refs[:pairs]), jnp.concatenate([r[0, :, :1] for r in refs[pairs : 2 * pairs]], axis=0)
-    gate_sum, up_sum, gate_w, up_w, down_w, hidden_ref = refs[2 * pairs : 2 * pairs + 6]
-    out_refs = refs[2 * pairs + 6 :]
-    gate = gate_sum[0] + jnp.dot(rows, gate_w[0], preferred_element_type=jnp.float32)
-    up = up_sum[0] + jnp.dot(rows, up_w[0], preferred_element_type=jnp.float32)
-    hidden = (gate / (1.0 + jnp.exp(-gate)) * up * weight).astype(jnp.bfloat16)
-    hidden_ref[0] = hidden
-    write_out(out_refs, jnp.dot(hidden, down_w[0], preferred_element_type=jnp.float32))
-
-
-def write_out(out_refs, out):
-    out = out.astype(jnp.bfloat16)
-    for p, ref in enumerate(out_refs):
-        ref[0] = out[p * 2 * CAP : (p + 1) * 2 * CAP]
-
-
-def middle(rows, width, weights, gate_sum, up_sum, w_gate, w_up, w_down):
+def middle_kernel(pairs, part, *refs):
+    rows_refs, weight_refs = refs[:pairs], refs[pairs : 2 * pairs]
+    gate_sum, up_sum, gate_hbm, up_hbm, down_hbm, hidden_ref = refs[2 * pairs : 2 * pairs + 6]
+    out_refs, scratch = refs[2 * pairs + 6 : 3 * pairs + 6], refs[3 * pairs + 6 :]
+    tail, full = slice(part, 2 * part), slice(None)
+    gate_w = Stream(gate_hbm, scratch[0], scratch[3], tail, full)
+    up_w = Stream(up_hbm, scratch[1], scratch[4], tail, full)
+    down_w = Stream(down_hbm, scratch[2], scratch[5], full, slice(0, part))
+
+    def work(local):
+        gate_now, up_now, down_now = gate_w.get(local), up_w.get(local), None
+        for block in row_blocks(pairs):
+            rows = rows_of(rows_refs, local, part, 1, block)
+            weight = jnp.concatenate([weight_refs[p][local, :, :1] for p in block], axis=0)
+            at = span(block)
+            gate = gate_sum[local, at] + jnp.dot(rows, gate_now, preferred_element_type=jnp.float32)
+            up = up_sum[local, at] + jnp.dot(rows, up_now, preferred_element_type=jnp.float32)
+            hidden = (gate / (1.0 + jnp.exp(-gate)) * up * weight).astype(jnp.bfloat16)
+            hidden_ref[local, at] = hidden
+            if down_now is None:
+                down_now = down_w.get(local)
+            write_out(out_refs, local, block, hidden, down_now)
+
+    over_experts(hidden_ref.shape[0], (gate_w, up_w, down_w), work)
+
+
+def write_out(out_refs, local, block, hidden, weight):
+    out = jnp.dot(hidden, weight, preferred_element_type=jnp.float32).astype(jnp.bfloat16)
+    for i, p in enumerate(block):
+        out_refs[p][local] = out[i * 2 * CAP : (i + 1) * 2 * CAP]
+
+
+def middle(rows, part, weights, gate_sum, up_sum, w_gate, w_up, w_down):
     pairs = len(rows)
     local_experts, _, hidden = w_gate.shape
-    count = pairs * rows[0].shape[1]
-    weight_spec = pl.BlockSpec((1, width, hidden), lambda l: (l, 1, 0))
-    sum_spec = pl.BlockSpec((1, count, hidden), lambda l: (l, 0, 0))
-    out_shapes = [jax.ShapeDtypeStruct((local_experts, 2 * CAP, width), jnp.bfloat16)] * pairs
+    count = pairs * 2 * CAP
+    out_shapes = [jax.ShapeDtypeStruct((local_experts, 2 * CAP, part), jnp.bfloat16)] * pairs
     got = pl.pallas_call(
-        functools.partial(middle_kernel, pairs),
-        grid=(local_experts,),
-        in_specs=column_specs(rows, width, 1)
-        + rows_specs(weights)
-        + [sum_spec] * 2
-        + [weight_spec] * 2
-        + [pl.BlockSpec((1, hidden, width), lambda l: (l, 0, 0))],
-        out_specs=[sum_spec] + rows_specs(out_shapes),
+        functools.partial(middle_kernel, pairs, part),
+        in_specs=[VMEM_SPEC] * (2 * pairs + 2) + [HBM_SPEC] * 3,
+        out_specs=[VMEM_SPEC] * (pairs + 1),
         out_shape=[jax.ShapeDtypeStruct((local_experts, count, hidden), jnp.bfloat16)] + out_shapes,
-        compiler_params=params(),
-        cost_estimate=pl.CostEstimate(
-            flops=6 * local_experts * count * width * hidden,
-            bytes_accessed=6 * local_experts * width * hidden + 8 * local_experts * count * hidden,
-            transcendentals=local_experts * count * hidden,
-        ),
+        scratch_shapes=stream_scratch((part, hidden), (part, hidden), (hidden, part)),
+        compiler_params=params(32 * MIB),
+        cost_estimate=pl.CostEstimate(flops=0, bytes_accessed=0, transcendentals=0),
     )(*rows, *weights, gate_sum, up_sum, w_gate, w_up, w_down)
     return got[0], got[1:]
 
 
-def finish_kernel(hidden_ref, down_w, *out_refs):
-    write_out(out_refs, jnp.dot(hidden_ref[0], down_w[0], preferred_element_type=jnp.float32))
-
-
-def finish(hidden, w_down, width, pairs):
+def finish_kernel(pairs, part, hidden_ref, down_hbm, *refs):
+    out_refs, (buffer, sem) = refs[:pairs], refs[pairs:]
+    down_w = Stream(down_hbm, buffer, sem, slice(None), slice(part, 2 * part))
+
+    def work(local):
+        weight = down_w.get(local)
+        for block in row_blocks(pairs):
+            write_out(out_refs, local, block, hidden_ref[local, span(block)], weight)
+
+    over_experts(hidden_ref.shape[0], (down_w,), work)
+
+
+def finish(hidden, w_down, part, pairs):
     local_experts, count, depth = hidden.shape
-    out_shapes = [jax.ShapeDtypeStruct((local_experts, 2 * CAP, width), jnp.bfloat16)] * pairs
     return pl.pallas_call(
-        finish_kernel,
-        grid=(local_experts,),
-        in_specs=[
-            pl.BlockSpec((1, count, depth), lambda l: (l, 0, 0)),
-            pl.BlockSpec((1, depth, width), lambda l: (l, 0, 1)),
-        ],
-        out_specs=rows_specs(out_shapes),
-        out_shape=out_shapes,
-        compiler_params=params(),
-        cost_estimate=pl.CostEstimate(
-            flops=2 * local_experts * count * width * depth,
-            bytes_accessed=2 * local_experts * (width * depth + count * depth + count * width),
-            transcendentals=0,
-        ),
+        functools.partial(finish_kernel, pairs, part),
+        in_specs=[VMEM_SPEC, HBM_SPEC],
+        out_specs=[VMEM_SPEC] * pairs,
+        out_shape=[jax.ShapeDtypeStruct((local_experts, 2 * CAP, part), jnp.bfloat16)] * pairs,
+        scratch_shapes=stream_scratch((depth, part)),
+        compiler_params=params(46 * MIB),
+        cost_estimate=pl.CostEstimate(flops=0, bytes_accessed=0, transcendentals=0),
     )(hidden, w_down)
 
 
@@ -252,12 +303,12 @@
             jax.ShapeDtypeStruct((tok, width), jnp.bfloat16),
         ),
         compiler_params=params(),
-        cost_estimate=pl.CostEstimate(
-            flops=4 * local_experts * slots * tok * width,
-            bytes_accessed=2 * width * (3 * tok + local_experts * slots),
-            transcendentals=0,
-        ),
+        cost_estimate=pl.CostEstimate(flops=0, bytes_accessed=0, transcendentals=0),
     )(code, *results)
+
+
+def after(value, *others):
+    return lax.optimization_barrier((value, *others))[0]
 
 
 def body(depth, lines, tokens, expert_ids, route_weight, w_gate, w_up, w_down):
@@ -294,25 +345,41 @@
         turns.append((d, d - 1, to_below))
         if depth - d > nearer:
             turns.append((depth - d, (depth - d + 1) % depth, to_above))
-    for r, source, move in turns:
-        line[r] = move(line[source])
-    pieces = {(r, 0): line[r] for r in range(depth)}
-    if lines > 1:
-        for r in [0] + [t[0] for t in turns[:-1]]:
-            pieces[r, 1] = swap_line(line[r])
-        pieces[nearer, 1] = [swap_line(v) for v in (line[nearer][:, : LANES + part], line[nearer][:, LANES + part :])]
-
     first = (index * local_experts).astype(jnp.int32).reshape(1)
-    rows, codes, weights = {}, {}, {}
-    for key, piece in pieces.items():
+    rows, codes, weights, late = {}, {}, {}, {}
+
+    def take(key, piece):
         halves = piece if isinstance(piece, list) else [piece]
         a, codes[key], weights[key] = dispatch(first, top, local_experts, halves[0], swap_core(halves[0]))
         rows[key] = [a, a]
         if len(halves) > 1:
-            rows[key][1] = dispatch_more(codes[key], halves[1], swap_core(halves[1]))
-    keys = list(rows)
+            late[key] = halves[1]
+
+    for r, source, move in turns:
+        line[r] = move(line[source])
+    if lines > 1:
+        far = {0: swap_line(line[0])}
+        for r, _, _ in turns[:-1]:
+            far[r] = swap_line(line[r])
+        for r in [0] + [t[0] for t in turns[:-1]]:
+            take((r, 0), line[r])
+        for r in [0] + [t[0] for t in turns[:-2]]:
+            take((r, 1), far[r])
+        last = after(line[nearer], *[rows[k][0] for k in rows])
+        far[nearer] = [swap_line(v) for v in (last[:, : LANES + part], last[:, LANES + part :])]
+        for r in far:
+            if (r, 1) not in rows:
+                take((r, 1), far[r])
+        take((nearer, 0), line[nearer])
+    else:
+        for r in range(depth):
+            take((r, 0), line[r])
+    keys = sorted(rows)
 
     gate_sum, up_sum = begin([rows[k][0] for k in keys], part, w_gate, w_up)
+    for key, half in late.items():
+        half, gate_sum, up_sum = lax.optimization_barrier((half, gate_sum, up_sum))
+        rows[key][1] = dispatch_more(codes[key], half, swap_core(half))
     hidden, out0 = middle(
         [rows[k][1] for k in keys], part, [weights[k] for k in keys], gate_sum, up_sum, w_gate, w_up, w_down
     )

time: 171 us -> 153 us (0.89)
  starting transfers between devices: 38.8 us -> 28.7 us
  local copies, waits for them, and re-layouts: 9.48 us -> 3.85 us
  Pallas kernels: 41.8 us -> 37.7 us
    ppermute x36, starting transfers between devices: 38.8 us -> 28.7 us  [send(): lax.ppermute(value, 'exp', [(place(*who), place(*move(*who))) for who in...]
    unnamed x22 -> x8, local copies, waits for them, and re-layouts: 8.61 us -> 3.69 us
    pallas_call x3, Pallas kernels: 27.9 us -> 25.6 us  [the longest x1 11.1 us: middle(): pl.pallas_call(functools.partial(middle_kernel, pairs, part), in_specs=[V...]
  transfers between devices with their start and end apart: 36 -> 36, of which waited for: 12 -> 15; matrix products, arithmetic and copies ran while one was open for 1% -> 1% of each run, Pallas kernels for 16% -> 17%
where the time goes in v4:
time: 153 us; the launch traced here: 152 us
  waiting for transfers between devices  76.4 us (50%)
  Pallas kernels  37.7 us (25%)
  starting transfers between devices  28.7 us (19%)
  other arithmetic  4.9 us (3%)
  local copies, waits for them, and re-layouts  3.85 us (3%)
    ppermute x36, waiting for transfers between devices, send(): lax.ppermute(value, 'exp', [(place(*who), place(*move(*who))) for who in...  76.4 us
    ppermute x36, starting transfers between devices, send(): lax.ppermute(value, 'exp', [(place(*who), place(*move(*who))) for who in...  28.7 us
    pallas_call x1, Pallas kernels, middle(): pl.pallas_call(functools.partial(middle_kernel, pairs, part), in_specs=[V...  11.1 us
    pallas_call x1, Pallas kernels, begin(): pl.pallas_call(functools.partial(begin_kernel, pairs, part), in_specs=[VM...  9.2 us
    pallas_call x8, Pallas kernels, dispatch(): pl.pallas_call(functools.partial(dispatch_kernel, top), in_specs=[pl.Bloc...  7.85 us
    pallas_call x1, Pallas kernels, finish(): pl.pallas_call(functools.partial(finish_kernel, pairs, part), in_specs=[V...  5.29 us
    pallas_call x10, Pallas kernels, combine(): pl.pallas_call(combine_kernel, out_shape=(jax.ShapeDtypeStruct((tok, widt...  4.02 us
    unnamed x8, local copies, waits for them, and re-layouts  3.69 us
  transfers between devices with their start and end apart: 36, of which 15 were waited for; matrix products, arithmetic and copies ran while one was open for 1% of the time, Pallas kernels for 17%

profile of v4, /device:TPU:0, one launch (start us, length us, event | category | flops | bytes accessed | tf_op | source)
XLA Modules:
  0.0 152.0 jit_solution(15519405329964009208)
XLA Ops:
  0.0 0.7 convert_element_type.103
  0.7 0.8 fusion.3
  1.6 1.1 fusion.1.x0_ref
  2.7 5.1 %collective-permute-start.3 = (bf16[128,2176]{1,0:T(8,128)(2,1)S(1)}, bf16[128,2176]{1,0:T(8,128)(2,1)S(1)}, u32[]{:S(2)}, u32[]{:S(2)}) collective-permute-start(bf16[128,2176]{1,0:T(8,128)(2,1)S(1)} %fusion.1.x0_ref), channel_id=1, source_target_pairs={{0,12},{1,13},{2,14},{3,15},{4,0},{5,1},{6,2},{7,3},{8,4},{9,5},{1... | collective-permute-start | bytes 1671176 | tf_op jit(solution)/shard_map/ppermute | solution.py:327
  7.8 1.5 collective-permute-start.1
  9.3 11.5 %collective-permute-done.3.x0_ref = bf16[128,2176]{1,0:T(8,128)(2,1)S(1)} collective-permute-done((bf16[128,2176]{1,0:T(8,128)(2,1)S(1)}, bf16[128,2176]{1,0:T(8,128)(2,1)S(1)}, u32[]{:S(2)}, u32[]{:S(2)}) %collective-permute-start.3) | collective-permute-done | bytes 557088 | tf_op jit(solution)/shard_map/ppermute | solution.py:327
  20.8 1.5 collective-permute-start.5
  22.3 10.2 %collective-permute-done.9.x0_ref = bf16[128,2176]{1,0:T(8,128)(2,1)S(1)} collective-permute-done((bf16[128,2176]{1,0:T(8,128)(2,1)S(1)}, bf16[128,2176]{1,0:T(8,128)(2,1)S(1)}, u32[]{:S(2)}, u32[]{:S(2)}) %collective-permute-start.9) | collective-permute-done | bytes 557088 | tf_op jit(solution)/shard_map/ppermute | solution.py:327
  33.0 0.8 collective-permute-done.5.x0_ref
  33.8 0.8 copy-done
  34.6 3.7 %collective-permute-start.7 = (bf16[128,2176]{1,0:T(8,128)(2,1)S(1)}, bf16[128,2176]{1,0:T(8,128)(2,1)S(1)}, u32[]{:S(2)}, u32[]{:S(2)}) collective-permute-start(bf16[128,2176]{1,0:T(8,128)(2,1)S(1)} %collective-permute-done.3.x0_ref), channel_id=1, source_target_pairs={{0,12},{1,13},{2,14},{3,15},{4,0},{5,1},{6,2},{7,3},{8,4},{9,5},{1... | collective-permute-start | bytes 1671176 | tf_op jit(solution)/shard_map/ppermute | solution.py:327
  38.3 0.8 copy-done.2
  39.1 1.5 collective-permute-start.14
  40.7 1.1 copy-done.1
  41.7 0.6 shard_map.64
  42.3 1.0 copy-done.3
  43.4 0.6 shard_map.69
  43.9 1.6 %shard_map.66 = (bf16[4,48,2048]{2,1,0:T(8,128)(2,1)S(1)}, s32[2,4,128]{2,1,0:T(4,128)S(1)}, f32[4,48,128]{2,1,0:T(8,128)S(1)}) custom-call(s32[1]{0:T(128)} %bitcast.first_ref, bf16[128,2176]{1,0:T(8,128)(2,1)S(1)} %collective-permute-done.3.x0_ref, bf16[128,2176]{1,0:T(8,128)(2,1)} %collective-permute-done.4.x1_ref), custom_call_target="tpu_custom_call" | custom-call | tf_op jit(solution)/shard_map/pallas_call | solution.py:95
  45.6 1.8 %shard_map.65 = (bf16[4,48,2048]{2,1,0:T(8,128)(2,1)S(1)}, s32[2,4,128]{2,1,0:T(4,128)S(1)}, f32[4,48,128]{2,1,0:T(8,128)S(1)}) custom-call(s32[1]{0:T(128)} %bitcast.first_ref, bf16[128,2176]{1,0:T(8,128)(2,1)} %collective-permute-done.1.x0_ref, bf16[128,2176]{1,0:T(8,128)(2,1)} %collective-permute-done.2.x1_ref), custom_call_target="tpu_custom_call" | custom-call | tf_op jit(solution)/shard_map/pallas_call | solution.py:95
  47.4 1.6 %shard_map.67 = (bf16[4,48,2048]{2,1,0:T(8,128)(2,1)S(1)}, s32[2,4,128]{2,1,0:T(4,128)S(1)}, f32[4,48,128]{2,1,0:T(8,128)S(1)}) custom-call(s32[1]{0:T(128)} %bitcast.first_ref, bf16[128,2176]{1,0:T(8,128)(2,1)S(1)} %collective-permute-done.5.x0_ref, bf16[128,2176]{1,0:T(8,128)(2,1)} %collective-permute-done.6.x1_ref), custom_call_target="tpu_custom_call" | custom-call | tf_op jit(solution)/shard_map/pallas_call | solution.py:95
  49.1 1.8 %collective-permute-done.7.x0_ref = bf16[128,2176]{1,0:T(8,128)(2,1)S(1)} collective-permute-done((bf16[128,2176]{1,0:T(8,128)(2,1)S(1)}, bf16[128,2176]{1,0:T(8,128)(2,1)S(1)}, u32[]{:S(2)}, u32[]{:S(2)}) %collective-permute-start.7) | collective-permute-done | bytes 557088 | tf_op jit(solution)/shard_map/ppermute | solution.py:327
  50.9 1.6 %collective-permute-start.11 = (bf16[128,1152]{1,0:T(8,128)(2,1)S(1)}, bf16[128,1152]{1,0:T(8,128)(2,1)S(1)}, u32[]{:S(2)}, u32[]{:S(2)}) collective-permute-start(bf16[128,1152]{1,0:T(8,128)(2,1)S(1)} %slice.6), channel_id=1, source_target_pairs={{0,2},{1,3},{2,0},{3,1},{4,6},{5,7},{6,4},{7,5},{8,10},{9,11},{10,... | collective-permute-start | bytes 884744 | tf_op jit(solution)/shard_map/ppermute | solution.py:327
  52.5 1.9 %collective-permute-done.14.x0_ref = bf16[128,2176]{1,0:T(8,128)(2,1)S(1)} collective-permute-done((bf16[128,2176]{1,0:T(8,128)(2,1)S(1)}, bf16[128,2176]{1,0:T(8,128)(2,1)S(1)}, u32[]{:S(2)}, u32[]{:S(2)}) %collective-permute-start.14) | collective-permute-done | bytes 557088 | tf_op jit(solution)/shard_map/ppermute | solution.py:327
  54.9 5.3 %collective-permute-done.11.x0_ref = bf16[128,1152]{1,0:T(8,128)(2,1)S(1)} collective-permute-done((bf16[128,1152]{1,0:T(8,128)(2,1)S(1)}, bf16[128,1152]{1,0:T(8,128)(2,1)S(1)}, u32[]{:S(2)}, u32[]{:S(2)}) %collective-permute-start.11) | collective-permute-done | bytes 294944 | tf_op jit(solution)/shard_map/ppermute | solution.py:327
  60.2 1.6 %collective-permute-start.13 = (bf16[128,1024]{1,0:T(8,128)(2,1)S(1)}, bf16[128,1024]{1,0:T(8,128)(2,1)S(1)}, u32[]{:S(2)}, u32[]{:S(2)}) collective-permute-start(bf16[128,1024]{1,0:T(8,128)(2,1)S(1)} %slice.7), channel_id=1, source_target_pairs={{0,2},{1,3},{2,0},{3,1},{4,6},{5,7},{6,4},{7,5},{8,10},{9,11},{10,... | collective-permute-start | bytes 786440 | tf_op jit(solution)/shard_map/ppermute | solution.py:327
  61.8 0.6 shard_map.71
  62.4 0.6 shard_map.68
  63.5 9.2 %shard_map.72 = (f32[4,384,768]{2,1,0:T(8,128)S(1)}, f32[4,384,768]{2,1,0:T(8,128)S(1)}) custom-call(bf16[4,48,2048]{2,1,0:T(8,128)(2,1)S(1)} %get-tuple-element.73.refs_0_, bf16[4,48,2048]{2,1,0:T(8,128)(2,1)S(1)} %get-tuple-element.74.refs_1_, bf16[4,48,2048]{2,1,0:T(8,128)(2,1)S(1)} %get-tuple-element.75.refs_2_, ...), custom_call_target="tpu_custom_call" | custom-call | tf_op jit(solution)/shard_map/pallas_call | solution.py:198
  73.0 1.3 collective-permute-done.16.x1_ref
  74.6 11.1 %shard_map.74 = (bf16[4,384,768]{2,1,0:T(8,128)(2,1)S(1)}, bf16[4,48,1024]{2,1,0:T(8,128)(2,1)S(1)}, bf16[4,48,1024]{2,1,0:T(8,128)(2,1)S(1)}, bf16[4,48,1024]{2...) custom-call(bf16[4,48,2048]{2,1,0:T(8,128)(2,1)S(1)} %get-tuple-elem, ...), custom_call_target="tpu_custom_call" | custom-call | tf_op jit(solution)/shard_map/pallas_call | solution.py:246
  86.3 5.3 %shard_map.75 = (bf16[4,48,1024]{2,1,0:T(8,128)(2,1)S(1)}, bf16[4,48,1024]{2,1,0:T(8,128)(2,1)S(1)}, bf16[4,48,1024]{2,1,0:T(8,128)(2,1)S(1)}, bf16[4,48,1024]{2...) custom-call(bf16[4,384,768]{2,1,0:T(8,128)(2,1)S(1)} %get-tuple-elem, ...), custom_call_target="tpu_custom_call" | custom-call | tf_op jit(solution)/shard_map/pallas_call | solution.py:272
  93.0 0.6 collective-permute-start.25
  94.4 0.6 collective-permute-start.21
  95.0 1.6 %collective-permute-start.29 = (bf16[128,1024]{1,0:T(8,128)(2,1)S(1)}, bf16[128,1024]{1,0:T(8,128)(2,1)S(1)}, u32[]{:S(2)}, u32[]{:S(2)}) collective-permute-start(bf16[128,1024]{1,0:T(8,128)(2,1)S(1)} %add_convert_fusion.7), channel_id=1, source_target_pairs={{0,2},{1,3},{2,0},{3,1},{4,6},{5,7},{6,4},{7,5},{8,10},{9,11},{10,... | collective-permute-start | bytes 786440 | tf_op jit(solution)/shard_map/ppermute | solution.py:327
  99.0 3.1 %collective-permute-done.25 = bf16[128,1024]{1,0:T(8,128)(2,1)S(1)} collective-permute-done((bf16[128,1024]{1,0:T(8,128)(2,1)S(1)}, bf16[128,1024]{1,0:T(8,128)(2,1)S(1)}, u32[]{:S(2)}, u32[]{:S(2)}) %collective-permute-start.25) | collective-permute-done | bytes 262176 | tf_op jit(solution)/shard_map/ppermute | solution.py:327
  102.3 0.6 collective-permute-start.32
  102.9 4.3 %collective-permute-done.29 = bf16[128,1024]{1,0:T(8,128)(2,1)S(1)} collective-permute-done((bf16[128,1024]{1,0:T(8,128)(2,1)S(1)}, bf16[128,1024]{1,0:T(8,128)(2,1)S(1)}, u32[]{:S(2)}, u32[]{:S(2)}) %collective-permute-start.29) | collective-permute-done | bytes 262176 | tf_op jit(solution)/shard_map/ppermute | solution.py:327
  107.5 1.6 %collective-permute-done.33 = bf16[128,2048]{1,0:T(8,128)(2,1)S(1)} collective-permute-done((bf16[128,2048]{1,0:T(8,128)(2,1)S(1)}, bf16[128,2048]{1,0:T(8,128)(2,1)S(1)}, u32[]{:S(2)}, u32[]{:S(2)}) %collective-permute-start.33) | collective-permute-done | bytes 524320 | tf_op jit(solution)/shard_map/ppermute | solution.py:327
  109.1 0.5 collective-permute-start.22
  109.8 1.6 %collective-permute-start.34 = (bf16[128,2048]{1,0:T(8,128)(2,1)S(1)}, bf16[128,2048]{1,0:T(8,128)(2,1)S(1)}, u32[]{:S(2)}, u32[]{:S(2)}) collective-permute-start(bf16[128,2048]{1,0:T(8,128)(2,1)S(1)} %add_convert_fusion.2), channel_id=1, source_target_pairs={{0,2},{1,3},{2,0},{3,1},{4,6},{5,7},{6,4},{7,5},{8,10},{9,11},{10,... | collective-permute-start | bytes 1572872 | tf_op jit(solution)/shard_map/ppermute | solution.py:327
  111.5 6.8 %collective-permute-done.26 = bf16[128,1024]{1,0:T(8,128)(2,1)S(1)} collective-permute-done((bf16[128,1024]{1,0:T(8,128)(2,1)S(1)}, bf16[128,1024]{1,0:T(8,128)(2,1)S(1)}, u32[]{:S(2)}, u32[]{:S(2)}) %collective-permute-start.26) | collective-permute-done | bytes 262176 | tf_op jit(solution)/shard_map/ppermute | solution.py:327
  118.3 5.3 %collective-permute-done.30 = bf16[128,1024]{1,0:T(8,128)(2,1)S(1)} collective-permute-done((bf16[128,1024]{1,0:T(8,128)(2,1)S(1)}, bf16[128,1024]{1,0:T(8,128)(2,1)S(1)}, u32[]{:S(2)}, u32[]{:S(2)}) %collective-permute-start.30) | collective-permute-done | bytes 262176 | tf_op jit(solution)/shard_map/ppermute | solution.py:327
  123.6 0.5 collective-permute-start.19
  124.5 10.6 %collective-permute-done.34 = bf16[128,2048]{1,0:T(8,128)(2,1)S(1)} collective-permute-done((bf16[128,2048]{1,0:T(8,128)(2,1)S(1)}, bf16[128,2048]{1,0:T(8,128)(2,1)S(1)}, u32[]{:S(2)}, u32[]{:S(2)}) %collective-permute-start.34) | collective-permute-done | bytes 524320 | tf_op jit(solution)/shard_map/ppermute | solution.py:327
  135.3 3.7 %collective-permute-start.35 = (bf16[128,2048]{1,0:T(8,128)(2,1)S(1)}, bf16[128,2048]{1,0:T(8,128)(2,1)S(1)}, u32[]{:S(2)}, u32[]{:S(2)}) collective-permute-start(bf16[128,2048]{1,0:T(8,128)(2,1)S(1)} %add_convert_fusion.1), channel_id=1, source_target_pairs={{0,12},{1,13},{2,14},{3,15},{4,0},{5,1},{6,2},{7,3},{8,4},{9,5},{1... | collective-permute-start | bytes 1572872 | tf_op jit(solution)/shard_map/ppermute | solution.py:327
  139.0 6.5 %collective-permute-done.19 = bf16[128,2048]{1,0:T(8,128)(2,1)S(1)} collective-permute-done((bf16[128,2048]{1,0:T(8,128)(2,1)S(1)}, bf16[128,2048]{1,0:T(8,128)(2,1)S(1)}, u32[]{:S(2)}, u32[]{:S(2)}) %collective-permute-start.19) | collective-permute-done | bytes 524320 | tf_op jit(solution)/shard_map/ppermute | solution.py:327
  145.5 5.3 %collective-permute-done.35 = bf16[128,2048]{1,0:T(8,128)(2,1)S(1)} collective-permute-done((bf16[128,2048]{1,0:T(8,128)(2,1)S(1)}, bf16[128,2048]{1,0:T(8,128)(2,1)S(1)}, u32[]{:S(2)}, u32[]{:S(2)}) %collective-permute-start.35) | collective-permute-done | bytes 524320 | tf_op jit(solution)/shard_map/ppermute | solution.py:327
  150.8 1.2 add_convert_fusion
  (71 shorter events, 8.7 us)
Async XLA Ops:
  2.7 18.1 %collective-permute-start.3 = (bf16[128,2176]{1,0:T(8,128)(2,1)S(1)}, bf16[128,2176]{1,0:T(8,128)(2,1)S(1)}, u32[]{:S(2)}, u32[]{:S(2)}) collective-permute-start(bf16[128,2176]{1,0:T(8,128)(2,1)S(1)} %fusion.1.x0_ref), channel_id=1, source_target_pairs={{0,12},{1,13},{2,14},{3,15},{4,0},{5,1},{6,2},{7,3},{8,4},{9,5},{1... | collective-permute-start | bytes 1671176 | tf_op jit(solution)/shard_map/ppermute | solution.py:327
  7.8 24.7 %collective-permute-start.9 = (bf16[128,2176]{1,0:T(8,128)(2,1)S(1)}, bf16[128,2176]{1,0:T(8,128)(2,1)S(1)}, u32[]{:S(2)}, u32[]{:S(2)}) collective-permute-start(bf16[128,2176]{1,0:T(8,128)(2,1)S(1)} %fusion.1.x0_ref), channel_id=1, source_target_pairs={{0,4},{1,5},{2,6},{3,7},{4,8},{5,9},{6,10},{7,11},{8,12},{9,13},{1... | collective-permute-start | bytes 1671176 | tf_op jit(solution)/shard_map/ppermute | solution.py:327
  7.8 25.2 %collective-permute-start.1 = (bf16[128,2176]{1,0:T(8,128)(2,1)S(1)}, bf16[128,2176]{1,0:T(8,128)(2,1)}, u32[]{:S(2)}, u32[]{:S(2)}) collective-permute-start(bf16[128,2176]{1,0:T(8,128)(2,1)S(1)} %fusion.1.x0_ref), channel_id=1, source_target_pairs={{0,2},{1,3},{2,0},{3,1},{4,6},{5,7},{6,4},{7,5},{8,10},{9,11},{10,... | collective-permute-start | bytes 1671176 | tf_op jit(solution)/shard_map/ppermute | solution.py:327
  20.8 13.0 %collective-permute-start.5 = (bf16[128,2176]{1,0:T(8,128)(2,1)S(1)}, bf16[128,2176]{1,0:T(8,128)(2,1)S(1)}, u32[]{:S(2)}, u32[]{:S(2)}) collective-permute-start(bf16[128,2176]{1,0:T(8,128)(2,1)S(1)} %collective-permute-done.3.x0_ref), channel_id=1, source_target_pairs={{0,2},{1,3},{2,0},{3,1},{4,6},{5,7},{6,4},{7,5},{8,10},{9,11},{10,... | collective-permute-start | bytes 1671176 | tf_op jit(solution)/shard_map/ppermute | solution.py:327
  22.3 11.5 %collective-permute-start = (bf16[128,2176]{1,0:T(8,128)(2,1)S(1)}, bf16[128,2176]{1,0:T(8,128)(2,1)S(1)}, u32[]{:S(2)}, u32[]{:S(2)}) collective-permute-start(bf16[128,2176]{1,0:T(8,128)(2,1)S(1)} %fusion.1.x0_ref), channel_id=1, source_target_pairs={{0,1},{1,0},{2,3},{3,2},{4,5},{5,4},{6,7},{7,6},{8,9},{9,8},{10,11... | collective-permute-start | bytes 1671176 | tf_op jit(solution)/shard_map/ppermute | solution.py:327
  32.5 5.8 %collective-permute-start.10 = (bf16[128,2176]{1,0:T(8,128)(2,1)S(1)}, bf16[128,2176]{1,0:T(8,128)(2,1)S(1)}, u32[]{:S(2)}, u32[]{:S(2)}) collective-permute-start(bf16[128,2176]{1,0:T(8,128)(2,1)S(1)} %collective-permute-done.9.x0_ref), channel_id=1, source_target_pairs={{0,1},{1,0},{2,3},{3,2},{4,5},{5,4},{6,7},{7,6},{8,9},{9,8},{10,11... | collective-permute-start | bytes 1671176 | tf_op jit(solution)/shard_map/ppermute | solution.py:327
  32.5 11.4 %collective-permute-start.4 = (bf16[128,2176]{1,0:T(8,128)(2,1)S(1)}, bf16[128,2176]{1,0:T(8,128)(2,1)}, u32[]{:S(2)}, u32[]{:S(2)}) collective-permute-start(bf16[128,2176]{1,0:T(8,128)(2,1)S(1)} %collective-permute-done.3.x0_ref), channel_id=1, source_target_pairs={{0,1},{1,0},{2,3},{3,2},{4,5},{5,4},{6,7},{7,6},{8,9},{9,8},{10,11... | collective-permute-start | bytes 1671176 | tf_op jit(solution)/shard_map/ppermute | solution.py:327
  33.0 12.6 %collective-permute-start.2 = (bf16[128,2176]{1,0:T(8,128)(2,1)}, bf16[128,2176]{1,0:T(8,128)(2,1)}, u32[]{:S(2)}, u32[]{:S(2)}) collective-permute-start(bf16[128,2176]{1,0:T(8,128)(2,1)} %collective-permute-done.1.x0_ref), channel_id=1, source_target_pairs={{0,1},{1,0},{2,3},{3,2},{4,5},{5,4},{6,7},{7,6},{8,9},{9,8},{10,11... | collective-permute-start | bytes 1671176 | tf_op jit(solution)/shard_map/ppermute | solution.py:327
  33.8 13.6 %collective-permute-start.6 = (bf16[128,2176]{1,0:T(8,128)(2,1)S(1)}, bf16[128,2176]{1,0:T(8,128)(2,1)}, u32[]{:S(2)}, u32[]{:S(2)}) collective-permute-start(bf16[128,2176]{1,0:T(8,128)(2,1)S(1)} %collective-permute-done.5.x0_ref), channel_id=1, source_target_pairs={{0,1},{1,0},{2,3},{3,2},{4,5},{5,4},{6,7},{7,6},{8,9},{9,8},{10,11... | collective-permute-start | bytes 1671176 | tf_op jit(solution)/shard_map/ppermute | solution.py:327
  33.8 0.8 copy-start
  34.6 16.3 %collective-permute-start.7 = (bf16[128,2176]{1,0:T(8,128)(2,1)S(1)}, bf16[128,2176]{1,0:T(8,128)(2,1)S(1)}, u32[]{:S(2)}, u32[]{:S(2)}) collective-permute-start(bf16[128,2176]{1,0:T(8,128)(2,1)S(1)} %collective-permute-done.3.x0_ref), channel_id=1, source_target_pairs={{0,12},{1,13},{2,14},{3,15},{4,0},{5,1},{6,2},{7,3},{8,4},{9,5},{1... | collective-permute-start | bytes 1671176 | tf_op jit(solution)/shard_map/ppermute | solution.py:327
  38.3 0.8 copy-start.2
  39.1 15.3 %collective-permute-start.14 = (bf16[128,2176]{1,0:T(8,128)(2,1)S(1)}, bf16[128,2176]{1,0:T(8,128)(2,1)S(1)}, u32[]{:S(2)}, u32[]{:S(2)}) collective-permute-start(bf16[128,2176]{1,0:T(8,128)(2,1)S(1)} %collective-permute-done.9.x0_ref), channel_id=1, source_target_pairs={{0,2},{1,3},{2,0},{3,1},{4,6},{5,7},{6,4},{7,5},{8,10},{9,11},{10,... | collective-permute-start | bytes 1671176 | tf_op jit(solution)/shard_map/ppermute | solution.py:327
  40.7 1.1 copy-start.1
  42.3 1.1 copy-start.3
  50.9 9.3 %collective-permute-start.11 = (bf16[128,1152]{1,0:T(8,128)(2,1)S(1)}, bf16[128,1152]{1,0:T(8,128)(2,1)S(1)}, u32[]{:S(2)}, u32[]{:S(2)}) collective-permute-start(bf16[128,1152]{1,0:T(8,128)(2,1)S(1)} %slice.6), channel_id=1, source_target_pairs={{0,2},{1,3},{2,0},{3,1},{4,6},{5,7},{6,4},{7,5},{8,10},{9,11},{10,... | collective-permute-start | bytes 884744 | tf_op jit(solution)/shard_map/ppermute | solution.py:327
  54.4 7.4 %collective-permute-start.15 = (bf16[128,2176]{1,0:T(8,128)(2,1)S(1)}, bf16[128,2176]{1,0:T(8,128)(2,1)S(1)}, u32[]{:S(2)}, u32[]{:S(2)}) collective-permute-start(bf16[128,2176]{1,0:T(8,128)(2,1)S(1)} %collective-permute-done.14.x0_ref), channel_id=1, source_target_pairs={{0,1},{1,0},{2,3},{3,2},{4,5},{5,4},{6,7},{7,6},{8,9},{9,8},{10,11... | collective-permute-start | bytes 1671176 | tf_op jit(solution)/shard_map/ppermute | solution.py:327
  54.4 8.0 %collective-permute-start.8 = (bf16[128,2176]{1,0:T(8,128)(2,1)S(1)}, bf16[128,2176]{1,0:T(8,128)(2,1)S(1)}, u32[]{:S(2)}, u32[]{:S(2)}) collective-permute-start(bf16[128,2176]{1,0:T(8,128)(2,1)S(1)} %collective-permute-done.7.x0_ref), channel_id=1, source_target_pairs={{0,1},{1,0},{2,3},{3,2},{4,5},{5,4},{6,7},{7,6},{8,9},{9,8},{10,11... | collective-permute-start | bytes 1671176 | tf_op jit(solution)/shard_map/ppermute | solution.py:327
  60.2 2.8 %collective-permute-start.12 = (bf16[128,1152]{1,0:T(8,128)(2,1)S(1)}, bf16[128,1152]{1,0:T(8,128)(2,1)S(1)}, u32[]{:S(2)}, u32[]{:S(2)}) collective-permute-start(bf16[128,1152]{1,0:T(8,128)(2,1)S(1)} %collective-permute-done.11.x0_ref), channel_id=1, source_target_pairs={{0,1},{1,0},{2,3},{3,2},{4,5},{5,4},{6,7},{7,6},{8,9},{9,8},{10,11... | collective-permute-start | bytes 884744 | tf_op jit(solution)/shard_map/ppermute | solution.py:327
  60.2 12.5 %collective-permute-start.13 = (bf16[128,1024]{1,0:T(8,128)(2,1)S(1)}, bf16[128,1024]{1,0:T(8,128)(2,1)S(1)}, u32[]{:S(2)}, u32[]{:S(2)}) collective-permute-start(bf16[128,1024]{1,0:T(8,128)(2,1)S(1)} %slice.7), channel_id=1, source_target_pairs={{0,2},{1,3},{2,0},{3,1},{4,6},{5,7},{6,4},{7,5},{8,10},{9,11},{10,... | collective-permute-start | bytes 786440 | tf_op jit(solution)/shard_map/ppermute | solution.py:327
  72.7 1.6 %collective-permute-start.16 = (bf16[128,1024]{1,0:T(8,128)(2,1)S(1)}, bf16[128,1024]{1,0:T(8,128)(2,1)S(1)}, u32[]{:S(2)}, u32[]{:S(2)}) collective-permute-start(bf16[128,1024]{1,0:T(8,128)(2,1)S(1)} %collective-permute-done.13.x0_ref), channel_id=1, source_target_pairs={{0,1},{1,0},{2,3},{3,2},{4,5},{5,4},{6,7},{7,6},{8,9},{9,8},{10,11... | collective-permute-start | bytes 786440 | tf_op jit(solution)/shard_map/ppermute | solution.py:327
  86.0 6.9 %collective-permute-start.24 = (bf16[128,1024]{1,0:T(8,128)(2,1)S(1)}, bf16[128,1024]{1,0:T(8,128)(2,1)S(1)}, u32[]{:S(2)}, u32[]{:S(2)}) collective-permute-start(bf16[128,1024]{1,0:T(8,128)(2,1)S(1)} %get-tuple-element.122), channel_id=1, source_target_pairs={{0,1},{1,0},{2,3},{3,2},{4,5},{5,4},{6,7},{7,6},{8,9},{9,8},{10,11... | collective-permute-start | bytes 786440 | tf_op jit(solution)/shard_map/ppermute | solution.py:327
  92.0 3.0 %collective-permute-start.28 = (bf16[128,1024]{1,0:T(8,128)(2,1)S(1)}, bf16[128,1024]{1,0:T(8,128)(2,1)S(1)}, u32[]{:S(2)}, u32[]{:S(2)}) collective-permute-start(bf16[128,1024]{1,0:T(8,128)(2,1)S(1)} %get-tuple-element.128), channel_id=1, source_target_pairs={{0,1},{1,0},{2,3},{3,2},{4,5},{5,4},{6,7},{7,6},{8,9},{9,8},{10,11... | collective-permute-start | bytes 786440 | tf_op jit(solution)/shard_map/ppermute | solution.py:327
  92.6 6.3 %collective-permute-start.23 = (bf16[128,1024]{1,0:T(8,128)(2,1)S(1)}, bf16[128,1024]{1,0:T(8,128)(2,1)S(1)}, u32[]{:S(2)}, u32[]{:S(2)}) collective-permute-start(bf16[128,1024]{1,0:T(8,128)(2,1)S(1)} %get-tuple-element.119), channel_id=1, source_target_pairs={{0,1},{1,0},{2,3},{3,2},{4,5},{5,4},{6,7},{7,6},{8,9},{9,8},{10,11... | collective-permute-start | bytes 786440 | tf_op jit(solution)/shard_map/ppermute | solution.py:327
  93.0 9.2 %collective-permute-start.25 = (bf16[128,1024]{1,0:T(8,128)(2,1)S(1)}, bf16[128,1024]{1,0:T(8,128)(2,1)S(1)}, u32[]{:S(2)}, u32[]{:S(2)}) collective-permute-start(bf16[128,1024]{1,0:T(8,128)(2,1)S(1)} %add_convert_fusion.9), channel_id=1, source_target_pairs={{0,2},{1,3},{2,0},{3,1},{4,6},{5,7},{6,4},{7,5},{8,10},{9,11},{10,... | collective-permute-start | bytes 786440 | tf_op jit(solution)/shard_map/ppermute | solution.py:327
  93.9 8.4 %collective-permute-start.27 = (bf16[128,1024]{1,0:T(8,128)(2,1)S(1)}, bf16[128,1024]{1,0:T(8,128)(2,1)S(1)}, u32[]{:S(2)}, u32[]{:S(2)}) collective-permute-start(bf16[128,1024]{1,0:T(8,128)(2,1)S(1)} %get-tuple-element.125), channel_id=1, source_target_pairs={{0,1},{1,0},{2,3},{3,2},{4,5},{5,4},{6,7},{7,6},{8,9},{9,8},{10,11... | collective-permute-start | bytes 786440 | tf_op jit(solution)/shard_map/ppermute | solution.py:327
  94.4 12.9 %collective-permute-start.21 = (bf16[128,2048]{1,0:T(8,128)(2,1)S(1)}, bf16[128,2048]{1,0:T(8,128)(2,1)S(1)}, u32[]{:S(2)}, u32[]{:S(2)}) collective-permute-start(bf16[128,2048]{1,0:T(8,128)(2,1)S(1)} %get-tuple-element.115), channel_id=1, source_target_pairs={{0,1},{1,0},{2,3},{3,2},{4,5},{5,4},{6,7},{7,6},{8,9},{9,8},{10,11... | collective-permute-start | bytes 1572872 | tf_op jit(solution)/shard_map/ppermute | solution.py:327
  95.0 12.1 %collective-permute-start.29 = (bf16[128,1024]{1,0:T(8,128)(2,1)S(1)}, bf16[128,1024]{1,0:T(8,128)(2,1)S(1)}, u32[]{:S(2)}, u32[]{:S(2)}) collective-permute-start(bf16[128,1024]{1,0:T(8,128)(2,1)S(1)} %add_convert_fusion.7), channel_id=1, source_target_pairs={{0,2},{1,3},{2,0},{3,1},{4,6},{5,7},{6,4},{7,5},{8,10},{9,11},{10,... | collective-permute-start | bytes 786440 | tf_op jit(solution)/shard_map/ppermute | solution.py:327
  99.0 10.7 %collective-permute-start.18 = (bf16[128,2048]{1,0:T(8,128)(2,1)S(1)}, bf16[128,2048]{1,0:T(8,128)(2,1)S(1)}, u32[]{:S(2)}, u32[]{:S(2)}) collective-permute-start(bf16[128,2048]{1,0:T(8,128)(2,1)S(1)} %get-tuple-element.105), channel_id=1, source_target_pairs={{0,1},{1,0},{2,3},{3,2},{4,5},{5,4},{6,7},{7,6},{8,9},{9,8},{10,11... | collective-permute-start | bytes 1572872 | tf_op jit(solution)/shard_map/ppermute | solution.py:327
  102.2 7.6 %collective-permute-start.20 = (bf16[128,2048]{1,0:T(8,128)(2,1)S(1)}, bf16[128,2048]{1,0:T(8,128)(2,1)S(1)}, u32[]{:S(2)}, u32[]{:S(2)}) collective-permute-start(bf16[128,2048]{1,0:T(8,128)(2,1)S(1)} %get-tuple-element.110), channel_id=1, source_target_pairs={{0,1},{1,0},{2,3},{3,2},{4,5},{5,4},{6,7},{7,6},{8,9},{9,8},{10,11... | collective-permute-start | bytes 1572872 | tf_op jit(solution)/shard_map/ppermute | solution.py:327
  102.3 22.2 %collective-permute-start.32 = (bf16[128,2048]{1,0:T(8,128)(2,1)S(1)}, bf16[128,2048]{1,0:T(8,128)(2,1)S(1)}, u32[]{:S(2)}, u32[]{:S(2)}) collective-permute-start(bf16[128,2048]{1,0:T(8,128)(2,1)S(1)} %get-tuple-element.133), channel_id=1, source_target_pairs={{0,1},{1,0},{2,3},{3,2},{4,5},{5,4},{6,7},{7,6},{8,9},{9,8},{10,11... | collective-permute-start | bytes 1572872 | tf_op jit(solution)/shard_map/ppermute | solution.py:327
  107.2 1.9 %collective-permute-start.33 = (bf16[128,2048]{1,0:T(8,128)(2,1)S(1)}, bf16[128,2048]{1,0:T(8,128)(2,1)S(1)}, u32[]{:S(2)}, u32[]{:S(2)}) collective-permute-start(bf16[128,2048]{1,0:T(8,128)(2,1)S(1)} %get-tuple-element.138), channel_id=1, source_target_pairs={{0,1},{1,0},{2,3},{3,2},{4,5},{5,4},{6,7},{7,6},{8,9},{9,8},{10,11... | collective-permute-start | bytes 1572872 | tf_op jit(solution)/shard_map/ppermute | solution.py:327
  107.3 11.0 %collective-permute-start.26 = (bf16[128,1024]{1,0:T(8,128)(2,1)S(1)}, bf16[128,1024]{1,0:T(8,128)(2,1)S(1)}, u32[]{:S(2)}, u32[]{:S(2)}) collective-permute-start(bf16[128,1024]{1,0:T(8,128)(2,1)S(1)} %add_convert_fusion.8), channel_id=1, source_target_pairs={{0,4},{1,5},{2,6},{3,7},{4,8},{5,9},{6,10},{7,11},{8,12},{9,13},{1... | collective-permute-start | bytes 786440 | tf_op jit(solution)/shard_map/ppermute | solution.py:327
  109.1 15.1 %collective-permute-start.22 = (bf16[128,2048]{1,0:T(8,128)(2,1)S(1)}, bf16[128,2048]{1,0:T(8,128)(2,1)S(1)}, u32[]{:S(2)}, u32[]{:S(2)}) collective-permute-start(bf16[128,2048]{1,0:T(8,128)(2,1)S(1)} %add_convert_fusion.4), channel_id=1, source_target_pairs={{0,2},{1,3},{2,0},{3,1},{4,6},{5,7},{6,4},{7,5},{8,10},{9,11},{10,... | collective-permute-start | bytes 1572872 | tf_op jit(solution)/shard_map/ppermute | solution.py:327
  109.7 13.9 %collective-permute-start.30 = (bf16[128,1024]{1,0:T(8,128)(2,1)S(1)}, bf16[128,1024]{1,0:T(8,128)(2,1)S(1)}, u32[]{:S(2)}, u32[]{:S(2)}) collective-permute-start(bf16[128,1024]{1,0:T(8,128)(2,1)S(1)} %add_convert_fusion.6), channel_id=1, source_target_pairs={{0,4},{1,5},{2,6},{3,7},{4,8},{5,9},{6,10},{7,11},{8,12},{9,13},{1... | collective-permute-start | bytes 786440 | tf_op jit(solution)/shard_map/ppermute | solution.py:327
  109.8 25.3 %collective-permute-start.34 = (bf16[128,2048]{1,0:T(8,128)(2,1)S(1)}, bf16[128,2048]{1,0:T(8,128)(2,1)S(1)}, u32[]{:S(2)}, u32[]{:S(2)}) collective-permute-start(bf16[128,2048]{1,0:T(8,128)(2,1)S(1)} %add_convert_fusion.2), channel_id=1, source_target_pairs={{0,2},{1,3},{2,0},{3,1},{4,6},{5,7},{6,4},{7,5},{8,10},{9,11},{10,... | collective-permute-start | bytes 1572872 | tf_op jit(solution)/shard_map/ppermute | solution.py:327
  118.3 20.7 %collective-permute-start.17 = (bf16[128,2048]{1,0:T(8,128)(2,1)S(1)}, bf16[128,2048]{1,0:T(8,128)(2,1)S(1)}, u32[]{:S(2)}, u32[]{:S(2)}) collective-permute-start(bf16[128,2048]{1,0:T(8,128)(2,1)S(1)} %get-tuple-element.100), channel_id=1, source_target_pairs={{0,1},{1,0},{2,3},{3,2},{4,5},{5,4},{6,7},{7,6},{8,9},{9,8},{10,11... | collective-permute-start | bytes 1572872 | tf_op jit(solution)/shard_map/ppermute | solution.py:327
  123.6 21.9 %collective-permute-start.19 = (bf16[128,2048]{1,0:T(8,128)(2,1)S(1)}, bf16[128,2048]{1,0:T(8,128)(2,1)S(1)}, u32[]{:S(2)}, u32[]{:S(2)}) collective-permute-start(bf16[128,2048]{1,0:T(8,128)(2,1)S(1)} %add_convert_fusion.5), channel_id=1, source_target_pairs={{0,2},{1,3},{2,0},{3,1},{4,6},{5,7},{6,4},{7,5},{8,10},{9,11},{10,... | collective-permute-start | bytes 1572872 | tf_op jit(solution)/shard_map/ppermute | solution.py:327
  124.4 21.1 %collective-permute-start.31 = (bf16[128,2048]{1,0:T(8,128)(2,1)S(1)}, bf16[128,2048]{1,0:T(8,128)(2,1)S(1)}, u32[]{:S(2)}, u32[]{:S(2)}) collective-permute-start(bf16[128,2048]{1,0:T(8,128)(2,1)S(1)} %add_convert_fusion.3), channel_id=1, source_target_pairs={{0,4},{1,5},{2,6},{3,7},{4,8},{5,9},{6,10},{7,11},{8,12},{9,13},{1... | collective-permute-start | bytes 1572872 | tf_op jit(solution)/shard_map/ppermute | solution.py:327
  135.3 15.6 %collective-permute-start.35 = (bf16[128,2048]{1,0:T(8,128)(2,1)S(1)}, bf16[128,2048]{1,0:T(8,128)(2,1)S(1)}, u32[]{:S(2)}, u32[]{:S(2)}) collective-permute-start(bf16[128,2048]{1,0:T(8,128)(2,1)S(1)} %add_convert_fusion.1), channel_id=1, source_target_pairs={{0,12},{1,13},{2,14},{3,15},{4,0},{5,1},{6,2},{7,3},{8,4},{9,5},{1... | collective-permute-start | bytes 1572872 | tf_op jit(solution)/shard_map/ppermute | solution.py:327

commit v5 on v4

--- a/solution.py
+++ b/solution.py
@@ -10,6 +10,7 @@
 CAP = 24
 CORES = 2
 LANES = 128
+LONG = 40_000_000_000
 MIB = 1024 * 1024
 SMALL_LIMIT = 6 * MIB
 
@@ -29,13 +30,25 @@
     return jnp.concatenate([jnp.where(hit, 1.0, 0.0).astype(jnp.bfloat16) for hit in hits], axis=0)
 
 
+def routes_kernel(ids_ref, weight_ref, tokens_ref, out_ref):
+    top, tok = ids_ref.shape
+    high = weight_ref[...].astype(jnp.bfloat16).astype(jnp.float32)
+    rest = weight_ref[...] - high
+    middle = rest.astype(jnp.bfloat16).astype(jnp.float32)
+    routes = jnp.concatenate([ids_ref[...].astype(jnp.float32), high, middle, rest - middle], axis=0)
+    out_ref[:, :LANES] = jnp.zeros((out_ref.shape[0], LANES), jnp.bfloat16)
+    out_ref[: 4 * top, :tok] = routes.astype(jnp.bfloat16)
+    out_ref[:, LANES:] = tokens_ref[...]
+
+
 def with_routes(tokens, expert_ids, route_weight):
-    high = route_weight.astype(jnp.bfloat16)
-    rest = route_weight - high.astype(jnp.float32)
-    middle = rest.astype(jnp.bfloat16)
-    low = (rest - middle.astype(jnp.float32)).astype(jnp.bfloat16)
-    routes = jnp.concatenate([expert_ids.astype(jnp.bfloat16), high, middle, low], axis=1)
-    return jnp.concatenate([jnp.pad(routes, ((0, 0), (0, LANES - routes.shape[1]))), tokens], axis=1)
+    tok, width = tokens.shape
+    return pl.pallas_call(
+        routes_kernel,
+        out_shape=jax.ShapeDtypeStruct((tok, LANES + width), jnp.bfloat16),
+        compiler_params=params(58 * MIB),
+        cost_estimate=pl.CostEstimate(flops=0, bytes_accessed=0, transcendentals=0),
+    )(expert_ids.T, route_weight.T, tokens)
 
 
 def dispatch_kernel(top, first_ref, x0_ref, x1_ref, rows_ref, code_ref, weight_ref):
@@ -44,7 +57,7 @@
     first = first_ref[0]
     members, wts = [], []
     for x_ref in (x0_ref, x1_ref):
-        routes = x_ref[:, :LANES].astype(jnp.float32).T
+        routes = x_ref[: 4 * top, :tok].astype(jnp.float32)
         ids = routes[:top].astype(jnp.int32)
         wt = routes[top : 2 * top] + (routes[2 * top : 3 * top] + routes[3 * top : 4 * top])
         for local in range(local_experts):
@@ -168,7 +181,7 @@
     return buffers + [pltpu.SemaphoreType.DMA((2,)) for _ in shapes]
 
 
-def begin_kernel(pairs, part, *refs):
+def begin_kernel(pairs, part, token_ref, *refs):
     rows_refs = refs[:pairs]
     gate_hbm, up_hbm, gate_ref, up_ref, gate_buf, up_buf, gate_sem, up_sem = refs[pairs:]
     head, full = slice(0, part), slice(None)
@@ -190,20 +203,20 @@
 HBM_SPEC = pl.BlockSpec(memory_space=pltpu.HBM)
 
 
-def begin(rows, part, w_gate, w_up):
+def begin(token, rows, part, w_gate, w_up):
     pairs = len(rows)
     local_experts, _, hidden = w_gate.shape
     count = pairs * 2 * CAP
     shape = jax.ShapeDtypeStruct((local_experts, count, hidden), jnp.float32)
     return pl.pallas_call(
         functools.partial(begin_kernel, pairs, part),
-        in_specs=[VMEM_SPEC] * pairs + [HBM_SPEC] * 2,
+        in_specs=[VMEM_SPEC] * (pairs + 1) + [HBM_SPEC] * 2,
         out_specs=(VMEM_SPEC,) * 2,
         out_shape=(shape, shape),
         scratch_shapes=stream_scratch((part, hidden), (part, hidden)),
         compiler_params=params(32 * MIB),
-        cost_estimate=pl.CostEstimate(flops=0, bytes_accessed=0, transcendentals=0),
-    )(*rows, w_gate, w_up)
+        cost_estimate=pl.CostEstimate(flops=LONG, bytes_accessed=0, transcendentals=0),
+    )(token, *rows, w_gate, w_up)
 
 
 def middle_kernel(pairs, part, *refs):
@@ -311,6 +324,42 @@
     return lax.optimization_barrier((value, *others))[0]
 
 
+def fence_kernel(in_ref, out_ref):
+    out_ref[...] = in_ref[...] + 1.0
+
+
+def tie(*values):
+    return lax.optimization_barrier(values)
+
+
+def fence(token, *later):
+    token = pl.pallas_call(
+        fence_kernel,
+        out_shape=jax.ShapeDtypeStruct(token.shape, token.dtype),
+        compiler_params=params(),
+        cost_estimate=pl.CostEstimate(flops=LONG, bytes_accessed=0, transcendentals=0),
+    )(token)
+    return tie(token, *later)
+
+
+def last_kernel(token_ref, a_ref, *refs):
+    refs, out_ref = refs[:-1], refs[-1]
+    total = a_ref[...]
+    for ref in refs:
+        total += ref[...].astype(jnp.float32)
+    out_ref[...] = total.astype(out_ref.dtype)
+
+
+def last_sum(token, *terms):
+    return pl.pallas_call(
+        last_kernel,
+        in_specs=[VMEM_SPEC] * (1 + len(terms)),
+        out_shape=jax.ShapeDtypeStruct(terms[0].shape, jnp.bfloat16),
+        compiler_params=params(),
+        cost_estimate=pl.CostEstimate(flops=0, bytes_accessed=0, transcendentals=0),
+    )(token, *terms)
+
+
 def body(depth, lines, tokens, expert_ids, route_weight, w_gate, w_up, w_down):
     width = tokens.shape[1]
     top = expert_ids.shape[1]
@@ -348,66 +397,115 @@
     first = (index * local_experts).astype(jnp.int32).reshape(1)
     rows, codes, weights, late = {}, {}, {}, {}
 
-    def take(key, piece):
+    def take(key, piece, other):
         halves = piece if isinstance(piece, list) else [piece]
-        a, codes[key], weights[key] = dispatch(first, top, local_experts, halves[0], swap_core(halves[0]))
-        rows[key] = [a, a]
+        rows[key], codes[key], weights[key] = dispatch(first, top, local_experts, halves[0], other)
         if len(halves) > 1:
             late[key] = halves[1]
 
-    for r, source, move in turns:
-        line[r] = move(line[source])
-    if lines > 1:
-        far = {0: swap_line(line[0])}
-        for r, _, _ in turns[:-1]:
-            far[r] = swap_line(line[r])
-        for r in [0] + [t[0] for t in turns[:-1]]:
-            take((r, 0), line[r])
-        for r in [0] + [t[0] for t in turns[:-2]]:
-            take((r, 1), far[r])
-        last = after(line[nearer], *[rows[k][0] for k in rows])
-        far[nearer] = [swap_line(v) for v in (last[:, : LANES + part], last[:, LANES + part :])]
-        for r in far:
-            if (r, 1) not in rows:
-                take((r, 1), far[r])
-        take((nearer, 0), line[nearer])
+    if lines > 1 and depth == 4:
+        line[1], far = to_below(line[0]), {0: swap_line(line[0])}
+        others = {(0, 0): swap_core(line[0])}
+        token, line[0] = fence(jnp.zeros((8, LANES), jnp.float32), line[0])
+        line[3] = to_above(line[0])
+        token, line[1], others[0, 0] = fence(token, line[1], others[0, 0])
+        far[1], others[1, 0] = swap_line(line[1]), swap_core(line[1])
+        token, line[1] = fence(token, line[1])
+        line[2] = to_below(line[1])
+        take((0, 0), line[0], others[0, 0])
+        token, line[1], rows[0, 0] = tie(token, line[1], rows[0, 0])
+        token, line[3], far[0], others[1, 0] = fence(token, line[3], far[0], others[1, 0])
+        far[3] = swap_line(line[3])
+        others[3, 0], others[0, 1] = swap_core(line[3]), swap_core(far[0])
+        take((1, 0), line[1], others[1, 0])
+        token, line[3], far[0], rows[1, 0] = tie(token, line[3], far[0], rows[1, 0])
+        others[1, 1] = swap_core(far[1])
+        token, line[2], others[3, 0], others[0, 1], others[1, 1] = fence(
+            token, line[2], others[3, 0], others[0, 1], others[1, 1]
+        )
+        head, tail = swap_line(line[2][:, : LANES + part]), swap_line(line[2][:, LANES + part :])
+        others[2, 0] = swap_core(line[2])
+        for key, piece in (((3, 0), line[3]), ((0, 1), far[0]), ((1, 1), far[1])):
+            take(key, piece, others[key])
+        token, rows[3, 0], rows[0, 1], rows[1, 1] = tie(token, rows[3, 0], rows[0, 1], rows[1, 1])
+        token, far[3], head = fence(token, far[3], head)
+        others[3, 1], others[2, 1] = swap_core(far[3]), swap_core(head)
+        take((2, 0), line[2], others[2, 0])
+        take((3, 1), far[3], others[3, 1])
+        take((2, 1), [head, tail], others[2, 1])
     else:
+        token = jnp.zeros((8, LANES), jnp.float32)
+        for r, source, move in turns:
+            line[r] = move(line[source])
         for r in range(depth):
-            take((r, 0), line[r])
+            take((r, 0), line[r], swap_core(line[r]))
+            if lines > 1:
+                piece = swap_line(line[r])
+                take((r, 1), piece, swap_core(piece))
     keys = sorted(rows)
 
-    gate_sum, up_sum = begin([rows[k][0] for k in keys], part, w_gate, w_up)
+    gate_sum, up_sum = begin(token, [rows[k] for k in keys], part, w_gate, w_up)
     for key, half in late.items():
         half, gate_sum, up_sum = lax.optimization_barrier((half, gate_sum, up_sum))
-        rows[key][1] = dispatch_more(codes[key], half, swap_core(half))
+        rows[key] = dispatch_more(codes[key], half, swap_core(half))
     hidden, out0 = middle(
-        [rows[k][1] for k in keys], part, [weights[k] for k in keys], gate_sum, up_sum, w_gate, w_up, w_down
+        [rows[k] for k in keys], part, [weights[k] for k in keys], gate_sum, up_sum, w_gate, w_up, w_down
     )
-    out1 = finish(hidden, w_down, part, len(keys))
-    results = {k: (out0[i], out1[i]) for i, k in enumerate(keys)}
+    out0 = dict(zip(keys, out0))
 
     wide = jnp.float32
     link = jnp.bfloat16 if depth <= 4 else wide
 
-    def across(r, parts=(0, 1)):
-        halves = []
+    def chip_sums(r, *parts):
+        sums = []
         for b in reversed(range(lines)):
-            y0, y1 = combine(codes[r, b], *[results[r, b][i] for i in parts])
-            halves.append(y0 + swap_core(y1).astype(wide))
-        if lines > 1:
-            return halves[1] + swap_line(halves[0].astype(jnp.bfloat16)).astype(wide)
-        return halves[0]
+            y0, y1 = combine(codes[r, b], *[part[r, b] for part in parts])
+            sums.append(y0 + swap_core(y1).astype(wide))
+        return sums[::-1]
+
+    def lined(sums):
+        return sums[0] + swap_line(sums[1].astype(link)).astype(wide) if lines > 1 else sums[0]
+
+    if lines > 1 and depth == 4:
+        early = chip_sums(2, out0)
+        token, first_half, hidden = tie(token, early[1].astype(link), hidden)
+        cross2 = swap_line(first_half)
+        token, hidden = fence(token, hidden)
+        out1 = dict(zip(keys, finish(hidden, w_down, part, len(keys))))
+        token, out1[2, 1] = tie(token, out1[2, 1])
+        rest = [(1, 0), (1, 1), (0, 0), (0, 1)]
+        half, third = chip_sums(2, out1), chip_sums(3, out0, out1)
+        aside, cross3, *tied = tie(half[1].astype(link), third[1].astype(link), *[codes[k] for k in rest])
+        codes.update(zip(rest, tied))
+        aside, cross3, ahead = to_above(aside), swap_line(cross3), to_above(half[0].astype(link))
+        token, cross2 = fence(token, cross2)
+        behind = to_above((early[0] + cross2).astype(link))
+        nearest, own = chip_sums(1, out0, out1), chip_sums(0, out0, out1)
+        token, aside = fence(token, aside)
+        cross1 = jnp.concatenate([nearest[1][:, :part], nearest[1][:, part:] + aside], axis=1).astype(link)
+        cross1 = swap_line(cross1)
+        token, last, cross3 = fence(token, own[1].astype(link), cross3)
+        below = to_below((third[0] + cross3).astype(link))
+        cross0 = swap_line(last)
+        token, cross1, behind, ahead = fence(token, cross1, behind, ahead)
+        above = to_above((nearest[0] + cross1 + jnp.concatenate([behind, ahead], axis=1)).astype(link))
+        return last_sum(token, own[0], cross0, above, below)
+
+    out1 = dict(zip(keys, finish(hidden, w_down, part, len(keys))))
+
+    def all_sums(r):
+        sums = chip_sums(r, out0, out1)
+        return sums[0] + swap_line(sums[1].astype(link)).astype(wide) if lines > 1 else sums[0]
+
+    def onward(move, value):
+        return move(value.astype(link)).astype(wide)
 
     got_up = got_down = 0.0
     for d in range(nearer, 0, -1):
-        if d == nearer:
-            got_up = [to_above(across(d, (i,)).astype(link)).astype(wide) for i in range(2)]
-            got_up = jnp.concatenate(got_up, axis=1)
-        else:
-            got_up = to_above((across(d) + got_up).astype(link)).astype(wide)
+        got_up = onward(to_above, all_sums(d) + got_up)
         if depth - d > nearer:
-            got_down = to_below((across(depth - d) + got_down).astype(link)).astype(wide)
-    return (across(0) + got_up + got_down).astype(jnp.bfloat16)
+            got_down = onward(to_below, all_sums(depth - d) + got_down)
+    return (all_sums(0) + got_up + got_down).astype(jnp.bfloat16)
 
 
 def solution(mesh):

time: 153 us -> 141 us (0.922)
  waiting for transfers between devices: 76.4 us -> 72.5 us
  other arithmetic: 4.9 us -> 1.35 us
  local copies, waits for them, and re-layouts: 3.85 us -> 1.15 us
  starting transfers between devices: 28.7 us -> 27.1 us
    ppermute x36, waiting for transfers between devices: 76.4 us -> 72.5 us  [send(): lax.ppermute(value, 'exp', [(place(*who), place(*move(*who))) for who in...]
    pallas_call x0 -> x13, Pallas kernels: none -> 3.02 us  [the longest x1 1.93 us: with_routes(): pl.pallas_call(routes_kernel, out_shape=jax.ShapeDtypeStruct((tok, LANES...]
    convert_element_type x12 -> x8, other arithmetic: 3.8 us -> 1 us  [the longest x1 0.3 us: body(): (nearest[0] + cross1 + jnp.concatenate([behind, ahead], axis=1)).astype(l...]
    pallas_call x8, Pallas kernels: 7.85 us -> 5.06 us  [dispatch(): pl.pallas_call(functools.partial(dispatch_kernel, top), in_specs=[pl.Bloc...]
    unnamed x8 -> x2, local copies, waits for them, and re-layouts: 3.69 us -> 1.08 us
    ppermute x36, starting transfers between devices: 28.7 us -> 27.1 us  [send(): lax.ppermute(value, 'exp', [(place(*who), place(*move(*who))) for who in...]
  transfers between devices with their start and end apart: 36 -> 36, of which waited for: 15 -> 14; matrix products, arithmetic and copies ran while one was open for 1% -> 1% of each run, Pallas kernels for 17% -> 17%
where the time goes in v5:
time: 141 us; the launch traced here: 140 us
  waiting for transfers between devices  72.5 us (51%)
  Pallas kernels  38 us (27%)
  starting transfers between devices  27.1 us (19%)
    ppermute x36, waiting for transfers between devices, send(): lax.ppermute(value, 'exp', [(place(*who), place(*move(*who))) for who in...  72.5 us
    ppermute x36, starting transfers between devices, send(): lax.ppermute(value, 'exp', [(place(*who), place(*move(*who))) for who in...  27.1 us
    pallas_call x1, Pallas kernels, middle(): pl.pallas_call(functools.partial(middle_kernel, pairs, part), in_specs=[V...  11.1 us
    pallas_call x1, Pallas kernels, begin(): pl.pallas_call(functools.partial(begin_kernel, pairs, part), in_specs=[VM...  9.2 us
    pallas_call x1, Pallas kernels, finish(): pl.pallas_call(functools.partial(finish_kernel, pairs, part), in_specs=[V...  5.29 us
    pallas_call x8, Pallas kernels, dispatch(): pl.pallas_call(functools.partial(dispatch_kernel, top), in_specs=[pl.Bloc...  5.06 us
    pallas_call x10, Pallas kernels, combine(): pl.pallas_call(combine_kernel, out_shape=(jax.ShapeDtypeStruct((tok, widt...  4.01 us
  transfers between devices with their start and end apart: 36, of which 14 were waited for; matrix products, arithmetic and copies ran while one was open for 1% of the time, Pallas kernels for 17%

profile of v5, /device:TPU:0, one launch (start us, length us, event | category | flops | bytes accessed | tf_op | source)
XLA Modules:
  0.0 140.5 jit_solution(5410036860310069210)
XLA Ops:
  0.0 1.9 %shard_map.65.x0_ref = bf16[128,2176]{1,0:T(8,128)(2,1)} custom-call(s32[8,128]{1,0:T(8,128)} %bitcast.3, f32[8,128]{1,0:T(8,128)} %bitcast.4, bf16[128,2048]{1,0:T(8,128)(2,1)} %tokens_ref.1), custom_call_target="tpu_custom_call" | custom-call | tf_op jit(solution)/shard_map/pallas_call | solution.py:46
  1.9 3.0 %collective-permute-start.3 = (bf16[128,2176]{1,0:T(8,128)(2,1)}, bf16[128,2176]{1,0:T(8,128)(2,1)}, u32[]{:S(2)}, u32[]{:S(2)}) collective-permute-start(bf16[128,2176]{1,0:T(8,128)(2,1)} %shard_map.65.x0_ref), channel_id=1, source_target_pairs={{0,2},{1,3},{2,0},{3,1},{4,6},{5,7},{6,4},{7,5},{8,10},{9,11},{10,... | collective-permute-start | bytes 1671176 | tf_op jit(solution)/shard_map/ppermute | solution.py:376
  4.9 3.6 %collective-permute-start = (bf16[128,2176]{1,0:T(8,128)(2,1)}, bf16[128,2176]{1,0:T(8,128)(2,1)S(1)}, u32[]{:S(2)}, u32[]{:S(2)}) collective-permute-start(bf16[128,2176]{1,0:T(8,128)(2,1)} %shard_map.65.x0_ref), channel_id=1, source_target_pairs={{0,12},{1,13},{2,14},{3,15},{4,0},{5,1},{6,2},{7,3},{8,4},{9,5},{1... | collective-permute-start | bytes 1671176 | tf_op jit(solution)/shard_map/ppermute | solution.py:376
  8.5 1.1 copy-done
  9.6 12.2 %collective-permute-done.x0_ref = bf16[128,2176]{1,0:T(8,128)(2,1)S(1)} collective-permute-done((bf16[128,2176]{1,0:T(8,128)(2,1)}, bf16[128,2176]{1,0:T(8,128)(2,1)S(1)}, u32[]{:S(2)}, u32[]{:S(2)}) %collective-permute-start) | collective-permute-done | bytes 557088 | tf_op jit(solution)/shard_map/ppermute | solution.py:376
  21.8 0.5 collective-permute-start.8
  22.3 4.2 %collective-permute-start.5 = (bf16[128,2176]{1,0:T(8,128)(2,1)S(1)}, bf16[128,2176]{1,0:T(8,128)(2,1)S(1)}, u32[]{:S(2)}, u32[]{:S(2)}) collective-permute-start(bf16[128,2176]{1,0:T(8,128)(2,1)S(1)} %collective-permute-done.x0_ref), channel_id=1, source_target_pairs={{0,12},{1,13},{2,14},{3,15},{4,0},{5,1},{6,2},{7,3},{8,4},{9,5},{1... | collective-permute-start | bytes 1671176 | tf_op jit(solution)/shard_map/ppermute | solution.py:376
  26.5 0.5 shard_map.68
  27.0 7.5 %collective-permute-done.2.x0_ref = bf16[128,2176]{1,0:T(8,128)(2,1)S(1)} collective-permute-done((bf16[128,2176]{1,0:T(8,128)(2,1)S(1)}, bf16[128,2176]{1,0:T(8,128)(2,1)S(1)}, u32[]{:S(2)}, u32[]{:S(2)}) %collective-permute-start.2) | collective-permute-done | bytes 557088 | tf_op jit(solution)/shard_map/ppermute | solution.py:376
  34.5 0.5 collective-permute-start.10
  35.1 0.5 collective-permute-start.7
  35.6 0.5 shard_map.70
  36.2 9.9 %collective-permute-done.5.x0_ref = bf16[128,2176]{1,0:T(8,128)(2,1)S(1)} collective-permute-done((bf16[128,2176]{1,0:T(8,128)(2,1)S(1)}, bf16[128,2176]{1,0:T(8,128)(2,1)S(1)}, u32[]{:S(2)}, u32[]{:S(2)}) %collective-permute-start.5) | collective-permute-done | bytes 557088 | tf_op jit(solution)/shard_map/ppermute | solution.py:376
  46.3 0.5 collective-permute-start.11
  46.8 0.5 shard_map.72
  47.3 1.6 %shard_map.73 = (bf16[4,48,2048]{2,1,0:T(8,128)(2,1)S(1)}, s32[2,4,128]{2,1,0:T(4,128)S(1)}, f32[4,48,128]{2,1,0:T(8,128)S(1)}) custom-call(s32[1]{0:T(128)} %bitcast.2.first_ref, bf16[128,2176]{1,0:T(8,128)(2,1)} %collective-permute-done.3.x0_ref, bf16[128,2176]{1,0:T(8,128)(2,1)S(1)} %collective-permute-done.7.x1_ref), custom_call_target="tpu_custom_call" | custom-call | tf_op jit(solution)/shard_map/pallas_call | solution.py:108
  48.9 0.5 shard_map.74
  49.4 6.2 %collective-permute-done.11.x0_ref = bf16[128,1152]{1,0:T(8,128)(2,1)S(1)} collective-permute-done((bf16[128,1152]{1,0:T(8,128)(2,1)S(1)}, bf16[128,1152]{1,0:T(8,128)(2,1)S(1)}, u32[]{:S(2)}, u32[]{:S(2)}) %collective-permute-start.11) | collective-permute-done | bytes 294944 | tf_op jit(solution)/shard_map/ppermute | solution.py:376
  55.6 0.5 collective-permute-start.12
  56.2 0.6 collective-permute-start.14
  56.8 0.5 shard_map.77
  57.3 0.7 collective-permute-done.12.x1_ref
  58.4 0.5 shard_map.78
  59.0 9.2 %shard_map.79 = (f32[4,384,768]{2,1,0:T(8,128)S(1)}, f32[4,384,768]{2,1,0:T(8,128)S(1)}) custom-call(f32[8,128]{1,0:T(8,128)S(1)} %shard_map.75.token_ref.in_ref, bf16[4,48,2048]{2,1,0:T(8,128)(2,1)S(1)} %get-tuple-element.155.refs_0_, bf16[4,48,2048]{2,1,0:T(8,128)(2,1)S(1)} %get-tuple-element.156.refs_1_, ...), custom_call_target="tpu_custom_call" | custom-call | flops 40000000000 | tf_op jit(solution)/shard_map/pallas_call | solution.py:211
  68.4 1.4 %collective-permute-done.16.x1_ref = bf16[128,1024]{1,0:T(8,128)(2,1)S(1)} collective-permute-done((bf16[128,1024]{1,0:T(8,128)(2,1)S(1)}, bf16[128,1024]{1,0:T(8,128)(2,1)S(1)}, u32[]{:S(2)}, u32[]{:S(2)}) %collective-permute-start.16) | collective-permute-done | bytes 262176 | tf_op jit(solution)/shard_map/ppermute | solution.py:376
  70.1 11.1 %shard_map.81 = (bf16[4,384,768]{2,1,0:T(8,128)(2,1)S(1)}, bf16[4,48,1024]{2,1,0:T(8,128)(2,1)S(1)}, bf16[4,48,1024]{2,1,0:T(8,128)(2,1)S(1)}, bf16[4,48,1024]{2...) custom-call(bf16[4,48,2048]{2,1,0:T(8,128)(2,1)S(1)} %get-tuple-elem, ...), custom_call_target="tpu_custom_call" | custom-call | tf_op jit(solution)/shard_map/pallas_call | solution.py:259
  82.5 0.6 collective-permute-done.17
  83.2 0.8 collective-permute-start.18
  84.0 5.3 %shard_map.84 = (bf16[4,48,1024]{2,1,0:T(8,128)(2,1)S(1)}, bf16[4,48,1024]{2,1,0:T(8,128)(2,1)S(1)}, bf16[4,48,1024]{2,1,0:T(8,128)(2,1)S(1)}, bf16[4,48,1024]{2...) custom-call(bf16[4,384,768]{2,1,0:T(8,128)(2,1)S(1)} %get-tuple-elem, ...), custom_call_target="tpu_custom_call" | custom-call | tf_op jit(solution)/shard_map/pallas_call | solution.py:285
  90.1 0.6 collective-permute-start.28
  91.6 0.6 collective-permute-start.34
  92.3 0.8 collective-permute-done.20
  93.2 0.7 collective-permute-start.21
  94.0 0.7 collective-permute-start.27
  94.8 1.3 collective-permute-start.23
  97.1 0.5 shard_map.95
  97.5 0.5 shard_map.96
  98.0 6.2 %collective-permute-done.21 = bf16[128,1024]{1,0:T(8,128)(2,1)S(1)} collective-permute-done((bf16[128,1024]{1,0:T(8,128)(2,1)S(1)}, bf16[128,1024]{1,0:T(8,128)(2,1)S(1)}, u32[]{:S(2)}, u32[]{:S(2)}) %collective-permute-start.21) | collective-permute-done | bytes 262176 | tf_op jit(solution)/shard_map/ppermute | solution.py:376
  104.4 3.9 %collective-permute-done.23 = bf16[128,2048]{1,0:T(8,128)(2,1)S(1)} collective-permute-done((bf16[128,2048]{1,0:T(8,128)(2,1)S(1)}, bf16[128,2048]{1,0:T(8,128)(2,1)S(1)}, u32[]{:S(2)}, u32[]{:S(2)}) %collective-permute-start.23) | collective-permute-done | bytes 524320 | tf_op jit(solution)/shard_map/ppermute | solution.py:376
  108.5 1.3 collective-permute-start.25
  110.3 0.9 collective-permute-start.31
  111.2 3.5 %collective-permute-done.29 = bf16[128,1024]{1,0:T(8,128)(2,1)S(1)} collective-permute-done((bf16[128,1024]{1,0:T(8,128)(2,1)S(1)}, bf16[128,1024]{1,0:T(8,128)(2,1)S(1)}, u32[]{:S(2)}, u32[]{:S(2)}) %collective-permute-start.29) | collective-permute-done | bytes 262176 | tf_op jit(solution)/shard_map/ppermute | solution.py:376
  114.7 1.5 %collective-permute-start.35 = (bf16[128,2048]{1,0:T(8,128)(2,1)S(1)}, bf16[128,2048]{1,0:T(8,128)(2,1)S(1)}, u32[]{:S(2)}, u32[]{:S(2)}) collective-permute-start(bf16[128,2048]{1,0:T(8,128)(2,1)S(1)} %add_convert_fusion), channel_id=1, source_target_pairs={{0,12},{1,13},{2,14},{3,15},{4,0},{5,1},{6,2},{7,3},{8,4},{9,5},{1... | collective-permute-start | bytes 1572872 | tf_op jit(solution)/shard_map/ppermute | solution.py:376
  116.2 7.1 %collective-permute-done.25 = bf16[128,2048]{1,0:T(8,128)(2,1)S(1)} collective-permute-done((bf16[128,2048]{1,0:T(8,128)(2,1)S(1)}, bf16[128,2048]{1,0:T(8,128)(2,1)S(1)}, u32[]{:S(2)}, u32[]{:S(2)}) %collective-permute-start.25) | collective-permute-done | bytes 524320 | tf_op jit(solution)/shard_map/ppermute | solution.py:376
  123.6 3.4 %collective-permute-start.33 = (bf16[128,2048]{1,0:T(8,128)(2,1)S(1)}, bf16[128,2048]{1,0:T(8,128)(2,1)S(1)}, u32[]{:S(2)}, u32[]{:S(2)}) collective-permute-start(bf16[128,2048]{1,0:T(8,128)(2,1)S(1)} %add_convert_fusion.1), channel_id=1, source_target_pairs={{0,4},{1,5},{2,6},{3,7},{4,8},{5,9},{6,10},{7,11},{8,12},{9,13},{1... | collective-permute-start | bytes 1572872 | tf_op jit(solution)/shard_map/ppermute | solution.py:376
  127.2 7.0 %collective-permute-done.31.refs_0_ = bf16[128,2048]{1,0:T(8,128)(2,1)S(1)} collective-permute-done((bf16[128,2048]{1,0:T(8,128)(2,1)S(1)}, bf16[128,2048]{1,0:T(8,128)(2,1)S(1)}, u32[]{:S(2)}, u32[]{:S(2)}) %collective-permute-start.31) | collective-permute-done | bytes 524320 | tf_op jit(solution)/shard_map/ppermute | solution.py:376
  134.2 5.3 %collective-permute-done.35.refs_2_ = bf16[128,2048]{1,0:T(8,128)(2,1)S(1)} collective-permute-done((bf16[128,2048]{1,0:T(8,128)(2,1)S(1)}, bf16[128,2048]{1,0:T(8,128)(2,1)S(1)}, u32[]{:S(2)}, u32[]{:S(2)}) %collective-permute-start.35) | collective-permute-done | bytes 524320 | tf_op jit(solution)/shard_map/ppermute | solution.py:376
  139.4 1.1 shard_map.98
  (77 shorter events, 6.8 us)
Async XLA Ops:
  1.9 32.6 %collective-permute-start.3 = (bf16[128,2176]{1,0:T(8,128)(2,1)}, bf16[128,2176]{1,0:T(8,128)(2,1)}, u32[]{:S(2)}, u32[]{:S(2)}) collective-permute-start(bf16[128,2176]{1,0:T(8,128)(2,1)} %shard_map.65.x0_ref), channel_id=1, source_target_pairs={{0,2},{1,3},{2,0},{3,1},{4,6},{5,7},{6,4},{7,5},{8,10},{9,11},{10,... | collective-permute-start | bytes 1671176 | tf_op jit(solution)/shard_map/ppermute | solution.py:376
  4.9 4.7 %collective-permute-start.1 = (bf16[128,2176]{1,0:T(8,128)(2,1)}, bf16[128,2176]{1,0:T(8,128)(2,1)S(1)}, u32[]{:S(2)}, u32[]{:S(2)}) collective-permute-start(bf16[128,2176]{1,0:T(8,128)(2,1)} %shard_map.65.x0_ref), channel_id=1, source_target_pairs={{0,1},{1,0},{2,3},{3,2},{4,5},{5,4},{6,7},{7,6},{8,9},{9,8},{10,11... | collective-permute-start | bytes 1671176 | tf_op jit(solution)/shard_map/ppermute | solution.py:376
  4.9 16.9 %collective-permute-start = (bf16[128,2176]{1,0:T(8,128)(2,1)}, bf16[128,2176]{1,0:T(8,128)(2,1)S(1)}, u32[]{:S(2)}, u32[]{:S(2)}) collective-permute-start(bf16[128,2176]{1,0:T(8,128)(2,1)} %shard_map.65.x0_ref), channel_id=1, source_target_pairs={{0,12},{1,13},{2,14},{3,15},{4,0},{5,1},{6,2},{7,3},{8,4},{9,5},{1... | collective-permute-start | bytes 1671176 | tf_op jit(solution)/shard_map/ppermute | solution.py:376
  8.5 1.1 copy-start
  9.6 24.9 %collective-permute-start.2 = (bf16[128,2176]{1,0:T(8,128)(2,1)S(1)}, bf16[128,2176]{1,0:T(8,128)(2,1)S(1)}, u32[]{:S(2)}, u32[]{:S(2)}) collective-permute-start(bf16[128,2176]{1,0:T(8,128)(2,1)S(1)} %copy-done), channel_id=1, source_target_pairs={{0,4},{1,5},{2,6},{3,7},{4,8},{5,9},{6,10},{7,11},{8,12},{9,13},{1... | collective-permute-start | bytes 1671176 | tf_op jit(solution)/shard_map/ppermute | solution.py:376
  21.8 14.3 %collective-permute-start.8 = (bf16[128,2176]{1,0:T(8,128)(2,1)S(1)}, bf16[128,2176]{1,0:T(8,128)(2,1)S(1)}, u32[]{:S(2)}, u32[]{:S(2)}) collective-permute-start(bf16[128,2176]{1,0:T(8,128)(2,1)S(1)} %collective-permute-done.x0_ref), channel_id=1, source_target_pairs={{0,2},{1,3},{2,0},{3,1},{4,6},{5,7},{6,4},{7,5},{8,10},{9,11},{10,... | collective-permute-start | bytes 1671176 | tf_op jit(solution)/shard_map/ppermute | solution.py:376
  22.3 12.2 %collective-permute-start.4 = (bf16[128,2176]{1,0:T(8,128)(2,1)S(1)}, bf16[128,2176]{1,0:T(8,128)(2,1)S(1)}, u32[]{:S(2)}, u32[]{:S(2)}) collective-permute-start(bf16[128,2176]{1,0:T(8,128)(2,1)S(1)} %collective-permute-done.x0_ref), channel_id=1, source_target_pairs={{0,1},{1,0},{2,3},{3,2},{4,5},{5,4},{6,7},{7,6},{8,9},{9,8},{10,11... | collective-permute-start | bytes 1671176 | tf_op jit(solution)/shard_map/ppermute | solution.py:376
  22.3 23.8 %collective-permute-start.5 = (bf16[128,2176]{1,0:T(8,128)(2,1)S(1)}, bf16[128,2176]{1,0:T(8,128)(2,1)S(1)}, u32[]{:S(2)}, u32[]{:S(2)}) collective-permute-start(bf16[128,2176]{1,0:T(8,128)(2,1)S(1)} %collective-permute-done.x0_ref), channel_id=1, source_target_pairs={{0,12},{1,13},{2,14},{3,15},{4,0},{5,1},{6,2},{7,3},{8,4},{9,5},{1... | collective-permute-start | bytes 1671176 | tf_op jit(solution)/shard_map/ppermute | solution.py:376
  34.5 14.9 %collective-permute-start.10 = (bf16[128,2176]{1,0:T(8,128)(2,1)S(1)}, bf16[128,2176]{1,0:T(8,128)(2,1)S(1)}, u32[]{:S(2)}, u32[]{:S(2)}) collective-permute-start(bf16[128,2176]{1,0:T(8,128)(2,1)S(1)} %collective-permute-done.2.x0_ref), channel_id=1, source_target_pairs={{0,2},{1,3},{2,0},{3,1},{4,6},{5,7},{6,4},{7,5},{8,10},{9,11},{10,... | collective-permute-start | bytes 1671176 | tf_op jit(solution)/shard_map/ppermute | solution.py:376
  35.1 11.0 %collective-permute-start.6 = (bf16[128,2176]{1,0:T(8,128)(2,1)S(1)}, bf16[128,2176]{1,0:T(8,128)(2,1)S(1)}, u32[]{:S(2)}, u32[]{:S(2)}) collective-permute-start(bf16[128,2176]{1,0:T(8,128)(2,1)S(1)} %collective-permute-done.2.x0_ref), channel_id=1, source_target_pairs={{0,1},{1,0},{2,3},{3,2},{4,5},{5,4},{6,7},{7,6},{8,9},{9,8},{10,11... | collective-permute-start | bytes 1671176 | tf_op jit(solution)/shard_map/ppermute | solution.py:376
  35.1 11.0 %collective-permute-start.7 = (bf16[128,2176]{1,0:T(8,128)(2,1)}, bf16[128,2176]{1,0:T(8,128)(2,1)S(1)}, u32[]{:S(2)}, u32[]{:S(2)}) collective-permute-start(bf16[128,2176]{1,0:T(8,128)(2,1)} %collective-permute-done.3.x0_ref), channel_id=1, source_target_pairs={{0,1},{1,0},{2,3},{3,2},{4,5},{5,4},{6,7},{7,6},{8,9},{9,8},{10,11... | collective-permute-start | bytes 1671176 | tf_op jit(solution)/shard_map/ppermute | solution.py:376
  36.1 10.0 %collective-permute-start.9 = (bf16[128,2176]{1,0:T(8,128)(2,1)S(1)}, bf16[128,2176]{1,0:T(8,128)(2,1)S(1)}, u32[]{:S(2)}, u32[]{:S(2)}) collective-permute-start(bf16[128,2176]{1,0:T(8,128)(2,1)S(1)} %collective-permute-done.8.x0_ref), channel_id=1, source_target_pairs={{0,1},{1,0},{2,3},{3,2},{4,5},{5,4},{6,7},{7,6},{8,9},{9,8},{10,11... | collective-permute-start | bytes 1671176 | tf_op jit(solution)/shard_map/ppermute | solution.py:376
  46.1 10.6 %collective-permute-start.13 = (bf16[128,2176]{1,0:T(8,128)(2,1)S(1)}, bf16[128,2176]{1,0:T(8,128)(2,1)S(1)}, u32[]{:S(2)}, u32[]{:S(2)}) collective-permute-start(bf16[128,2176]{1,0:T(8,128)(2,1)S(1)} %collective-permute-done.5.x0_ref), channel_id=1, source_target_pairs={{0,1},{1,0},{2,3},{3,2},{4,5},{5,4},{6,7},{7,6},{8,9},{9,8},{10,11... | collective-permute-start | bytes 1671176 | tf_op jit(solution)/shard_map/ppermute | solution.py:376
  46.3 9.4 %collective-permute-start.11 = (bf16[128,1152]{1,0:T(8,128)(2,1)S(1)}, bf16[128,1152]{1,0:T(8,128)(2,1)S(1)}, u32[]{:S(2)}, u32[]{:S(2)}) collective-permute-start(bf16[128,1152]{1,0:T(8,128)(2,1)S(1)} %slice.13), channel_id=1, source_target_pairs={{0,2},{1,3},{2,0},{3,1},{4,6},{5,7},{6,4},{7,5},{8,10},{9,11},{10,... | collective-permute-start | bytes 884744 | tf_op jit(solution)/shard_map/ppermute | solution.py:376
  55.6 2.8 %collective-permute-start.15 = (bf16[128,2176]{1,0:T(8,128)(2,1)S(1)}, bf16[128,2176]{1,0:T(8,128)(2,1)S(1)}, u32[]{:S(2)}, u32[]{:S(2)}) collective-permute-start(bf16[128,2176]{1,0:T(8,128)(2,1)S(1)} %collective-permute-done.10.x0_ref), channel_id=1, source_target_pairs={{0,1},{1,0},{2,3},{3,2},{4,5},{5,4},{6,7},{7,6},{8,9},{9,8},{10,11... | collective-permute-start | bytes 1671176 | tf_op jit(solution)/shard_map/ppermute | solution.py:376
  55.6 2.4 %collective-permute-start.12 = (bf16[128,1152]{1,0:T(8,128)(2,1)S(1)}, bf16[128,1152]{1,0:T(8,128)(2,1)S(1)}, u32[]{:S(2)}, u32[]{:S(2)}) collective-permute-start(bf16[128,1152]{1,0:T(8,128)(2,1)S(1)} %collective-permute-done.11.x0_ref), channel_id=1, source_target_pairs={{0,1},{1,0},{2,3},{3,2},{4,5},{5,4},{6,7},{7,6},{8,9},{9,8},{10,11... | collective-permute-start | bytes 884744 | tf_op jit(solution)/shard_map/ppermute | solution.py:376
  56.2 12.0 %collective-permute-start.14 = (bf16[128,1024]{1,0:T(8,128)(2,1)S(1)}, bf16[128,1024]{1,0:T(8,128)(2,1)S(1)}, u32[]{:S(2)}, u32[]{:S(2)}) collective-permute-start(bf16[128,1024]{1,0:T(8,128)(2,1)S(1)} %slice.14), channel_id=1, source_target_pairs={{0,2},{1,3},{2,0},{3,1},{4,6},{5,7},{6,4},{7,5},{8,10},{9,11},{10,... | collective-permute-start | bytes 786440 | tf_op jit(solution)/shard_map/ppermute | solution.py:376
  68.2 1.6 %collective-permute-start.16 = (bf16[128,1024]{1,0:T(8,128)(2,1)S(1)}, bf16[128,1024]{1,0:T(8,128)(2,1)S(1)}, u32[]{:S(2)}, u32[]{:S(2)}) collective-permute-start(bf16[128,1024]{1,0:T(8,128)(2,1)S(1)} %collective-permute-done.14.x0_ref), channel_id=1, source_target_pairs={{0,1},{1,0},{2,3},{3,2},{4,5},{5,4},{6,7},{7,6},{8,9},{9,8},{10,11... | collective-permute-start | bytes 786440 | tf_op jit(solution)/shard_map/ppermute | solution.py:376
  81.5 1.6 %collective-permute-start.17 = (bf16[128,1024]{1,0:T(8,128)(2,1)S(1)}, bf16[128,1024]{1,0:T(8,128)(2,1)S(1)}, u32[]{:S(2)}, u32[]{:S(2)}) collective-permute-start(bf16[128,1024]{1,0:T(8,128)(2,1)S(1)} %get-tuple-element.179), channel_id=1, source_target_pairs={{0,1},{1,0},{2,3},{3,2},{4,5},{5,4},{6,7},{7,6},{8,9},{9,8},{10,11... | collective-permute-start | bytes 786440 | tf_op jit(solution)/shard_map/ppermute | solution.py:376
  82.0 11.9 %collective-permute-start.26 = (bf16[128,1024]{1,0:T(8,128)(2,1)S(1)}, bf16[128,1024]{1,0:T(8,128)(2,1)S(1)}, u32[]{:S(2)}, u32[]{:S(2)}) collective-permute-start(bf16[128,1024]{1,0:T(8,128)(2,1)S(1)} %get-tuple-element.219), channel_id=1, source_target_pairs={{0,1},{1,0},{2,3},{3,2},{4,5},{5,4},{6,7},{7,6},{8,9},{9,8},{10,11... | collective-permute-start | bytes 786440 | tf_op jit(solution)/shard_map/ppermute | solution.py:376
  83.2 8.4 %collective-permute-start.18 = (bf16[128,1024]{1,0:T(8,128)(2,1)S(1)}, bf16[128,1024]{1,0:T(8,128)(2,1)S(1)}, u32[]{:S(2)}, u32[]{:S(2)}) collective-permute-start(bf16[128,1024]{1,0:T(8,128)(2,1)S(1)} %add_convert_fusion.7), channel_id=1, source_target_pairs={{0,2},{1,3},{2,0},{3,1},{4,6},{5,7},{6,4},{7,5},{8,10},{9,11},{10,... | collective-permute-start | bytes 786440 | tf_op jit(solution)/shard_map/ppermute | solution.py:376
  89.7 2.6 %collective-permute-start.19 = (bf16[128,1024]{1,0:T(8,128)(2,1)S(1)}, bf16[128,1024]{1,0:T(8,128)(2,1)S(1)}, u32[]{:S(2)}, u32[]{:S(2)}) collective-permute-start(bf16[128,1024]{1,0:T(8,128)(2,1)S(1)} %get-tuple-element.191), channel_id=1, source_target_pairs={{0,1},{1,0},{2,3},{3,2},{4,5},{5,4},{6,7},{7,6},{8,9},{9,8},{10,11... | collective-permute-start | bytes 786440 | tf_op jit(solution)/shard_map/ppermute | solution.py:376
  90.1 4.6 %collective-permute-start.28 = (bf16[128,1024]{1,0:T(8,128)(2,1)S(1)}, bf16[128,1024]{1,0:T(8,128)(2,1)S(1)}, u32[]{:S(2)}, u32[]{:S(2)}) collective-permute-start(bf16[128,1024]{1,0:T(8,128)(2,1)S(1)} %get-tuple-element.223), channel_id=1, source_target_pairs={{0,1},{1,0},{2,3},{3,2},{4,5},{5,4},{6,7},{7,6},{8,9},{9,8},{10,11... | collective-permute-start | bytes 786440 | tf_op jit(solution)/shard_map/ppermute | solution.py:376
  91.1 2.0 %collective-permute-start.20 = (bf16[128,2048]{1,0:T(8,128)(2,1)S(1)}, bf16[128,2048]{1,0:T(8,128)(2,1)S(1)}, u32[]{:S(2)}, u32[]{:S(2)}) collective-permute-start(bf16[128,2048]{1,0:T(8,128)(2,1)S(1)} %get-tuple-element.196), channel_id=1, source_target_pairs={{0,1},{1,0},{2,3},{3,2},{4,5},{5,4},{6,7},{7,6},{8,9},{9,8},{10,11... | collective-permute-start | bytes 1572872 | tf_op jit(solution)/shard_map/ppermute | solution.py:376
  91.6 18.2 %collective-permute-start.34 = (bf16[128,2048]{1,0:T(8,128)(2,1)S(1)}, bf16[128,2048]{1,0:T(8,128)(2,1)S(1)}, u32[]{:S(2)}, u32[]{:S(2)}) collective-permute-start(bf16[128,2048]{1,0:T(8,128)(2,1)S(1)} %get-tuple-element.243), channel_id=1, source_target_pairs={{0,1},{1,0},{2,3},{3,2},{4,5},{5,4},{6,7},{7,6},{8,9},{9,8},{10,11... | collective-permute-start | bytes 1572872 | tf_op jit(solution)/shard_map/ppermute | solution.py:376
  93.2 11.0 %collective-permute-start.21 = (bf16[128,1024]{1,0:T(8,128)(2,1)S(1)}, bf16[128,1024]{1,0:T(8,128)(2,1)S(1)}, u32[]{:S(2)}, u32[]{:S(2)}) collective-permute-start(bf16[128,1024]{1,0:T(8,128)(2,1)S(1)} %add_convert_fusion.6), channel_id=1, source_target_pairs={{0,4},{1,5},{2,6},{3,7},{4,8},{5,9},{6,10},{7,11},{8,12},{9,13},{1... | collective-permute-start | bytes 786440 | tf_op jit(solution)/shard_map/ppermute | solution.py:376
  94.0 16.3 %collective-permute-start.27 = (bf16[128,1024]{1,0:T(8,128)(2,1)S(1)}, bf16[128,1024]{1,0:T(8,128)(2,1)S(1)}, u32[]{:S(2)}, u32[]{:S(2)}) collective-permute-start(bf16[128,1024]{1,0:T(8,128)(2,1)S(1)} %add_convert_fusion.5), channel_id=1, source_target_pairs={{0,4},{1,5},{2,6},{3,7},{4,8},{5,9},{6,10},{7,11},{8,12},{9,13},{1... | collective-permute-start | bytes 786440 | tf_op jit(solution)/shard_map/ppermute | solution.py:376
  94.8 13.5 %collective-permute-start.23 = (bf16[128,2048]{1,0:T(8,128)(2,1)S(1)}, bf16[128,2048]{1,0:T(8,128)(2,1)S(1)}, u32[]{:S(2)}, u32[]{:S(2)}) collective-permute-start(bf16[128,2048]{1,0:T(8,128)(2,1)S(1)} %add_convert_fusion.3), channel_id=1, source_target_pairs={{0,2},{1,3},{2,0},{3,1},{4,6},{5,7},{6,4},{7,5},{8,10},{9,11},{10,... | collective-permute-start | bytes 1572872 | tf_op jit(solution)/shard_map/ppermute | solution.py:376
  96.5 7.7 %collective-permute-start.22 = (bf16[128,2048]{1,0:T(8,128)(2,1)S(1)}, bf16[128,2048]{1,0:T(8,128)(2,1)S(1)}, u32[]{:S(2)}, u32[]{:S(2)}) collective-permute-start(bf16[128,2048]{1,0:T(8,128)(2,1)S(1)} %get-tuple-element.207), channel_id=1, source_target_pairs={{0,1},{1,0},{2,3},{3,2},{4,5},{5,4},{6,7},{7,6},{8,9},{9,8},{10,11... | collective-permute-start | bytes 1572872 | tf_op jit(solution)/shard_map/ppermute | solution.py:376
  104.2 4.1 %collective-permute-start.24 = (bf16[128,2048]{1,0:T(8,128)(2,1)S(1)}, bf16[128,2048]{1,0:T(8,128)(2,1)S(1)}, u32[]{:S(2)}, u32[]{:S(2)}) collective-permute-start(bf16[128,2048]{1,0:T(8,128)(2,1)S(1)} %get-tuple-element.214), channel_id=1, source_target_pairs={{0,1},{1,0},{2,3},{3,2},{4,5},{5,4},{6,7},{7,6},{8,9},{9,8},{10,11... | collective-permute-start | bytes 1572872 | tf_op jit(solution)/shard_map/ppermute | solution.py:376
  104.2 10.5 %collective-permute-start.29 = (bf16[128,1024]{1,0:T(8,128)(2,1)S(1)}, bf16[128,1024]{1,0:T(8,128)(2,1)S(1)}, u32[]{:S(2)}, u32[]{:S(2)}) collective-permute-start(bf16[128,1024]{1,0:T(8,128)(2,1)S(1)} %add_convert_fusion.4), channel_id=1, source_target_pairs={{0,4},{1,5},{2,6},{3,7},{4,8},{5,9},{6,10},{7,11},{8,12},{9,13},{1... | collective-permute-start | bytes 786440 | tf_op jit(solution)/shard_map/ppermute | solution.py:376
  108.2 15.1 %collective-permute-start.32 = (bf16[128,2048]{1,0:T(8,128)(2,1)S(1)}, bf16[128,2048]{1,0:T(8,128)(2,1)S(1)}, u32[]{:S(2)}, u32[]{:S(2)}) collective-permute-start(bf16[128,2048]{1,0:T(8,128)(2,1)S(1)} %get-tuple-element.235), channel_id=1, source_target_pairs={{0,1},{1,0},{2,3},{3,2},{4,5},{5,4},{6,7},{7,6},{8,9},{9,8},{10,11... | collective-permute-start | bytes 1572872 | tf_op jit(solution)/shard_map/ppermute | solution.py:376
  108.5 14.8 %collective-permute-start.25 = (bf16[128,2048]{1,0:T(8,128)(2,1)S(1)}, bf16[128,2048]{1,0:T(8,128)(2,1)S(1)}, u32[]{:S(2)}, u32[]{:S(2)}) collective-permute-start(bf16[128,2048]{1,0:T(8,128)(2,1)S(1)} %pad_maximum_fusion), channel_id=1, source_target_pairs={{0,2},{1,3},{2,0},{3,1},{4,6},{5,7},{6,4},{7,5},{8,10},{9,11},{10,... | collective-permute-start | bytes 1572872 | tf_op jit(solution)/shard_map/ppermute | solution.py:376
  109.8 17.2 %collective-permute-start.30 = (bf16[128,2048]{1,0:T(8,128)(2,1)S(1)}, bf16[128,2048]{1,0:T(8,128)(2,1)S(1)}, u32[]{:S(2)}, u32[]{:S(2)}) collective-permute-start(bf16[128,2048]{1,0:T(8,128)(2,1)S(1)} %get-tuple-element.229), channel_id=1, source_target_pairs={{0,1},{1,0},{2,3},{3,2},{4,5},{5,4},{6,7},{7,6},{8,9},{9,8},{10,11... | collective-permute-start | bytes 1572872 | tf_op jit(solution)/shard_map/ppermute | solution.py:376
  110.3 23.9 %collective-permute-start.31 = (bf16[128,2048]{1,0:T(8,128)(2,1)S(1)}, bf16[128,2048]{1,0:T(8,128)(2,1)S(1)}, u32[]{:S(2)}, u32[]{:S(2)}) collective-permute-start(bf16[128,2048]{1,0:T(8,128)(2,1)S(1)} %add_convert_fusion.2), channel_id=1, source_target_pairs={{0,2},{1,3},{2,0},{3,1},{4,6},{5,7},{6,4},{7,5},{8,10},{9,11},{10,... | collective-permute-start | bytes 1572872 | tf_op jit(solution)/shard_map/ppermute | solution.py:376
  114.7 24.7 %collective-permute-start.35 = (bf16[128,2048]{1,0:T(8,128)(2,1)S(1)}, bf16[128,2048]{1,0:T(8,128)(2,1)S(1)}, u32[]{:S(2)}, u32[]{:S(2)}) collective-permute-start(bf16[128,2048]{1,0:T(8,128)(2,1)S(1)} %add_convert_fusion), channel_id=1, source_target_pairs={{0,12},{1,13},{2,14},{3,15},{4,0},{5,1},{6,2},{7,3},{8,4},{9,5},{1... | collective-permute-start | bytes 1572872 | tf_op jit(solution)/shard_map/ppermute | solution.py:376
  123.6 15.8 %collective-permute-start.33 = (bf16[128,2048]{1,0:T(8,128)(2,1)S(1)}, bf16[128,2048]{1,0:T(8,128)(2,1)S(1)}, u32[]{:S(2)}, u32[]{:S(2)}) collective-permute-start(bf16[128,2048]{1,0:T(8,128)(2,1)S(1)} %add_convert_fusion.1), channel_id=1, source_target_pairs={{0,4},{1,5},{2,6},{3,7},{4,8},{5,9},{6,10},{7,11},{8,12},{9,13},{1... | collective-permute-start | bytes 1572872 | tf_op jit(solution)/shard_map/ppermute | solution.py:376

commit v6 on v5

--- a/solution.py
+++ b/solution.py
@@ -133,12 +133,12 @@
     return [range(p, min(p + 8, pairs)) for p in range(0, pairs, 8)]
 
 
-def columns_of(refs, part, chunk):
-    return [slice(chunk * part, (chunk + 1) * part) if r.shape[2] > part else slice(None) for r in refs]
-
-
-def rows_of(refs, local, part, chunk, block):
-    where = columns_of(refs, part, chunk)
+def columns_of(refs, first, last):
+    return [slice(first, last) if r.shape[2] > last - first else slice(None) for r in refs]
+
+
+def rows_of(refs, local, first, last, block):
+    where = columns_of(refs, first, last)
     return jnp.concatenate([refs[p][local, :, where[p]] for p in block], axis=0)
 
 
@@ -151,34 +151,26 @@
         self.hbm, self.buffer, self.sems, self.where = hbm, buffer, sems, (rows, columns)
 
     def copy(self, local):
-        slot = local % 2
-        return pltpu.make_async_copy(self.hbm.at[(local,) + self.where], self.buffer.at[slot], self.sems.at[slot])
+        return pltpu.make_async_copy(self.hbm.at[(local,) + self.where], self.buffer.at[local], self.sems.at[local])
 
     def start(self, local):
         self.copy(local).start()
 
     def get(self, local):
         self.copy(local).wait()
-        return self.buffer[local % 2]
+        return self.buffer[local]
 
 
 def over_experts(count, streams, work):
-    for stream in streams:
-        stream.start(0)
-
-    @pl.loop(0, count)
-    def _(local):
-        @pl.when(local + 1 < count)
-        def _():
-            for stream in streams:
-                stream.start(local + 1)
-
-        work(local)
-
-
-def stream_scratch(*shapes):
-    buffers = [pltpu.VMEM((2,) + shape, jnp.bfloat16) for shape in shapes]
-    return buffers + [pltpu.SemaphoreType.DMA((2,)) for _ in shapes]
+    for local in range(count):
+        for stream in streams:
+            stream.start(local)
+    pl.loop(0, count)(work)
+
+
+def stream_scratch(count, *shapes):
+    buffers = [pltpu.VMEM((count,) + shape, jnp.bfloat16) for shape in shapes]
+    return buffers + [pltpu.SemaphoreType.DMA((count,)) for _ in shapes]
 
 
 def begin_kernel(pairs, part, token_ref, *refs):
@@ -193,7 +185,7 @@
         for stream, out_ref in ((gate_w, gate_ref), (up_w, up_ref)):
             weight = stream.get(local)
             for block in blocks:
-                rows = rows_of(rows_refs, local, part, 0, block)
+                rows = rows_of(rows_refs, local, 0, part, block)
                 out_ref[local, span(block)] = jnp.dot(rows, weight, preferred_element_type=jnp.float32)
 
     over_experts(gate_ref.shape[0], (gate_w, up_w), work)
@@ -213,17 +205,17 @@
         in_specs=[VMEM_SPEC] * (pairs + 1) + [HBM_SPEC] * 2,
         out_specs=(VMEM_SPEC,) * 2,
         out_shape=(shape, shape),
-        scratch_shapes=stream_scratch((part, hidden), (part, hidden)),
+        scratch_shapes=stream_scratch(local_experts, (part, hidden), (part, hidden)),
         compiler_params=params(32 * MIB),
         cost_estimate=pl.CostEstimate(flops=LONG, bytes_accessed=0, transcendentals=0),
     )(token, *rows, w_gate, w_up)
 
 
-def middle_kernel(pairs, part, *refs):
+def middle_kernel(pairs, cut, part, *refs):
     rows_refs, weight_refs = refs[:pairs], refs[pairs : 2 * pairs]
     gate_sum, up_sum, gate_hbm, up_hbm, down_hbm, hidden_ref = refs[2 * pairs : 2 * pairs + 6]
     out_refs, scratch = refs[2 * pairs + 6 : 3 * pairs + 6], refs[3 * pairs + 6 :]
-    tail, full = slice(part, 2 * part), slice(None)
+    tail, full = slice(cut, gate_hbm.shape[1]), slice(None)
     gate_w = Stream(gate_hbm, scratch[0], scratch[3], tail, full)
     up_w = Stream(up_hbm, scratch[1], scratch[4], tail, full)
     down_w = Stream(down_hbm, scratch[2], scratch[5], full, slice(0, part))
@@ -231,7 +223,7 @@
     def work(local):
         gate_now, up_now, down_now = gate_w.get(local), up_w.get(local), None
         for block in row_blocks(pairs):
-            rows = rows_of(rows_refs, local, part, 1, block)
+            rows = rows_of(rows_refs, local, cut, gate_hbm.shape[1], block)
             weight = jnp.concatenate([weight_refs[p][local, :, :1] for p in block], axis=0)
             at = span(block)
             gate = gate_sum[local, at] + jnp.dot(rows, gate_now, preferred_element_type=jnp.float32)
@@ -251,17 +243,17 @@
         out_refs[p][local] = out[i * 2 * CAP : (i + 1) * 2 * CAP]
 
 
-def middle(rows, part, weights, gate_sum, up_sum, w_gate, w_up, w_down):
+def middle(rows, cut, part, weights, gate_sum, up_sum, w_gate, w_up, w_down):
     pairs = len(rows)
-    local_experts, _, hidden = w_gate.shape
+    local_experts, width, hidden = w_gate.shape
     count = pairs * 2 * CAP
     out_shapes = [jax.ShapeDtypeStruct((local_experts, 2 * CAP, part), jnp.bfloat16)] * pairs
     got = pl.pallas_call(
-        functools.partial(middle_kernel, pairs, part),
+        functools.partial(middle_kernel, pairs, cut, part),
         in_specs=[VMEM_SPEC] * (2 * pairs + 2) + [HBM_SPEC] * 3,
         out_specs=[VMEM_SPEC] * (pairs + 1),
         out_shape=[jax.ShapeDtypeStruct((local_experts, count, hidden), jnp.bfloat16)] + out_shapes,
-        scratch_shapes=stream_scratch((part, hidden), (part, hidden), (hidden, part)),
+        scratch_shapes=stream_scratch(local_experts, (width - cut, hidden), (width - cut, hidden), (hidden, part)),
         compiler_params=params(32 * MIB),
         cost_estimate=pl.CostEstimate(flops=0, bytes_accessed=0, transcendentals=0),
     )(*rows, *weights, gate_sum, up_sum, w_gate, w_up, w_down)
@@ -287,7 +279,7 @@
         in_specs=[VMEM_SPEC, HBM_SPEC],
         out_specs=[VMEM_SPEC] * pairs,
         out_shape=[jax.ShapeDtypeStruct((local_experts, 2 * CAP, part), jnp.bfloat16)] * pairs,
-        scratch_shapes=stream_scratch((depth, part)),
+        scratch_shapes=stream_scratch(local_experts, (depth, part)),
         compiler_params=params(46 * MIB),
         cost_estimate=pl.CostEstimate(flops=0, bytes_accessed=0, transcendentals=0),
     )(hidden, w_down)
@@ -366,6 +358,7 @@
     local_experts = w_gate.shape[0]
     index = lax.axis_index("exp")
     part = width // 2
+    cut = width * 3 // 8
 
     def place(pz, py, pc):
         return (pz % depth * lines + py) * CORES + pc
@@ -423,7 +416,7 @@
         token, line[2], others[3, 0], others[0, 1], others[1, 1] = fence(
             token, line[2], others[3, 0], others[0, 1], others[1, 1]
         )
-        head, tail = swap_line(line[2][:, : LANES + part]), swap_line(line[2][:, LANES + part :])
+        head, tail = swap_line(line[2][:, : LANES + cut]), swap_line(line[2][:, LANES + cut :])
         others[2, 0] = swap_core(line[2])
         for key, piece in (((3, 0), line[3]), ((0, 1), far[0]), ((1, 1), far[1])):
             take(key, piece, others[key])
@@ -444,12 +437,12 @@
                 take((r, 1), piece, swap_core(piece))
     keys = sorted(rows)
 
-    gate_sum, up_sum = begin(token, [rows[k] for k in keys], part, w_gate, w_up)
+    gate_sum, up_sum = begin(token, [rows[k] for k in keys], cut, w_gate, w_up)
     for key, half in late.items():
         half, gate_sum, up_sum = lax.optimization_barrier((half, gate_sum, up_sum))
         rows[key] = dispatch_more(codes[key], half, swap_core(half))
     hidden, out0 = middle(
-        [rows[k] for k in keys], part, [weights[k] for k in keys], gate_sum, up_sum, w_gate, w_up, w_down
+        [rows[k] for k in keys], cut, part, [weights[k] for k in keys], gate_sum, up_sum, w_gate, w_up, w_down
     )
     out0 = dict(zip(keys, out0))
 

time: 141 us -> 139 us (0.986)
    pallas_call x1, Pallas kernels: 9.2 us -> 7.49 us  [begin(): pl.pallas_call(functools.partial(begin_kernel, pairs, part), in_specs=[VM...]
    pallas_call x1, Pallas kernels: 11.1 us -> 12.7 us  [middle(): pl.pallas_call(functools.partial(middle_kernel, pairs, cut, part), in_spe...]
  transfers between devices with their start and end apart: 36 -> 36, of which waited for: 14 -> 15; matrix products, arithmetic and copies ran while one was open for 1% -> 1% of each run, Pallas kernels for 17% -> 15%
where the time goes in v6:
time: 139 us; the launch traced here: 138 us
  waiting for transfers between devices  71.8 us (52%)
  Pallas kernels  37.1 us (27%)
  starting transfers between devices  26.7 us (19%)
    ppermute x36, waiting for transfers between devices, send(): lax.ppermute(value, 'exp', [(place(*who), place(*move(*who))) for who in...  71.8 us
    ppermute x36, starting transfers between devices, send(): lax.ppermute(value, 'exp', [(place(*who), place(*move(*who))) for who in...  26.7 us
    pallas_call x1, Pallas kernels, middle(): pl.pallas_call(functools.partial(middle_kernel, pairs, cut, part), in_spe...  12.7 us
    pallas_call x1, Pallas kernels, begin(): pl.pallas_call(functools.partial(begin_kernel, pairs, part), in_specs=[VM...  7.49 us
    pallas_call x8, Pallas kernels, dispatch(): pl.pallas_call(functools.partial(dispatch_kernel, top), in_specs=[pl.Bloc...  5.01 us
    pallas_call x1, Pallas kernels, finish(): pl.pallas_call(functools.partial(finish_kernel, pairs, part), in_specs=[V...  4.56 us
    pallas_call x10, Pallas kernels, combine(): pl.pallas_call(combine_kernel, out_shape=(jax.ShapeDtypeStruct((tok, widt...  4.01 us
  transfers between devices with their start and end apart: 36, of which 15 were waited for; matrix products, arithmetic and copies ran while one was open for 1% of the time, Pallas kernels for 15%

profile of v6, /device:TPU:0, one launch (start us, length us, event | category | flops | bytes accessed | tf_op | source)
XLA Modules:
  0.0 138.5 jit_solution(2145620573614654033)
XLA Ops:
  0.0 1.9 %shard_map.65.x0_ref = bf16[128,2176]{1,0:T(8,128)(2,1)} custom-call(s32[8,128]{1,0:T(8,128)} %bitcast.3, f32[8,128]{1,0:T(8,128)} %bitcast.4, bf16[128,2048]{1,0:T(8,128)(2,1)} %tokens_ref.1), custom_call_target="tpu_custom_call" | custom-call | tf_op jit(solution)/shard_map/pallas_call | solution.py:46
  1.9 3.0 %collective-permute-start.3 = (bf16[128,2176]{1,0:T(8,128)(2,1)}, bf16[128,2176]{1,0:T(8,128)(2,1)}, u32[]{:S(2)}, u32[]{:S(2)}) collective-permute-start(bf16[128,2176]{1,0:T(8,128)(2,1)} %shard_map.65.x0_ref), channel_id=1, source_target_pairs={{0,2},{1,3},{2,0},{3,1},{4,6},{5,7},{6,4},{7,5},{8,10},{9,11},{10,... | collective-permute-start | bytes 1671176 | tf_op jit(solution)/shard_map/ppermute | solution.py:369
  4.9 3.6 %collective-permute-start = (bf16[128,2176]{1,0:T(8,128)(2,1)}, bf16[128,2176]{1,0:T(8,128)(2,1)S(1)}, u32[]{:S(2)}, u32[]{:S(2)}) collective-permute-start(bf16[128,2176]{1,0:T(8,128)(2,1)} %shard_map.65.x0_ref), channel_id=1, source_target_pairs={{0,12},{1,13},{2,14},{3,15},{4,0},{5,1},{6,2},{7,3},{8,4},{9,5},{1... | collective-permute-start | bytes 1671176 | tf_op jit(solution)/shard_map/ppermute | solution.py:369
  8.5 1.1 copy-done
  9.6 12.2 %collective-permute-done.x0_ref = bf16[128,2176]{1,0:T(8,128)(2,1)S(1)} collective-permute-done((bf16[128,2176]{1,0:T(8,128)(2,1)}, bf16[128,2176]{1,0:T(8,128)(2,1)S(1)}, u32[]{:S(2)}, u32[]{:S(2)}) %collective-permute-start) | collective-permute-done | bytes 557088 | tf_op jit(solution)/shard_map/ppermute | solution.py:369
  21.8 0.5 collective-permute-start.8
  22.3 4.2 %collective-permute-start.5 = (bf16[128,2176]{1,0:T(8,128)(2,1)S(1)}, bf16[128,2176]{1,0:T(8,128)(2,1)S(1)}, u32[]{:S(2)}, u32[]{:S(2)}) collective-permute-start(bf16[128,2176]{1,0:T(8,128)(2,1)S(1)} %collective-permute-done.x0_ref), channel_id=1, source_target_pairs={{0,12},{1,13},{2,14},{3,15},{4,0},{5,1},{6,2},{7,3},{8,4},{9,5},{1... | collective-permute-start | bytes 1671176 | tf_op jit(solution)/shard_map/ppermute | solution.py:369
  26.5 0.5 shard_map.68
  27.0 7.5 %collective-permute-done.2.x0_ref = bf16[128,2176]{1,0:T(8,128)(2,1)S(1)} collective-permute-done((bf16[128,2176]{1,0:T(8,128)(2,1)S(1)}, bf16[128,2176]{1,0:T(8,128)(2,1)S(1)}, u32[]{:S(2)}, u32[]{:S(2)}) %collective-permute-start.2) | collective-permute-done | bytes 557088 | tf_op jit(solution)/shard_map/ppermute | solution.py:369
  34.5 0.5 collective-permute-start.10
  35.1 0.5 collective-permute-start.7
  35.6 0.5 shard_map.70
  36.2 9.9 %collective-permute-done.5.x0_ref = bf16[128,2176]{1,0:T(8,128)(2,1)S(1)} collective-permute-done((bf16[128,2176]{1,0:T(8,128)(2,1)S(1)}, bf16[128,2176]{1,0:T(8,128)(2,1)S(1)}, u32[]{:S(2)}, u32[]{:S(2)}) %collective-permute-start.5) | collective-permute-done | bytes 557088 | tf_op jit(solution)/shard_map/ppermute | solution.py:369
  46.3 0.5 collective-permute-start.11
  46.8 0.5 shard_map.72
  47.3 1.6 %shard_map.73 = (bf16[4,48,2048]{2,1,0:T(8,128)(2,1)S(1)}, s32[2,4,128]{2,1,0:T(4,128)S(1)}, f32[4,48,128]{2,1,0:T(8,128)S(1)}) custom-call(s32[1]{0:T(128)} %bitcast.2.first_ref, bf16[128,2176]{1,0:T(8,128)(2,1)} %collective-permute-done.3.x0_ref, bf16[128,2176]{1,0:T(8,128)(2,1)S(1)} %collective-permute-done.7.x1_ref), custom_call_target="tpu_custom_call" | custom-call | tf_op jit(solution)/shard_map/pallas_call | solution.py:108
  48.9 0.5 shard_map.74
  49.4 4.8 %collective-permute-done.11.x0_ref = bf16[128,896]{1,0:T(8,128)(2,1)S(1)} collective-permute-done((bf16[128,896]{1,0:T(8,128)(2,1)S(1)}, bf16[128,896]{1,0:T(8,128)(2,1)S(1)}, u32[]{:S(2)}, u32[]{:S(2)}) %collective-permute-start.11) | collective-permute-done | bytes 229408 | tf_op jit(solution)/shard_map/ppermute | solution.py:369
  54.2 0.5 collective-permute-start.12
  54.8 0.6 collective-permute-start.14
  55.3 1.2 collective-permute-done.12.x1_ref
  56.9 0.5 shard_map.77
  57.4 0.5 shard_map.78
  58.0 7.5 %shard_map.79 = (f32[4,384,768]{2,1,0:T(8,128)S(1)}, f32[4,384,768]{2,1,0:T(8,128)S(1)}) custom-call(f32[8,128]{1,0:T(8,128)S(1)} %shard_map.75.token_ref.in_ref, bf16[4,48,2048]{2,1,0:T(8,128)(2,1)S(1)} %get-tuple-element.155.refs_0_, bf16[4,48,2048]{2,1,0:T(8,128)(2,1)S(1)} %get-tuple-element.156.refs_1_, ...), custom_call_target="tpu_custom_call" | custom-call | flops 40000000000 | tf_op jit(solution)/shard_map/pallas_call | solution.py:203
  65.7 1.5 %collective-permute-done.16.x1_ref = bf16[128,1280]{1,0:T(8,128)(2,1)S(1)} collective-permute-done((bf16[128,1280]{1,0:T(8,128)(2,1)S(1)}, bf16[128,1280]{1,0:T(8,128)(2,1)S(1)}, u32[]{:S(2)}, u32[]{:S(2)}) %collective-permute-start.16) | collective-permute-done | bytes 327712 | tf_op jit(solution)/shard_map/ppermute | solution.py:369
  67.5 12.7 %shard_map.81 = (bf16[4,384,768]{2,1,0:T(8,128)(2,1)S(1)}, bf16[4,48,1024]{2,1,0:T(8,128)(2,1)S(1)}, bf16[4,48,1024]{2,1,0:T(8,128)(2,1)S(1)}, bf16[4,48,1024]{2...) custom-call(bf16[4,48,2048]{2,1,0:T(8,128)(2,1)S(1)} %get-tuple-elem, ...), custom_call_target="tpu_custom_call" | custom-call | tf_op jit(solution)/shard_map/pallas_call | solution.py:251
  81.5 0.6 collective-permute-done.17
  82.2 0.6 collective-permute-start.18
  82.8 4.6 %shard_map.84 = (bf16[4,48,1024]{2,1,0:T(8,128)(2,1)S(1)}, bf16[4,48,1024]{2,1,0:T(8,128)(2,1)S(1)}, bf16[4,48,1024]{2,1,0:T(8,128)(2,1)S(1)}, bf16[4,48,1024]{2...) custom-call(bf16[4,384,768]{2,1,0:T(8,128)(2,1)S(1)} %get-tuple-elem, ...), custom_call_target="tpu_custom_call" | custom-call | tf_op jit(solution)/shard_map/pallas_call | solution.py:277
  88.1 0.6 collective-permute-start.28
  88.6 0.5 shard_map.88
  89.6 1.0 collective-permute-done.18
  91.2 0.8 collective-permute-start.21
  92.0 0.7 collective-permute-start.27
  92.8 1.6 %collective-permute-start.23 = (bf16[128,2048]{1,0:T(8,128)(2,1)S(1)}, bf16[128,2048]{1,0:T(8,128)(2,1)S(1)}, u32[]{:S(2)}, u32[]{:S(2)}) collective-permute-start(bf16[128,2048]{1,0:T(8,128)(2,1)S(1)} %add_convert_fusion.3), channel_id=1, source_target_pairs={{0,2},{1,3},{2,0},{3,1},{4,6},{5,7},{6,4},{7,5},{8,10},{9,11},{10,... | collective-permute-start | bytes 1572872 | tf_op jit(solution)/shard_map/ppermute | solution.py:369
  95.4 0.5 shard_map.95
  95.8 0.5 shard_map.96
  96.3 5.9 %collective-permute-done.21 = bf16[128,1024]{1,0:T(8,128)(2,1)S(1)} collective-permute-done((bf16[128,1024]{1,0:T(8,128)(2,1)S(1)}, bf16[128,1024]{1,0:T(8,128)(2,1)S(1)}, u32[]{:S(2)}, u32[]{:S(2)}) %collective-permute-start.21) | collective-permute-done | bytes 262176 | tf_op jit(solution)/shard_map/ppermute | solution.py:369
  102.4 3.9 %collective-permute-done.23 = bf16[128,2048]{1,0:T(8,128)(2,1)S(1)} collective-permute-done((bf16[128,2048]{1,0:T(8,128)(2,1)S(1)}, bf16[128,2048]{1,0:T(8,128)(2,1)S(1)}, u32[]{:S(2)}, u32[]{:S(2)}) %collective-permute-start.23) | collective-permute-done | bytes 524320 | tf_op jit(solution)/shard_map/ppermute | solution.py:369
  106.6 1.6 %collective-permute-start.25 = (bf16[128,2048]{1,0:T(8,128)(2,1)S(1)}, bf16[128,2048]{1,0:T(8,128)(2,1)S(1)}, u32[]{:S(2)}, u32[]{:S(2)}) collective-permute-start(bf16[128,2048]{1,0:T(8,128)(2,1)S(1)} %pad_maximum_fusion), channel_id=1, source_target_pairs={{0,2},{1,3},{2,0},{3,1},{4,6},{5,7},{6,4},{7,5},{8,10},{9,11},{10,... | collective-permute-start | bytes 1572872 | tf_op jit(solution)/shard_map/ppermute | solution.py:369
  108.6 0.6 collective-permute-start.31
  109.2 3.5 %collective-permute-done.29 = bf16[128,1024]{1,0:T(8,128)(2,1)S(1)} collective-permute-done((bf16[128,1024]{1,0:T(8,128)(2,1)S(1)}, bf16[128,1024]{1,0:T(8,128)(2,1)S(1)}, u32[]{:S(2)}, u32[]{:S(2)}) %collective-permute-start.29) | collective-permute-done | bytes 262176 | tf_op jit(solution)/shard_map/ppermute | solution.py:369
  112.7 1.5 %collective-permute-start.35 = (bf16[128,2048]{1,0:T(8,128)(2,1)S(1)}, bf16[128,2048]{1,0:T(8,128)(2,1)S(1)}, u32[]{:S(2)}, u32[]{:S(2)}) collective-permute-start(bf16[128,2048]{1,0:T(8,128)(2,1)S(1)} %add_convert_fusion), channel_id=1, source_target_pairs={{0,12},{1,13},{2,14},{3,15},{4,0},{5,1},{6,2},{7,3},{8,4},{9,5},{1... | collective-permute-start | bytes 1572872 | tf_op jit(solution)/shard_map/ppermute | solution.py:369
  114.2 7.1 %collective-permute-done.25 = bf16[128,2048]{1,0:T(8,128)(2,1)S(1)} collective-permute-done((bf16[128,2048]{1,0:T(8,128)(2,1)S(1)}, bf16[128,2048]{1,0:T(8,128)(2,1)S(1)}, u32[]{:S(2)}, u32[]{:S(2)}) %collective-permute-start.25) | collective-permute-done | bytes 524320 | tf_op jit(solution)/shard_map/ppermute | solution.py:369
  121.6 3.4 %collective-permute-start.33 = (bf16[128,2048]{1,0:T(8,128)(2,1)S(1)}, bf16[128,2048]{1,0:T(8,128)(2,1)S(1)}, u32[]{:S(2)}, u32[]{:S(2)}) collective-permute-start(bf16[128,2048]{1,0:T(8,128)(2,1)S(1)} %add_convert_fusion.1), channel_id=1, source_target_pairs={{0,4},{1,5},{2,6},{3,7},{4,8},{5,9},{6,10},{7,11},{8,12},{9,13},{1... | collective-permute-start | bytes 1572872 | tf_op jit(solution)/shard_map/ppermute | solution.py:369
  125.2 7.0 %collective-permute-done.31.refs_0_ = bf16[128,2048]{1,0:T(8,128)(2,1)S(1)} collective-permute-done((bf16[128,2048]{1,0:T(8,128)(2,1)S(1)}, bf16[128,2048]{1,0:T(8,128)(2,1)S(1)}, u32[]{:S(2)}, u32[]{:S(2)}) %collective-permute-start.31) | collective-permute-done | bytes 524320 | tf_op jit(solution)/shard_map/ppermute | solution.py:369
  132.2 5.2 %collective-permute-done.35.refs_2_ = bf16[128,2048]{1,0:T(8,128)(2,1)S(1)} collective-permute-done((bf16[128,2048]{1,0:T(8,128)(2,1)S(1)}, bf16[128,2048]{1,0:T(8,128)(2,1)S(1)}, u32[]{:S(2)}, u32[]{:S(2)}) %collective-permute-start.35) | collective-permute-done | bytes 524320 | tf_op jit(solution)/shard_map/ppermute | solution.py:369
  137.4 1.1 shard_map.98
  (77 shorter events, 6.8 us)
Async XLA Ops:
  1.9 32.6 %collective-permute-start.3 = (bf16[128,2176]{1,0:T(8,128)(2,1)}, bf16[128,2176]{1,0:T(8,128)(2,1)}, u32[]{:S(2)}, u32[]{:S(2)}) collective-permute-start(bf16[128,2176]{1,0:T(8,128)(2,1)} %shard_map.65.x0_ref), channel_id=1, source_target_pairs={{0,2},{1,3},{2,0},{3,1},{4,6},{5,7},{6,4},{7,5},{8,10},{9,11},{10,... | collective-permute-start | bytes 1671176 | tf_op jit(solution)/shard_map/ppermute | solution.py:369
  4.9 4.7 %collective-permute-start.1 = (bf16[128,2176]{1,0:T(8,128)(2,1)}, bf16[128,2176]{1,0:T(8,128)(2,1)S(1)}, u32[]{:S(2)}, u32[]{:S(2)}) collective-permute-start(bf16[128,2176]{1,0:T(8,128)(2,1)} %shard_map.65.x0_ref), channel_id=1, source_target_pairs={{0,1},{1,0},{2,3},{3,2},{4,5},{5,4},{6,7},{7,6},{8,9},{9,8},{10,11... | collective-permute-start | bytes 1671176 | tf_op jit(solution)/shard_map/ppermute | solution.py:369
  4.9 16.9 %collective-permute-start = (bf16[128,2176]{1,0:T(8,128)(2,1)}, bf16[128,2176]{1,0:T(8,128)(2,1)S(1)}, u32[]{:S(2)}, u32[]{:S(2)}) collective-permute-start(bf16[128,2176]{1,0:T(8,128)(2,1)} %shard_map.65.x0_ref), channel_id=1, source_target_pairs={{0,12},{1,13},{2,14},{3,15},{4,0},{5,1},{6,2},{7,3},{8,4},{9,5},{1... | collective-permute-start | bytes 1671176 | tf_op jit(solution)/shard_map/ppermute | solution.py:369
  8.5 1.1 copy-start
  9.6 24.9 %collective-permute-start.2 = (bf16[128,2176]{1,0:T(8,128)(2,1)S(1)}, bf16[128,2176]{1,0:T(8,128)(2,1)S(1)}, u32[]{:S(2)}, u32[]{:S(2)}) collective-permute-start(bf16[128,2176]{1,0:T(8,128)(2,1)S(1)} %copy-done), channel_id=1, source_target_pairs={{0,4},{1,5},{2,6},{3,7},{4,8},{5,9},{6,10},{7,11},{8,12},{9,13},{1... | collective-permute-start | bytes 1671176 | tf_op jit(solution)/shard_map/ppermute | solution.py:369
  21.8 14.3 %collective-permute-start.8 = (bf16[128,2176]{1,0:T(8,128)(2,1)S(1)}, bf16[128,2176]{1,0:T(8,128)(2,1)S(1)}, u32[]{:S(2)}, u32[]{:S(2)}) collective-permute-start(bf16[128,2176]{1,0:T(8,128)(2,1)S(1)} %collective-permute-done.x0_ref), channel_id=1, source_target_pairs={{0,2},{1,3},{2,0},{3,1},{4,6},{5,7},{6,4},{7,5},{8,10},{9,11},{10,... | collective-permute-start | bytes 1671176 | tf_op jit(solution)/shard_map/ppermute | solution.py:369
  22.3 12.2 %collective-permute-start.4 = (bf16[128,2176]{1,0:T(8,128)(2,1)S(1)}, bf16[128,2176]{1,0:T(8,128)(2,1)S(1)}, u32[]{:S(2)}, u32[]{:S(2)}) collective-permute-start(bf16[128,2176]{1,0:T(8,128)(2,1)S(1)} %collective-permute-done.x0_ref), channel_id=1, source_target_pairs={{0,1},{1,0},{2,3},{3,2},{4,5},{5,4},{6,7},{7,6},{8,9},{9,8},{10,11... | collective-permute-start | bytes 1671176 | tf_op jit(solution)/shard_map/ppermute | solution.py:369
  22.3 23.8 %collective-permute-start.5 = (bf16[128,2176]{1,0:T(8,128)(2,1)S(1)}, bf16[128,2176]{1,0:T(8,128)(2,1)S(1)}, u32[]{:S(2)}, u32[]{:S(2)}) collective-permute-start(bf16[128,2176]{1,0:T(8,128)(2,1)S(1)} %collective-permute-done.x0_ref), channel_id=1, source_target_pairs={{0,12},{1,13},{2,14},{3,15},{4,0},{5,1},{6,2},{7,3},{8,4},{9,5},{1... | collective-permute-start | bytes 1671176 | tf_op jit(solution)/shard_map/ppermute | solution.py:369
  34.5 14.8 %collective-permute-start.10 = (bf16[128,2176]{1,0:T(8,128)(2,1)S(1)}, bf16[128,2176]{1,0:T(8,128)(2,1)S(1)}, u32[]{:S(2)}, u32[]{:S(2)}) collective-permute-start(bf16[128,2176]{1,0:T(8,128)(2,1)S(1)} %collective-permute-done.2.x0_ref), channel_id=1, source_target_pairs={{0,2},{1,3},{2,0},{3,1},{4,6},{5,7},{6,4},{7,5},{8,10},{9,11},{10,... | collective-permute-start | bytes 1671176 | tf_op jit(solution)/shard_map/ppermute | solution.py:369
  35.1 11.0 %collective-permute-start.6 = (bf16[128,2176]{1,0:T(8,128)(2,1)S(1)}, bf16[128,2176]{1,0:T(8,128)(2,1)S(1)}, u32[]{:S(2)}, u32[]{:S(2)}) collective-permute-start(bf16[128,2176]{1,0:T(8,128)(2,1)S(1)} %collective-permute-done.2.x0_ref), channel_id=1, source_target_pairs={{0,1},{1,0},{2,3},{3,2},{4,5},{5,4},{6,7},{7,6},{8,9},{9,8},{10,11... | collective-permute-start | bytes 1671176 | tf_op jit(solution)/shard_map/ppermute | solution.py:369
  35.1 11.0 %collective-permute-start.7 = (bf16[128,2176]{1,0:T(8,128)(2,1)}, bf16[128,2176]{1,0:T(8,128)(2,1)S(1)}, u32[]{:S(2)}, u32[]{:S(2)}) collective-permute-start(bf16[128,2176]{1,0:T(8,128)(2,1)} %collective-permute-done.3.x0_ref), channel_id=1, source_target_pairs={{0,1},{1,0},{2,3},{3,2},{4,5},{5,4},{6,7},{7,6},{8,9},{9,8},{10,11... | collective-permute-start | bytes 1671176 | tf_op jit(solution)/shard_map/ppermute | solution.py:369
  36.1 10.0 %collective-permute-start.9 = (bf16[128,2176]{1,0:T(8,128)(2,1)S(1)}, bf16[128,2176]{1,0:T(8,128)(2,1)S(1)}, u32[]{:S(2)}, u32[]{:S(2)}) collective-permute-start(bf16[128,2176]{1,0:T(8,128)(2,1)S(1)} %collective-permute-done.8.x0_ref), channel_id=1, source_target_pairs={{0,1},{1,0},{2,3},{3,2},{4,5},{5,4},{6,7},{7,6},{8,9},{9,8},{10,11... | collective-permute-start | bytes 1671176 | tf_op jit(solution)/shard_map/ppermute | solution.py:369
  46.1 10.8 %collective-permute-start.13 = (bf16[128,2176]{1,0:T(8,128)(2,1)S(1)}, bf16[128,2176]{1,0:T(8,128)(2,1)S(1)}, u32[]{:S(2)}, u32[]{:S(2)}) collective-permute-start(bf16[128,2176]{1,0:T(8,128)(2,1)S(1)} %collective-permute-done.5.x0_ref), channel_id=1, source_target_pairs={{0,1},{1,0},{2,3},{3,2},{4,5},{5,4},{6,7},{7,6},{8,9},{9,8},{10,11... | collective-permute-start | bytes 1671176 | tf_op jit(solution)/shard_map/ppermute | solution.py:369
  46.3 8.0 %collective-permute-start.11 = (bf16[128,896]{1,0:T(8,128)(2,1)S(1)}, bf16[128,896]{1,0:T(8,128)(2,1)S(1)}, u32[]{:S(2)}, u32[]{:S(2)}) collective-permute-start(bf16[128,896]{1,0:T(8,128)(2,1)S(1)} %slice.13), channel_id=1, source_target_pairs={{0,2},{1,3},{2,0},{3,1},{4,6},{5,7},{6,4},{7,5},{8,10},{9,11},{10,... | collective-permute-start | bytes 688136 | tf_op jit(solution)/shard_map/ppermute | solution.py:369
  54.2 3.2 %collective-permute-start.15 = (bf16[128,2176]{1,0:T(8,128)(2,1)S(1)}, bf16[128,2176]{1,0:T(8,128)(2,1)S(1)}, u32[]{:S(2)}, u32[]{:S(2)}) collective-permute-start(bf16[128,2176]{1,0:T(8,128)(2,1)S(1)} %collective-permute-done.10.x0_ref), channel_id=1, source_target_pairs={{0,1},{1,0},{2,3},{3,2},{4,5},{5,4},{6,7},{7,6},{8,9},{9,8},{10,11... | collective-permute-start | bytes 1671176 | tf_op jit(solution)/shard_map/ppermute | solution.py:369
  54.2 2.3 %collective-permute-start.12 = (bf16[128,896]{1,0:T(8,128)(2,1)S(1)}, bf16[128,896]{1,0:T(8,128)(2,1)S(1)}, u32[]{:S(2)}, u32[]{:S(2)}) collective-permute-start(bf16[128,896]{1,0:T(8,128)(2,1)S(1)} %collective-permute-done.11.x0_ref), channel_id=1, source_target_pairs={{0,1},{1,0},{2,3},{3,2},{4,5},{5,4},{6,7},{7,6},{8,9},{9,8},{10,11... | collective-permute-start | bytes 688136 | tf_op jit(solution)/shard_map/ppermute | solution.py:369
  54.8 10.7 %collective-permute-start.14 = (bf16[128,1280]{1,0:T(8,128)(2,1)S(1)}, bf16[128,1280]{1,0:T(8,128)(2,1)S(1)}, u32[]{:S(2)}, u32[]{:S(2)}) collective-permute-start(bf16[128,1280]{1,0:T(8,128)(2,1)S(1)} %slice.14), channel_id=1, source_target_pairs={{0,2},{1,3},{2,0},{3,1},{4,6},{5,7},{6,4},{7,5},{8,10},{9,11},{10,... | collective-permute-start | bytes 983048 | tf_op jit(solution)/shard_map/ppermute | solution.py:369
  65.5 1.7 %collective-permute-start.16 = (bf16[128,1280]{1,0:T(8,128)(2,1)S(1)}, bf16[128,1280]{1,0:T(8,128)(2,1)S(1)}, u32[]{:S(2)}, u32[]{:S(2)}) collective-permute-start(bf16[128,1280]{1,0:T(8,128)(2,1)S(1)} %collective-permute-done.14.x0_ref), channel_id=1, source_target_pairs={{0,1},{1,0},{2,3},{3,2},{4,5},{5,4},{6,7},{7,6},{8,9},{9,8},{10,11... | collective-permute-start | bytes 983048 | tf_op jit(solution)/shard_map/ppermute | solution.py:369
  80.5 1.6 %collective-permute-start.17 = (bf16[128,1024]{1,0:T(8,128)(2,1)S(1)}, bf16[128,1024]{1,0:T(8,128)(2,1)S(1)}, u32[]{:S(2)}, u32[]{:S(2)}) collective-permute-start(bf16[128,1024]{1,0:T(8,128)(2,1)S(1)} %get-tuple-element.179), channel_id=1, source_target_pairs={{0,1},{1,0},{2,3},{3,2},{4,5},{5,4},{6,7},{7,6},{8,9},{9,8},{10,11... | collective-permute-start | bytes 786440 | tf_op jit(solution)/shard_map/ppermute | solution.py:369
  81.0 10.9 %collective-permute-start.26 = (bf16[128,1024]{1,0:T(8,128)(2,1)S(1)}, bf16[128,1024]{1,0:T(8,128)(2,1)S(1)}, u32[]{:S(2)}, u32[]{:S(2)}) collective-permute-start(bf16[128,1024]{1,0:T(8,128)(2,1)S(1)} %get-tuple-element.219), channel_id=1, source_target_pairs={{0,1},{1,0},{2,3},{3,2},{4,5},{5,4},{6,7},{7,6},{8,9},{9,8},{10,11... | collective-permute-start | bytes 786440 | tf_op jit(solution)/shard_map/ppermute | solution.py:369
  82.2 8.4 %collective-permute-start.18 = (bf16[128,1024]{1,0:T(8,128)(2,1)S(1)}, bf16[128,1024]{1,0:T(8,128)(2,1)S(1)}, u32[]{:S(2)}, u32[]{:S(2)}) collective-permute-start(bf16[128,1024]{1,0:T(8,128)(2,1)S(1)} %add_convert_fusion.7), channel_id=1, source_target_pairs={{0,2},{1,3},{2,0},{3,1},{4,6},{5,7},{6,4},{7,5},{8,10},{9,11},{10,... | collective-permute-start | bytes 786440 | tf_op jit(solution)/shard_map/ppermute | solution.py:369
  87.7 3.0 %collective-permute-start.19 = (bf16[128,1024]{1,0:T(8,128)(2,1)S(1)}, bf16[128,1024]{1,0:T(8,128)(2,1)S(1)}, u32[]{:S(2)}, u32[]{:S(2)}) collective-permute-start(bf16[128,1024]{1,0:T(8,128)(2,1)S(1)} %get-tuple-element.191), channel_id=1, source_target_pairs={{0,1},{1,0},{2,3},{3,2},{4,5},{5,4},{6,7},{7,6},{8,9},{9,8},{10,11... | collective-permute-start | bytes 786440 | tf_op jit(solution)/shard_map/ppermute | solution.py:369
  88.1 4.6 %collective-permute-start.28 = (bf16[128,1024]{1,0:T(8,128)(2,1)S(1)}, bf16[128,1024]{1,0:T(8,128)(2,1)S(1)}, u32[]{:S(2)}, u32[]{:S(2)}) collective-permute-start(bf16[128,1024]{1,0:T(8,128)(2,1)S(1)} %get-tuple-element.223), channel_id=1, source_target_pairs={{0,1},{1,0},{2,3},{3,2},{4,5},{5,4},{6,7},{7,6},{8,9},{9,8},{10,11... | collective-permute-start | bytes 786440 | tf_op jit(solution)/shard_map/ppermute | solution.py:369
  89.1 2.0 %collective-permute-start.20 = (bf16[128,2048]{1,0:T(8,128)(2,1)S(1)}, bf16[128,2048]{1,0:T(8,128)(2,1)S(1)}, u32[]{:S(2)}, u32[]{:S(2)}) collective-permute-start(bf16[128,2048]{1,0:T(8,128)(2,1)S(1)} %get-tuple-element.196), channel_id=1, source_target_pairs={{0,1},{1,0},{2,3},{3,2},{4,5},{5,4},{6,7},{7,6},{8,9},{9,8},{10,11... | collective-permute-start | bytes 1572872 | tf_op jit(solution)/shard_map/ppermute | solution.py:369
  90.6 17.5 %collective-permute-start.34 = (bf16[128,2048]{1,0:T(8,128)(2,1)S(1)}, bf16[128,2048]{1,0:T(8,128)(2,1)S(1)}, u32[]{:S(2)}, u32[]{:S(2)}) collective-permute-start(bf16[128,2048]{1,0:T(8,128)(2,1)S(1)} %get-tuple-element.243), channel_id=1, source_target_pairs={{0,1},{1,0},{2,3},{3,2},{4,5},{5,4},{6,7},{7,6},{8,9},{9,8},{10,11... | collective-permute-start | bytes 1572872 | tf_op jit(solution)/shard_map/ppermute | solution.py:369
  91.2 11.0 %collective-permute-start.21 = (bf16[128,1024]{1,0:T(8,128)(2,1)S(1)}, bf16[128,1024]{1,0:T(8,128)(2,1)S(1)}, u32[]{:S(2)}, u32[]{:S(2)}) collective-permute-start(bf16[128,1024]{1,0:T(8,128)(2,1)S(1)} %add_convert_fusion.6), channel_id=1, source_target_pairs={{0,4},{1,5},{2,6},{3,7},{4,8},{5,9},{6,10},{7,11},{8,12},{9,13},{1... | collective-permute-start | bytes 786440 | tf_op jit(solution)/shard_map/ppermute | solution.py:369
  92.0 16.5 %collective-permute-start.27 = (bf16[128,1024]{1,0:T(8,128)(2,1)S(1)}, bf16[128,1024]{1,0:T(8,128)(2,1)S(1)}, u32[]{:S(2)}, u32[]{:S(2)}) collective-permute-start(bf16[128,1024]{1,0:T(8,128)(2,1)S(1)} %add_convert_fusion.5), channel_id=1, source_target_pairs={{0,4},{1,5},{2,6},{3,7},{4,8},{5,9},{6,10},{7,11},{8,12},{9,13},{1... | collective-permute-start | bytes 786440 | tf_op jit(solution)/shard_map/ppermute | solution.py:369
  92.8 13.5 %collective-permute-start.23 = (bf16[128,2048]{1,0:T(8,128)(2,1)S(1)}, bf16[128,2048]{1,0:T(8,128)(2,1)S(1)}, u32[]{:S(2)}, u32[]{:S(2)}) collective-permute-start(bf16[128,2048]{1,0:T(8,128)(2,1)S(1)} %add_convert_fusion.3), channel_id=1, source_target_pairs={{0,2},{1,3},{2,0},{3,1},{4,6},{5,7},{6,4},{7,5},{8,10},{9,11},{10,... | collective-permute-start | bytes 1572872 | tf_op jit(solution)/shard_map/ppermute | solution.py:369
  94.8 7.4 %collective-permute-start.22 = (bf16[128,2048]{1,0:T(8,128)(2,1)S(1)}, bf16[128,2048]{1,0:T(8,128)(2,1)S(1)}, u32[]{:S(2)}, u32[]{:S(2)}) collective-permute-start(bf16[128,2048]{1,0:T(8,128)(2,1)S(1)} %get-tuple-element.207), channel_id=1, source_target_pairs={{0,1},{1,0},{2,3},{3,2},{4,5},{5,4},{6,7},{7,6},{8,9},{9,8},{10,11... | collective-permute-start | bytes 1572872 | tf_op jit(solution)/shard_map/ppermute | solution.py:369
  102.2 4.1 %collective-permute-start.24 = (bf16[128,2048]{1,0:T(8,128)(2,1)S(1)}, bf16[128,2048]{1,0:T(8,128)(2,1)S(1)}, u32[]{:S(2)}, u32[]{:S(2)}) collective-permute-start(bf16[128,2048]{1,0:T(8,128)(2,1)S(1)} %get-tuple-element.214), channel_id=1, source_target_pairs={{0,1},{1,0},{2,3},{3,2},{4,5},{5,4},{6,7},{7,6},{8,9},{9,8},{10,11... | collective-permute-start | bytes 1572872 | tf_op jit(solution)/shard_map/ppermute | solution.py:369
  102.2 10.5 %collective-permute-start.29 = (bf16[128,1024]{1,0:T(8,128)(2,1)S(1)}, bf16[128,1024]{1,0:T(8,128)(2,1)S(1)}, u32[]{:S(2)}, u32[]{:S(2)}) collective-permute-start(bf16[128,1024]{1,0:T(8,128)(2,1)S(1)} %add_convert_fusion.4), channel_id=1, source_target_pairs={{0,4},{1,5},{2,6},{3,7},{4,8},{5,9},{6,10},{7,11},{8,12},{9,13},{1... | collective-permute-start | bytes 786440 | tf_op jit(solution)/shard_map/ppermute | solution.py:369
  106.3 15.1 %collective-permute-start.32 = (bf16[128,2048]{1,0:T(8,128)(2,1)S(1)}, bf16[128,2048]{1,0:T(8,128)(2,1)S(1)}, u32[]{:S(2)}, u32[]{:S(2)}) collective-permute-start(bf16[128,2048]{1,0:T(8,128)(2,1)S(1)} %get-tuple-element.235), channel_id=1, source_target_pairs={{0,1},{1,0},{2,3},{3,2},{4,5},{5,4},{6,7},{7,6},{8,9},{9,8},{10,11... | collective-permute-start | bytes 1572872 | tf_op jit(solution)/shard_map/ppermute | solution.py:369
  106.6 14.8 %collective-permute-start.25 = (bf16[128,2048]{1,0:T(8,128)(2,1)S(1)}, bf16[128,2048]{1,0:T(8,128)(2,1)S(1)}, u32[]{:S(2)}, u32[]{:S(2)}) collective-permute-start(bf16[128,2048]{1,0:T(8,128)(2,1)S(1)} %pad_maximum_fusion), channel_id=1, source_target_pairs={{0,2},{1,3},{2,0},{3,1},{4,6},{5,7},{6,4},{7,5},{8,10},{9,11},{10,... | collective-permute-start | bytes 1572872 | tf_op jit(solution)/shard_map/ppermute | solution.py:369
  108.1 16.9 %collective-permute-start.30 = (bf16[128,2048]{1,0:T(8,128)(2,1)S(1)}, bf16[128,2048]{1,0:T(8,128)(2,1)S(1)}, u32[]{:S(2)}, u32[]{:S(2)}) collective-permute-start(bf16[128,2048]{1,0:T(8,128)(2,1)S(1)} %get-tuple-element.229), channel_id=1, source_target_pairs={{0,1},{1,0},{2,3},{3,2},{4,5},{5,4},{6,7},{7,6},{8,9},{9,8},{10,11... | collective-permute-start | bytes 1572872 | tf_op jit(solution)/shard_map/ppermute | solution.py:369
  108.6 23.6 %collective-permute-start.31 = (bf16[128,2048]{1,0:T(8,128)(2,1)S(1)}, bf16[128,2048]{1,0:T(8,128)(2,1)S(1)}, u32[]{:S(2)}, u32[]{:S(2)}) collective-permute-start(bf16[128,2048]{1,0:T(8,128)(2,1)S(1)} %add_convert_fusion.2), channel_id=1, source_target_pairs={{0,2},{1,3},{2,0},{3,1},{4,6},{5,7},{6,4},{7,5},{8,10},{9,11},{10,... | collective-permute-start | bytes 1572872 | tf_op jit(solution)/shard_map/ppermute | solution.py:369
  112.7 24.7 %collective-permute-start.35 = (bf16[128,2048]{1,0:T(8,128)(2,1)S(1)}, bf16[128,2048]{1,0:T(8,128)(2,1)S(1)}, u32[]{:S(2)}, u32[]{:S(2)}) collective-permute-start(bf16[128,2048]{1,0:T(8,128)(2,1)S(1)} %add_convert_fusion), channel_id=1, source_target_pairs={{0,12},{1,13},{2,14},{3,15},{4,0},{5,1},{6,2},{7,3},{8,4},{9,5},{1... | collective-permute-start | bytes 1572872 | tf_op jit(solution)/shard_map/ppermute | solution.py:369
  121.6 15.8 %collective-permute-start.33 = (bf16[128,2048]{1,0:T(8,128)(2,1)S(1)}, bf16[128,2048]{1,0:T(8,128)(2,1)S(1)}, u32[]{:S(2)}, u32[]{:S(2)}) collective-permute-start(bf16[128,2048]{1,0:T(8,128)(2,1)S(1)} %add_convert_fusion.1), channel_id=1, source_target_pairs={{0,4},{1,5},{2,6},{3,7},{4,8},{5,9},{6,10},{7,11},{8,12},{9,13},{1... | collective-permute-start | bytes 1572872 | tf_op jit(solution)/shard_map/ppermute | solution.py:369

commit v7 on v6

--- a/solution.py
+++ b/solution.py
@@ -147,7 +147,8 @@
 
 
 class Stream:
-    def __init__(self, hbm, buffer, sems, rows, columns):
+    def __init__(self, hbm, buffer, sems, rows, columns, given=None):
+        self.given = given
         self.hbm, self.buffer, self.sems, self.where = hbm, buffer, sems, (rows, columns)
 
     def copy(self, local):
@@ -157,15 +158,25 @@
         self.copy(local).start()
 
     def get(self, local):
+        if self.given and isinstance(local, int):
+            return self.given[0][...]
         self.copy(local).wait()
         return self.buffer[local]
 
 
-def over_experts(count, streams, work):
+def over_experts(count, streams, work, others=()):
     for local in range(count):
         for stream in streams:
-            stream.start(local)
-    pl.loop(0, count)(work)
+            if local or not stream.given:
+                stream.start(local)
+    for copy in others:
+        copy.start()
+    if any(stream.given for stream in streams):
+        work(0)
+        if count > 1:
+            pl.loop(1, count)(work)
+    else:
+        pl.loop(0, count)(work)
 
 
 def stream_scratch(count, *shapes):
@@ -175,7 +186,8 @@
 
 def begin_kernel(pairs, part, token_ref, *refs):
     rows_refs = refs[:pairs]
-    gate_hbm, up_hbm, gate_ref, up_ref, gate_buf, up_buf, gate_sem, up_sem = refs[pairs:]
+    gate_hbm, up_hbm, gate_ref, up_ref, *ahead = refs[pairs : pairs + 6]
+    gate_buf, up_buf, gate_sem, up_sem, ahead_sem = refs[pairs + 6 :]
     head, full = slice(0, part), slice(None)
     gate_w = Stream(gate_hbm, gate_buf, gate_sem, head, full)
     up_w = Stream(up_hbm, up_buf, up_sem, head, full)
@@ -188,7 +200,13 @@
                 rows = rows_of(rows_refs, local, 0, part, block)
                 out_ref[local, span(block)] = jnp.dot(rows, weight, preferred_element_type=jnp.float32)
 
-    over_experts(gate_ref.shape[0], (gate_w, up_w), work)
+    copies = [
+        pltpu.make_async_copy(hbm.at[0, slice(part, hbm.shape[1]), :], out, ahead_sem.at[i])
+        for i, (hbm, out) in enumerate(zip((gate_hbm, up_hbm), ahead))
+    ]
+    over_experts(gate_ref.shape[0], (gate_w, up_w), work, copies)
+    for copy in copies:
+        copy.wait()
 
 
 VMEM_SPEC = pl.BlockSpec(memory_space=pltpu.VMEM)
@@ -197,27 +215,28 @@
 
 def begin(token, rows, part, w_gate, w_up):
     pairs = len(rows)
-    local_experts, _, hidden = w_gate.shape
+    local_experts, width, hidden = w_gate.shape
     count = pairs * 2 * CAP
     shape = jax.ShapeDtypeStruct((local_experts, count, hidden), jnp.float32)
+    ahead = jax.ShapeDtypeStruct((width - part, hidden), jnp.bfloat16)
     return pl.pallas_call(
         functools.partial(begin_kernel, pairs, part),
         in_specs=[VMEM_SPEC] * (pairs + 1) + [HBM_SPEC] * 2,
-        out_specs=(VMEM_SPEC,) * 2,
-        out_shape=(shape, shape),
-        scratch_shapes=stream_scratch(local_experts, (part, hidden), (part, hidden)),
-        compiler_params=params(32 * MIB),
+        out_specs=(VMEM_SPEC,) * 4,
+        out_shape=(shape, shape, ahead, ahead),
+        scratch_shapes=stream_scratch(local_experts, (part, hidden), (part, hidden)) + [pltpu.SemaphoreType.DMA((2,))],
+        compiler_params=params(28 * MIB),
         cost_estimate=pl.CostEstimate(flops=LONG, bytes_accessed=0, transcendentals=0),
     )(token, *rows, w_gate, w_up)
 
 
 def middle_kernel(pairs, cut, part, *refs):
     rows_refs, weight_refs = refs[:pairs], refs[pairs : 2 * pairs]
-    gate_sum, up_sum, gate_hbm, up_hbm, down_hbm, hidden_ref = refs[2 * pairs : 2 * pairs + 6]
-    out_refs, scratch = refs[2 * pairs + 6 : 3 * pairs + 6], refs[3 * pairs + 6 :]
+    gate_sum, up_sum, gate_first, up_first, gate_hbm, up_hbm, down_hbm, hidden_ref = refs[2 * pairs : 2 * pairs + 8]
+    out_refs, scratch = refs[2 * pairs + 8 : 3 * pairs + 8], refs[3 * pairs + 8 :]
     tail, full = slice(cut, gate_hbm.shape[1]), slice(None)
-    gate_w = Stream(gate_hbm, scratch[0], scratch[3], tail, full)
-    up_w = Stream(up_hbm, scratch[1], scratch[4], tail, full)
+    gate_w = Stream(gate_hbm, scratch[0], scratch[3], tail, full, [gate_first])
+    up_w = Stream(up_hbm, scratch[1], scratch[4], tail, full, [up_first])
     down_w = Stream(down_hbm, scratch[2], scratch[5], full, slice(0, part))
 
     def work(local):
@@ -243,20 +262,20 @@
         out_refs[p][local] = out[i * 2 * CAP : (i + 1) * 2 * CAP]
 
 
-def middle(rows, cut, part, weights, gate_sum, up_sum, w_gate, w_up, w_down):
+def middle(rows, cut, part, weights, sums, w_gate, w_up, w_down):
     pairs = len(rows)
     local_experts, width, hidden = w_gate.shape
     count = pairs * 2 * CAP
     out_shapes = [jax.ShapeDtypeStruct((local_experts, 2 * CAP, part), jnp.bfloat16)] * pairs
     got = pl.pallas_call(
         functools.partial(middle_kernel, pairs, cut, part),
-        in_specs=[VMEM_SPEC] * (2 * pairs + 2) + [HBM_SPEC] * 3,
+        in_specs=[VMEM_SPEC] * (2 * pairs + 4) + [HBM_SPEC] * 3,
         out_specs=[VMEM_SPEC] * (pairs + 1),
         out_shape=[jax.ShapeDtypeStruct((local_experts, count, hidden), jnp.bfloat16)] + out_shapes,
         scratch_shapes=stream_scratch(local_experts, (width - cut, hidden), (width - cut, hidden), (hidden, part)),
-        compiler_params=params(32 * MIB),
-        cost_estimate=pl.CostEstimate(flops=0, bytes_accessed=0, transcendentals=0),
-    )(*rows, *weights, gate_sum, up_sum, w_gate, w_up, w_down)
+        compiler_params=params(28 * MIB),
+        cost_estimate=pl.CostEstimate(flops=0, bytes_accessed=0, transcendentals=0),
+    )(*rows, *weights, *sums, w_gate, w_up, w_down)
     return got[0], got[1:]
 
 
@@ -397,11 +416,10 @@
             late[key] = halves[1]
 
     if lines > 1 and depth == 4:
-        line[1], far = to_below(line[0]), {0: swap_line(line[0])}
-        others = {(0, 0): swap_core(line[0])}
+        line[1], others = to_below(line[0]), {(0, 0): swap_core(line[0])}
         token, line[0] = fence(jnp.zeros((8, LANES), jnp.float32), line[0])
-        line[3] = to_above(line[0])
-        token, line[1], others[0, 0] = fence(token, line[1], others[0, 0])
+        far, line[3] = {0: swap_line(line[0])}, to_above(line[0])
+        token, line[1], others[0, 0] = tie(token, line[1], others[0, 0])
         far[1], others[1, 0] = swap_line(line[1]), swap_core(line[1])
         token, line[1] = fence(token, line[1])
         line[2] = to_below(line[1])
@@ -437,12 +455,12 @@
                 take((r, 1), piece, swap_core(piece))
     keys = sorted(rows)
 
-    gate_sum, up_sum = begin(token, [rows[k] for k in keys], cut, w_gate, w_up)
+    sums = begin(token, [rows[k] for k in keys], cut, w_gate, w_up)
     for key, half in late.items():
-        half, gate_sum, up_sum = lax.optimization_barrier((half, gate_sum, up_sum))
+        half, *sums = lax.optimization_barrier((half, *sums))
         rows[key] = dispatch_more(codes[key], half, swap_core(half))
     hidden, out0 = middle(
-        [rows[k] for k in keys], cut, part, [weights[k] for k in keys], gate_sum, up_sum, w_gate, w_up, w_down
+        [rows[k] for k in keys], cut, part, [weights[k] for k in keys], sums, w_gate, w_up, w_down
     )
     out0 = dict(zip(keys, out0))
 

time: 139 us -> 138 us (level)
  starting transfers between devices: 26.7 us -> 32.3 us
  waiting for transfers between devices: 71.8 us -> 66.7 us
  Pallas kernels: 37.1 us -> 35.6 us
    ppermute x36, starting transfers between devices: 26.7 us -> 32.3 us  [send(): lax.ppermute(value, 'exp', [(place(*who), place(*move(*who))) for who in...]
    ppermute x36, waiting for transfers between devices: 71.8 us -> 66.7 us  [send(): lax.ppermute(value, 'exp', [(place(*who), place(*move(*who))) for who in...]
  transfers between devices with their start and end apart: 36 -> 36, of which waited for: 15 -> 14; matrix products, arithmetic and copies ran while one was open for 1% -> 1% of each run, Pallas kernels for 15% -> 14%
where the time goes in v7:
time: 138 us
  waiting for transfers between devices  66.7 us (48%)
  Pallas kernels  35.6 us (26%)
  starting transfers between devices  32.3 us (23%)
    ppermute x36, waiting for transfers between devices, send(): lax.ppermute(value, 'exp', [(place(*who), place(*move(*who))) for who in...  66.7 us
    ppermute x36, starting transfers between devices, send(): lax.ppermute(value, 'exp', [(place(*who), place(*move(*who))) for who in...  32.3 us
    pallas_call x1, Pallas kernels, middle(): pl.pallas_call(functools.partial(middle_kernel, pairs, cut, part), in_spe...  12.2 us
    pallas_call x1, Pallas kernels, begin(): pl.pallas_call(functools.partial(begin_kernel, pairs, part), in_specs=[VM...  7.52 us
    pallas_call x1, Pallas kernels, finish(): pl.pallas_call(functools.partial(finish_kernel, pairs, part), in_specs=[V...  4.56 us
    pallas_call x10, Pallas kernels, combine(): pl.pallas_call(combine_kernel, out_shape=(jax.ShapeDtypeStruct((tok, widt...  4 us
    pallas_call x8, Pallas kernels, dispatch(): pl.pallas_call(functools.partial(dispatch_kernel, top), in_specs=[pl.Bloc...  3.97 us
  transfers between devices with their start and end apart: 36, of which 14 were waited for; matrix products, arithmetic and copies ran while one was open for 1% of the time, Pallas kernels for 14%

profile of v7, /device:TPU:0, one launch (start us, length us, event | category | flops | bytes accessed | tf_op | source)
XLA Modules:
  0.0 137.6 jit_solution(14605188885340447574)
XLA Ops:
  0.0 1.9 %shard_map.65.x0_ref = bf16[128,2176]{1,0:T(8,128)(2,1)} custom-call(s32[8,128]{1,0:T(8,128)} %bitcast.3, f32[8,128]{1,0:T(8,128)} %bitcast.4, bf16[128,2048]{1,0:T(8,128)(2,1)} %tokens_ref.1), custom_call_target="tpu_custom_call" | custom-call | tf_op jit(solution)/shard_map/pallas_call | solution.py:46
  2.4 4.6 %collective-permute-start = (bf16[128,2176]{1,0:T(8,128)(2,1)}, bf16[128,2176]{1,0:T(8,128)(2,1)S(1)}, u32[]{:S(2)}, u32[]{:S(2)}) collective-permute-start(bf16[128,2176]{1,0:T(8,128)(2,1)} %shard_map.65.x0_ref), channel_id=1, source_target_pairs={{0,12},{1,13},{2,14},{3,15},{4,0},{5,1},{6,2},{7,3},{8,4},{9,5},{1... | collective-permute-start | bytes 1671176 | tf_op jit(solution)/shard_map/ppermute | solution.py:388
  7.0 1.1 copy-done
  8.1 1.5 %collective-permute-start.3 = (bf16[128,2176]{1,0:T(8,128)(2,1)S(1)}, bf16[128,2176]{1,0:T(8,128)(2,1)S(1)}, u32[]{:S(2)}, u32[]{:S(2)}) collective-permute-start(bf16[128,2176]{1,0:T(8,128)(2,1)S(1)} %copy-done), channel_id=1, source_target_pairs={{0,2},{1,3},{2,0},{3,1},{4,6},{5,7},{6,4},{7,5},{8,10},{9,11},{10,... | collective-permute-start | bytes 1671176 | tf_op jit(solution)/shard_map/ppermute | solution.py:388
  9.6 10.7 %collective-permute-done.x0_ref = bf16[128,2176]{1,0:T(8,128)(2,1)S(1)} collective-permute-done((bf16[128,2176]{1,0:T(8,128)(2,1)}, bf16[128,2176]{1,0:T(8,128)(2,1)S(1)}, u32[]{:S(2)}, u32[]{:S(2)}) %collective-permute-start) | collective-permute-done | bytes 557088 | tf_op jit(solution)/shard_map/ppermute | solution.py:388
  20.3 1.5 %collective-permute-start.8 = (bf16[128,2176]{1,0:T(8,128)(2,1)S(1)}, bf16[128,2176]{1,0:T(8,128)(2,1)S(1)}, u32[]{:S(2)}, u32[]{:S(2)}) collective-permute-start(bf16[128,2176]{1,0:T(8,128)(2,1)S(1)} %collective-permute-done.x0_ref), channel_id=1, source_target_pairs={{0,2},{1,3},{2,0},{3,1},{4,6},{5,7},{6,4},{7,5},{8,10},{9,11},{10,... | collective-permute-start | bytes 1671176 | tf_op jit(solution)/shard_map/ppermute | solution.py:388
  21.8 4.2 %collective-permute-start.5 = (bf16[128,2176]{1,0:T(8,128)(2,1)S(1)}, bf16[128,2176]{1,0:T(8,128)(2,1)S(1)}, u32[]{:S(2)}, u32[]{:S(2)}) collective-permute-start(bf16[128,2176]{1,0:T(8,128)(2,1)S(1)} %collective-permute-done.x0_ref), channel_id=1, source_target_pairs={{0,12},{1,13},{2,14},{3,15},{4,0},{5,1},{6,2},{7,3},{8,4},{9,5},{1... | collective-permute-start | bytes 1671176 | tf_op jit(solution)/shard_map/ppermute | solution.py:388
  26.0 0.5 shard_map.67
  26.5 6.5 %collective-permute-done.2.x0_ref = bf16[128,2176]{1,0:T(8,128)(2,1)S(1)} collective-permute-done((bf16[128,2176]{1,0:T(8,128)(2,1)S(1)}, bf16[128,2176]{1,0:T(8,128)(2,1)S(1)}, u32[]{:S(2)}, u32[]{:S(2)}) %collective-permute-start.2) | collective-permute-done | bytes 557088 | tf_op jit(solution)/shard_map/ppermute | solution.py:388
  33.0 1.5 %collective-permute-start.10 = (bf16[128,2176]{1,0:T(8,128)(2,1)S(1)}, bf16[128,2176]{1,0:T(8,128)(2,1)S(1)}, u32[]{:S(2)}, u32[]{:S(2)}) collective-permute-start(bf16[128,2176]{1,0:T(8,128)(2,1)S(1)} %collective-permute-done.2.x0_ref), channel_id=1, source_target_pairs={{0,2},{1,3},{2,0},{3,1},{4,6},{5,7},{6,4},{7,5},{8,10},{9,11},{10,... | collective-permute-start | bytes 1671176 | tf_op jit(solution)/shard_map/ppermute | solution.py:388
  34.6 0.5 collective-permute-start.7
  35.1 0.5 shard_map.69
  35.7 8.9 %collective-permute-done.5.x0_ref = bf16[128,2176]{1,0:T(8,128)(2,1)S(1)} collective-permute-done((bf16[128,2176]{1,0:T(8,128)(2,1)S(1)}, bf16[128,2176]{1,0:T(8,128)(2,1)S(1)}, u32[]{:S(2)}, u32[]{:S(2)}) %collective-permute-start.5) | collective-permute-done | bytes 557088 | tf_op jit(solution)/shard_map/ppermute | solution.py:388
  44.7 1.5 %collective-permute-start.11 = (bf16[128,896]{1,0:T(8,128)(2,1)S(1)}, bf16[128,896]{1,0:T(8,128)(2,1)S(1)}, u32[]{:S(2)}, u32[]{:S(2)}) collective-permute-start(bf16[128,896]{1,0:T(8,128)(2,1)S(1)} %slice.13), channel_id=1, source_target_pairs={{0,2},{1,3},{2,0},{3,1},{4,6},{5,7},{6,4},{7,5},{8,10},{9,11},{10,... | collective-permute-start | bytes 688136 | tf_op jit(solution)/shard_map/ppermute | solution.py:388
  46.3 0.5 shard_map.71
  46.8 0.5 shard_map.72
  47.3 0.5 shard_map.73
  47.9 4.8 %collective-permute-done.11.x0_ref = bf16[128,896]{1,0:T(8,128)(2,1)S(1)} collective-permute-done((bf16[128,896]{1,0:T(8,128)(2,1)S(1)}, bf16[128,896]{1,0:T(8,128)(2,1)S(1)}, u32[]{:S(2)}, u32[]{:S(2)}) %collective-permute-start.11) | collective-permute-done | bytes 229408 | tf_op jit(solution)/shard_map/ppermute | solution.py:388
  52.7 0.5 collective-permute-start.12
  53.2 1.6 %collective-permute-start.14 = (bf16[128,1280]{1,0:T(8,128)(2,1)S(1)}, bf16[128,1280]{1,0:T(8,128)(2,1)S(1)}, u32[]{:S(2)}, u32[]{:S(2)}) collective-permute-start(bf16[128,1280]{1,0:T(8,128)(2,1)S(1)} %slice.14), channel_id=1, source_target_pairs={{0,2},{1,3},{2,0},{3,1},{4,6},{5,7},{6,4},{7,5},{8,10},{9,11},{10,... | collective-permute-start | bytes 983048 | tf_op jit(solution)/shard_map/ppermute | solution.py:388
  55.4 0.5 shard_map.76
  55.9 0.5 shard_map.77
  56.4 7.5 %shard_map.78 = (f32[4,384,768]{2,1,0:T(8,128)S(1)}, f32[4,384,768]{2,1,0:T(8,128)S(1)}, bf16[1280,768]{1,0:T(8,128)(2,1)S(1)}, bf16[1280,768]{1,0:T(8,128)(2,1)S(1)}) custom-call(f32[8,128]{1,0:T(8,128)S(1)} %shard_map.74.token_ref.in_ref, bf16[4,48,2048]{2,1,0:T(8,128)(2,1)S(1)} %get-tuple-element.159.refs_0_, ...), custom_call_target="tpu_custom_call" | custom-call | flops 40000000000 | tf_op jit(solution)/shard_map/pallas_call | solution.py:222
  64.2 1.5 %collective-permute-done.16.x1_ref = bf16[128,1280]{1,0:T(8,128)(2,1)S(1)} collective-permute-done((bf16[128,1280]{1,0:T(8,128)(2,1)S(1)}, bf16[128,1280]{1,0:T(8,128)(2,1)S(1)}, u32[]{:S(2)}, u32[]{:S(2)}) %collective-permute-start.16) | collective-permute-done | bytes 327712 | tf_op jit(solution)/shard_map/ppermute | solution.py:388
  66.0 12.2 %shard_map.80 = (bf16[4,384,768]{2,1,0:T(8,128)(2,1)S(1)}, bf16[4,48,1024]{2,1,0:T(8,128)(2,1)S(1)}, bf16[4,48,1024]{2,1,0:T(8,128)(2,1)S(1)}, bf16[4,48,1024]{2...) custom-call(bf16[4,48,2048]{2,1,0:T(8,128)(2,1)S(1)} %get-tuple-elem, ...), custom_call_target="tpu_custom_call" | custom-call | tf_op jit(solution)/shard_map/pallas_call | solution.py:270
  79.5 0.6 collective-permute-done.17
  80.2 1.6 %collective-permute-start.18 = (bf16[128,1024]{1,0:T(8,128)(2,1)S(1)}, bf16[128,1024]{1,0:T(8,128)(2,1)S(1)}, u32[]{:S(2)}, u32[]{:S(2)}) collective-permute-start(bf16[128,1024]{1,0:T(8,128)(2,1)S(1)} %add_convert_fusion.7), channel_id=1, source_target_pairs={{0,2},{1,3},{2,0},{3,1},{4,6},{5,7},{6,4},{7,5},{8,10},{9,11},{10,... | collective-permute-start | bytes 786440 | tf_op jit(solution)/shard_map/ppermute | solution.py:388
  81.8 4.6 %shard_map.83 = (bf16[4,48,1024]{2,1,0:T(8,128)(2,1)S(1)}, bf16[4,48,1024]{2,1,0:T(8,128)(2,1)S(1)}, bf16[4,48,1024]{2,1,0:T(8,128)(2,1)S(1)}, bf16[4,48,1024]{2...) custom-call(bf16[4,384,768]{2,1,0:T(8,128)(2,1)S(1)} %get-tuple-elem, ...), custom_call_target="tpu_custom_call" | custom-call | tf_op jit(solution)/shard_map/pallas_call | solution.py:296
  87.1 0.6 collective-permute-start.28
  88.2 0.5 shard_map.96
  88.7 0.6 collective-permute-start.34
  89.3 0.8 collective-permute-done.20
  90.2 0.7 collective-permute-start.21
  91.1 1.0 collective-permute-start.27
  92.2 1.7 %collective-permute-start.23 = (bf16[128,2048]{1,0:T(8,128)(2,1)S(1)}, bf16[128,2048]{1,0:T(8,128)(2,1)S(1)}, u32[]{:S(2)}, u32[]{:S(2)}) collective-permute-start(bf16[128,2048]{1,0:T(8,128)(2,1)S(1)} %add_convert_fusion.3), channel_id=1, source_target_pairs={{0,2},{1,3},{2,0},{3,1},{4,6},{5,7},{6,4},{7,5},{8,10},{9,11},{10,... | collective-permute-start | bytes 1572872 | tf_op jit(solution)/shard_map/ppermute | solution.py:388
  94.9 0.5 shard_map.94
  95.4 0.5 shard_map.95
  95.8 5.4 %collective-permute-done.21 = bf16[128,1024]{1,0:T(8,128)(2,1)S(1)} collective-permute-done((bf16[128,1024]{1,0:T(8,128)(2,1)S(1)}, bf16[128,1024]{1,0:T(8,128)(2,1)S(1)}, u32[]{:S(2)}, u32[]{:S(2)}) %collective-permute-start.21) | collective-permute-done | bytes 262176 | tf_op jit(solution)/shard_map/ppermute | solution.py:388
  101.4 4.4 %collective-permute-done.23 = bf16[128,2048]{1,0:T(8,128)(2,1)S(1)} collective-permute-done((bf16[128,2048]{1,0:T(8,128)(2,1)S(1)}, bf16[128,2048]{1,0:T(8,128)(2,1)S(1)}, u32[]{:S(2)}, u32[]{:S(2)}) %collective-permute-start.23) | collective-permute-done | bytes 524320 | tf_op jit(solution)/shard_map/ppermute | solution.py:388
  106.1 1.6 %collective-permute-start.25 = (bf16[128,2048]{1,0:T(8,128)(2,1)S(1)}, bf16[128,2048]{1,0:T(8,128)(2,1)S(1)}, u32[]{:S(2)}, u32[]{:S(2)}) collective-permute-start(bf16[128,2048]{1,0:T(8,128)(2,1)S(1)} %pad_maximum_fusion), channel_id=1, source_target_pairs={{0,2},{1,3},{2,0},{3,1},{4,6},{5,7},{6,4},{7,5},{8,10},{9,11},{10,... | collective-permute-start | bytes 1572872 | tf_op jit(solution)/shard_map/ppermute | solution.py:388
  108.2 0.6 collective-permute-start.31
  108.7 3.0 %collective-permute-done.29 = bf16[128,1024]{1,0:T(8,128)(2,1)S(1)} collective-permute-done((bf16[128,1024]{1,0:T(8,128)(2,1)S(1)}, bf16[128,1024]{1,0:T(8,128)(2,1)S(1)}, u32[]{:S(2)}, u32[]{:S(2)}) %collective-permute-start.29) | collective-permute-done | bytes 262176 | tf_op jit(solution)/shard_map/ppermute | solution.py:388
  111.8 1.5 %collective-permute-start.35 = (bf16[128,2048]{1,0:T(8,128)(2,1)S(1)}, bf16[128,2048]{1,0:T(8,128)(2,1)S(1)}, u32[]{:S(2)}, u32[]{:S(2)}) collective-permute-start(bf16[128,2048]{1,0:T(8,128)(2,1)S(1)} %add_convert_fusion), channel_id=1, source_target_pairs={{0,12},{1,13},{2,14},{3,15},{4,0},{5,1},{6,2},{7,3},{8,4},{9,5},{1... | collective-permute-start | bytes 1572872 | tf_op jit(solution)/shard_map/ppermute | solution.py:388
  113.2 7.6 %collective-permute-done.25 = bf16[128,2048]{1,0:T(8,128)(2,1)S(1)} collective-permute-done((bf16[128,2048]{1,0:T(8,128)(2,1)S(1)}, bf16[128,2048]{1,0:T(8,128)(2,1)S(1)}, u32[]{:S(2)}, u32[]{:S(2)}) %collective-permute-start.25) | collective-permute-done | bytes 524320 | tf_op jit(solution)/shard_map/ppermute | solution.py:388
  121.2 2.9 %collective-permute-start.33 = (bf16[128,2048]{1,0:T(8,128)(2,1)S(1)}, bf16[128,2048]{1,0:T(8,128)(2,1)S(1)}, u32[]{:S(2)}, u32[]{:S(2)}) collective-permute-start(bf16[128,2048]{1,0:T(8,128)(2,1)S(1)} %add_convert_fusion.1), channel_id=1, source_target_pairs={{0,4},{1,5},{2,6},{3,7},{4,8},{5,9},{6,10},{7,11},{8,12},{9,13},{1... | collective-permute-start | bytes 1572872 | tf_op jit(solution)/shard_map/ppermute | solution.py:388
  124.2 7.5 %collective-permute-done.31.refs_0_ = bf16[128,2048]{1,0:T(8,128)(2,1)S(1)} collective-permute-done((bf16[128,2048]{1,0:T(8,128)(2,1)S(1)}, bf16[128,2048]{1,0:T(8,128)(2,1)S(1)}, u32[]{:S(2)}, u32[]{:S(2)}) %collective-permute-start.31) | collective-permute-done | bytes 524320 | tf_op jit(solution)/shard_map/ppermute | solution.py:388
  131.7 4.8 %collective-permute-done.35.refs_2_ = bf16[128,2048]{1,0:T(8,128)(2,1)S(1)} collective-permute-done((bf16[128,2048]{1,0:T(8,128)(2,1)S(1)}, bf16[128,2048]{1,0:T(8,128)(2,1)S(1)}, u32[]{:S(2)}, u32[]{:S(2)}) %collective-permute-start.35) | collective-permute-done | bytes 524320 | tf_op jit(solution)/shard_map/ppermute | solution.py:388
  136.5 1.1 shard_map.97
  (76 shorter events, 7.0 us)
Async XLA Ops:
  1.9 7.7 %collective-permute-start.1 = (bf16[128,2176]{1,0:T(8,128)(2,1)}, bf16[128,2176]{1,0:T(8,128)(2,1)S(1)}, u32[]{:S(2)}, u32[]{:S(2)}) collective-permute-start(bf16[128,2176]{1,0:T(8,128)(2,1)} %shard_map.65.x0_ref), channel_id=1, source_target_pairs={{0,1},{1,0},{2,3},{3,2},{4,5},{5,4},{6,7},{7,6},{8,9},{9,8},{10,11... | collective-permute-start | bytes 1671176 | tf_op jit(solution)/shard_map/ppermute | solution.py:388
  2.4 17.9 %collective-permute-start = (bf16[128,2176]{1,0:T(8,128)(2,1)}, bf16[128,2176]{1,0:T(8,128)(2,1)S(1)}, u32[]{:S(2)}, u32[]{:S(2)}) collective-permute-start(bf16[128,2176]{1,0:T(8,128)(2,1)} %shard_map.65.x0_ref), channel_id=1, source_target_pairs={{0,12},{1,13},{2,14},{3,15},{4,0},{5,1},{6,2},{7,3},{8,4},{9,5},{1... | collective-permute-start | bytes 1671176 | tf_op jit(solution)/shard_map/ppermute | solution.py:388
  7.0 1.1 copy-start
  8.1 18.5 %collective-permute-start.3 = (bf16[128,2176]{1,0:T(8,128)(2,1)S(1)}, bf16[128,2176]{1,0:T(8,128)(2,1)S(1)}, u32[]{:S(2)}, u32[]{:S(2)}) collective-permute-start(bf16[128,2176]{1,0:T(8,128)(2,1)S(1)} %copy-done), channel_id=1, source_target_pairs={{0,2},{1,3},{2,0},{3,1},{4,6},{5,7},{6,4},{7,5},{8,10},{9,11},{10,... | collective-permute-start | bytes 1671176 | tf_op jit(solution)/shard_map/ppermute | solution.py:388
  9.6 23.4 %collective-permute-start.2 = (bf16[128,2176]{1,0:T(8,128)(2,1)S(1)}, bf16[128,2176]{1,0:T(8,128)(2,1)S(1)}, u32[]{:S(2)}, u32[]{:S(2)}) collective-permute-start(bf16[128,2176]{1,0:T(8,128)(2,1)S(1)} %copy-done), channel_id=1, source_target_pairs={{0,4},{1,5},{2,6},{3,7},{4,8},{5,9},{6,10},{7,11},{8,12},{9,13},{1... | collective-permute-start | bytes 1671176 | tf_op jit(solution)/shard_map/ppermute | solution.py:388
  20.3 15.3 %collective-permute-start.8 = (bf16[128,2176]{1,0:T(8,128)(2,1)S(1)}, bf16[128,2176]{1,0:T(8,128)(2,1)S(1)}, u32[]{:S(2)}, u32[]{:S(2)}) collective-permute-start(bf16[128,2176]{1,0:T(8,128)(2,1)S(1)} %collective-permute-done.x0_ref), channel_id=1, source_target_pairs={{0,2},{1,3},{2,0},{3,1},{4,6},{5,7},{6,4},{7,5},{8,10},{9,11},{10,... | collective-permute-start | bytes 1671176 | tf_op jit(solution)/shard_map/ppermute | solution.py:388
  21.8 11.2 %collective-permute-start.4 = (bf16[128,2176]{1,0:T(8,128)(2,1)S(1)}, bf16[128,2176]{1,0:T(8,128)(2,1)S(1)}, u32[]{:S(2)}, u32[]{:S(2)}) collective-permute-start(bf16[128,2176]{1,0:T(8,128)(2,1)S(1)} %collective-permute-done.x0_ref), channel_id=1, source_target_pairs={{0,1},{1,0},{2,3},{3,2},{4,5},{5,4},{6,7},{7,6},{8,9},{9,8},{10,11... | collective-permute-start | bytes 1671176 | tf_op jit(solution)/shard_map/ppermute | solution.py:388
  21.8 22.8 %collective-permute-start.5 = (bf16[128,2176]{1,0:T(8,128)(2,1)S(1)}, bf16[128,2176]{1,0:T(8,128)(2,1)S(1)}, u32[]{:S(2)}, u32[]{:S(2)}) collective-permute-start(bf16[128,2176]{1,0:T(8,128)(2,1)S(1)} %collective-permute-done.x0_ref), channel_id=1, source_target_pairs={{0,12},{1,13},{2,14},{3,15},{4,0},{5,1},{6,2},{7,3},{8,4},{9,5},{1... | collective-permute-start | bytes 1671176 | tf_op jit(solution)/shard_map/ppermute | solution.py:388
  33.0 14.8 %collective-permute-start.10 = (bf16[128,2176]{1,0:T(8,128)(2,1)S(1)}, bf16[128,2176]{1,0:T(8,128)(2,1)S(1)}, u32[]{:S(2)}, u32[]{:S(2)}) collective-permute-start(bf16[128,2176]{1,0:T(8,128)(2,1)S(1)} %collective-permute-done.2.x0_ref), channel_id=1, source_target_pairs={{0,2},{1,3},{2,0},{3,1},{4,6},{5,7},{6,4},{7,5},{8,10},{9,11},{10,... | collective-permute-start | bytes 1671176 | tf_op jit(solution)/shard_map/ppermute | solution.py:388
  34.5 10.0 %collective-permute-start.6 = (bf16[128,2176]{1,0:T(8,128)(2,1)S(1)}, bf16[128,2176]{1,0:T(8,128)(2,1)S(1)}, u32[]{:S(2)}, u32[]{:S(2)}) collective-permute-start(bf16[128,2176]{1,0:T(8,128)(2,1)S(1)} %collective-permute-done.2.x0_ref), channel_id=1, source_target_pairs={{0,1},{1,0},{2,3},{3,2},{4,5},{5,4},{6,7},{7,6},{8,9},{9,8},{10,11... | collective-permute-start | bytes 1671176 | tf_op jit(solution)/shard_map/ppermute | solution.py:388
  34.6 10.0 %collective-permute-start.7 = (bf16[128,2176]{1,0:T(8,128)(2,1)S(1)}, bf16[128,2176]{1,0:T(8,128)(2,1)S(1)}, u32[]{:S(2)}, u32[]{:S(2)}) collective-permute-start(bf16[128,2176]{1,0:T(8,128)(2,1)S(1)} %collective-permute-done.3.x0_ref), channel_id=1, source_target_pairs={{0,1},{1,0},{2,3},{3,2},{4,5},{5,4},{6,7},{7,6},{8,9},{9,8},{10,11... | collective-permute-start | bytes 1671176 | tf_op jit(solution)/shard_map/ppermute | solution.py:388
  35.6 9.0 %collective-permute-start.9 = (bf16[128,2176]{1,0:T(8,128)(2,1)S(1)}, bf16[128,2176]{1,0:T(8,128)(2,1)S(1)}, u32[]{:S(2)}, u32[]{:S(2)}) collective-permute-start(bf16[128,2176]{1,0:T(8,128)(2,1)S(1)} %collective-permute-done.8.x0_ref), channel_id=1, source_target_pairs={{0,1},{1,0},{2,3},{3,2},{4,5},{5,4},{6,7},{7,6},{8,9},{9,8},{10,11... | collective-permute-start | bytes 1671176 | tf_op jit(solution)/shard_map/ppermute | solution.py:388
  44.6 10.8 %collective-permute-start.13 = (bf16[128,2176]{1,0:T(8,128)(2,1)S(1)}, bf16[128,2176]{1,0:T(8,128)(2,1)S(1)}, u32[]{:S(2)}, u32[]{:S(2)}) collective-permute-start(bf16[128,2176]{1,0:T(8,128)(2,1)S(1)} %collective-permute-done.5.x0_ref), channel_id=1, source_target_pairs={{0,1},{1,0},{2,3},{3,2},{4,5},{5,4},{6,7},{7,6},{8,9},{9,8},{10,11... | collective-permute-start | bytes 1671176 | tf_op jit(solution)/shard_map/ppermute | solution.py:388
  44.7 8.0 %collective-permute-start.11 = (bf16[128,896]{1,0:T(8,128)(2,1)S(1)}, bf16[128,896]{1,0:T(8,128)(2,1)S(1)}, u32[]{:S(2)}, u32[]{:S(2)}) collective-permute-start(bf16[128,896]{1,0:T(8,128)(2,1)S(1)} %slice.13), channel_id=1, source_target_pairs={{0,2},{1,3},{2,0},{3,1},{4,6},{5,7},{6,4},{7,5},{8,10},{9,11},{10,... | collective-permute-start | bytes 688136 | tf_op jit(solution)/shard_map/ppermute | solution.py:388
  52.7 3.2 %collective-permute-start.15 = (bf16[128,2176]{1,0:T(8,128)(2,1)S(1)}, bf16[128,2176]{1,0:T(8,128)(2,1)S(1)}, u32[]{:S(2)}, u32[]{:S(2)}) collective-permute-start(bf16[128,2176]{1,0:T(8,128)(2,1)S(1)} %collective-permute-done.10.x0_ref), channel_id=1, source_target_pairs={{0,1},{1,0},{2,3},{3,2},{4,5},{5,4},{6,7},{7,6},{8,9},{9,8},{10,11... | collective-permute-start | bytes 1671176 | tf_op jit(solution)/shard_map/ppermute | solution.py:388
  52.7 2.3 %collective-permute-start.12 = (bf16[128,896]{1,0:T(8,128)(2,1)S(1)}, bf16[128,896]{1,0:T(8,128)(2,1)S(1)}, u32[]{:S(2)}, u32[]{:S(2)}) collective-permute-start(bf16[128,896]{1,0:T(8,128)(2,1)S(1)} %collective-permute-done.11.x0_ref), channel_id=1, source_target_pairs={{0,1},{1,0},{2,3},{3,2},{4,5},{5,4},{6,7},{7,6},{8,9},{9,8},{10,11... | collective-permute-start | bytes 688136 | tf_op jit(solution)/shard_map/ppermute | solution.py:388
  53.2 10.7 %collective-permute-start.14 = (bf16[128,1280]{1,0:T(8,128)(2,1)S(1)}, bf16[128,1280]{1,0:T(8,128)(2,1)S(1)}, u32[]{:S(2)}, u32[]{:S(2)}) collective-permute-start(bf16[128,1280]{1,0:T(8,128)(2,1)S(1)} %slice.14), channel_id=1, source_target_pairs={{0,2},{1,3},{2,0},{3,1},{4,6},{5,7},{6,4},{7,5},{8,10},{9,11},{10,... | collective-permute-start | bytes 983048 | tf_op jit(solution)/shard_map/ppermute | solution.py:388
  64.0 1.7 %collective-permute-start.16 = (bf16[128,1280]{1,0:T(8,128)(2,1)S(1)}, bf16[128,1280]{1,0:T(8,128)(2,1)S(1)}, u32[]{:S(2)}, u32[]{:S(2)}) collective-permute-start(bf16[128,1280]{1,0:T(8,128)(2,1)S(1)} %collective-permute-done.14.x0_ref), channel_id=1, source_target_pairs={{0,1},{1,0},{2,3},{3,2},{4,5},{5,4},{6,7},{7,6},{8,9},{9,8},{10,11... | collective-permute-start | bytes 983048 | tf_op jit(solution)/shard_map/ppermute | solution.py:388
  78.6 1.6 %collective-permute-start.17 = (bf16[128,1024]{1,0:T(8,128)(2,1)S(1)}, bf16[128,1024]{1,0:T(8,128)(2,1)S(1)}, u32[]{:S(2)}, u32[]{:S(2)}) collective-permute-start(bf16[128,1024]{1,0:T(8,128)(2,1)S(1)} %get-tuple-element.187), channel_id=1, source_target_pairs={{0,1},{1,0},{2,3},{3,2},{4,5},{5,4},{6,7},{7,6},{8,9},{9,8},{10,11... | collective-permute-start | bytes 786440 | tf_op jit(solution)/shard_map/ppermute | solution.py:388
  79.1 11.9 %collective-permute-start.26 = (bf16[128,1024]{1,0:T(8,128)(2,1)S(1)}, bf16[128,1024]{1,0:T(8,128)(2,1)S(1)}, u32[]{:S(2)}, u32[]{:S(2)}) collective-permute-start(bf16[128,1024]{1,0:T(8,128)(2,1)S(1)} %get-tuple-element.227), channel_id=1, source_target_pairs={{0,1},{1,0},{2,3},{3,2},{4,5},{5,4},{6,7},{7,6},{8,9},{9,8},{10,11... | collective-permute-start | bytes 786440 | tf_op jit(solution)/shard_map/ppermute | solution.py:388
  80.2 8.5 %collective-permute-start.18 = (bf16[128,1024]{1,0:T(8,128)(2,1)S(1)}, bf16[128,1024]{1,0:T(8,128)(2,1)S(1)}, u32[]{:S(2)}, u32[]{:S(2)}) collective-permute-start(bf16[128,1024]{1,0:T(8,128)(2,1)S(1)} %add_convert_fusion.7), channel_id=1, source_target_pairs={{0,2},{1,3},{2,0},{3,1},{4,6},{5,7},{6,4},{7,5},{8,10},{9,11},{10,... | collective-permute-start | bytes 786440 | tf_op jit(solution)/shard_map/ppermute | solution.py:388
  86.7 2.5 %collective-permute-start.19 = (bf16[128,1024]{1,0:T(8,128)(2,1)S(1)}, bf16[128,1024]{1,0:T(8,128)(2,1)S(1)}, u32[]{:S(2)}, u32[]{:S(2)}) collective-permute-start(bf16[128,1024]{1,0:T(8,128)(2,1)S(1)} %get-tuple-element.199), channel_id=1, source_target_pairs={{0,1},{1,0},{2,3},{3,2},{4,5},{5,4},{6,7},{7,6},{8,9},{9,8},{10,11... | collective-permute-start | bytes 786440 | tf_op jit(solution)/shard_map/ppermute | solution.py:388
  87.1 5.0 %collective-permute-start.28 = (bf16[128,1024]{1,0:T(8,128)(2,1)S(1)}, bf16[128,1024]{1,0:T(8,128)(2,1)S(1)}, u32[]{:S(2)}, u32[]{:S(2)}) collective-permute-start(bf16[128,1024]{1,0:T(8,128)(2,1)S(1)} %get-tuple-element.231), channel_id=1, source_target_pairs={{0,1},{1,0},{2,3},{3,2},{4,5},{5,4},{6,7},{7,6},{8,9},{9,8},{10,11... | collective-permute-start | bytes 786440 | tf_op jit(solution)/shard_map/ppermute | solution.py:388
  88.1 2.0 %collective-permute-start.20 = (bf16[128,2048]{1,0:T(8,128)(2,1)S(1)}, bf16[128,2048]{1,0:T(8,128)(2,1)S(1)}, u32[]{:S(2)}, u32[]{:S(2)}) collective-permute-start(bf16[128,2048]{1,0:T(8,128)(2,1)S(1)} %get-tuple-element.204), channel_id=1, source_target_pairs={{0,1},{1,0},{2,3},{3,2},{4,5},{5,4},{6,7},{7,6},{8,9},{9,8},{10,11... | collective-permute-start | bytes 1572872 | tf_op jit(solution)/shard_map/ppermute | solution.py:388
  88.7 19.0 %collective-permute-start.34 = (bf16[128,2048]{1,0:T(8,128)(2,1)S(1)}, bf16[128,2048]{1,0:T(8,128)(2,1)S(1)}, u32[]{:S(2)}, u32[]{:S(2)}) collective-permute-start(bf16[128,2048]{1,0:T(8,128)(2,1)S(1)} %get-tuple-element.251), channel_id=1, source_target_pairs={{0,1},{1,0},{2,3},{3,2},{4,5},{5,4},{6,7},{7,6},{8,9},{9,8},{10,11... | collective-permute-start | bytes 1572872 | tf_op jit(solution)/shard_map/ppermute | solution.py:388
  90.2 11.0 %collective-permute-start.21 = (bf16[128,1024]{1,0:T(8,128)(2,1)S(1)}, bf16[128,1024]{1,0:T(8,128)(2,1)S(1)}, u32[]{:S(2)}, u32[]{:S(2)}) collective-permute-start(bf16[128,1024]{1,0:T(8,128)(2,1)S(1)} %add_convert_fusion.6), channel_id=1, source_target_pairs={{0,4},{1,5},{2,6},{3,7},{4,8},{5,9},{6,10},{7,11},{8,12},{9,13},{1... | collective-permute-start | bytes 786440 | tf_op jit(solution)/shard_map/ppermute | solution.py:388
  91.1 17.1 %collective-permute-start.27 = (bf16[128,1024]{1,0:T(8,128)(2,1)S(1)}, bf16[128,1024]{1,0:T(8,128)(2,1)S(1)}, u32[]{:S(2)}, u32[]{:S(2)}) collective-permute-start(bf16[128,1024]{1,0:T(8,128)(2,1)S(1)} %add_convert_fusion.5), channel_id=1, source_target_pairs={{0,4},{1,5},{2,6},{3,7},{4,8},{5,9},{6,10},{7,11},{8,12},{9,13},{1... | collective-permute-start | bytes 786440 | tf_op jit(solution)/shard_map/ppermute | solution.py:388
  92.2 13.6 %collective-permute-start.23 = (bf16[128,2048]{1,0:T(8,128)(2,1)S(1)}, bf16[128,2048]{1,0:T(8,128)(2,1)S(1)}, u32[]{:S(2)}, u32[]{:S(2)}) collective-permute-start(bf16[128,2048]{1,0:T(8,128)(2,1)S(1)} %add_convert_fusion.3), channel_id=1, source_target_pairs={{0,2},{1,3},{2,0},{3,1},{4,6},{5,7},{6,4},{7,5},{8,10},{9,11},{10,... | collective-permute-start | bytes 1572872 | tf_op jit(solution)/shard_map/ppermute | solution.py:388
  94.4 6.9 %collective-permute-start.22 = (bf16[128,2048]{1,0:T(8,128)(2,1)S(1)}, bf16[128,2048]{1,0:T(8,128)(2,1)S(1)}, u32[]{:S(2)}, u32[]{:S(2)}) collective-permute-start(bf16[128,2048]{1,0:T(8,128)(2,1)S(1)} %get-tuple-element.215), channel_id=1, source_target_pairs={{0,1},{1,0},{2,3},{3,2},{4,5},{5,4},{6,7},{7,6},{8,9},{9,8},{10,11... | collective-permute-start | bytes 1572872 | tf_op jit(solution)/shard_map/ppermute | solution.py:388
  101.2 4.6 %collective-permute-start.24 = (bf16[128,2048]{1,0:T(8,128)(2,1)S(1)}, bf16[128,2048]{1,0:T(8,128)(2,1)S(1)}, u32[]{:S(2)}, u32[]{:S(2)}) collective-permute-start(bf16[128,2048]{1,0:T(8,128)(2,1)S(1)} %get-tuple-element.222), channel_id=1, source_target_pairs={{0,1},{1,0},{2,3},{3,2},{4,5},{5,4},{6,7},{7,6},{8,9},{9,8},{10,11... | collective-permute-start | bytes 1572872 | tf_op jit(solution)/shard_map/ppermute | solution.py:388
  101.2 10.5 %collective-permute-start.29 = (bf16[128,1024]{1,0:T(8,128)(2,1)S(1)}, bf16[128,1024]{1,0:T(8,128)(2,1)S(1)}, u32[]{:S(2)}, u32[]{:S(2)}) collective-permute-start(bf16[128,1024]{1,0:T(8,128)(2,1)S(1)} %add_convert_fusion.4), channel_id=1, source_target_pairs={{0,4},{1,5},{2,6},{3,7},{4,8},{5,9},{6,10},{7,11},{8,12},{9,13},{1... | collective-permute-start | bytes 786440 | tf_op jit(solution)/shard_map/ppermute | solution.py:388
  105.8 15.1 %collective-permute-start.32 = (bf16[128,2048]{1,0:T(8,128)(2,1)S(1)}, bf16[128,2048]{1,0:T(8,128)(2,1)S(1)}, u32[]{:S(2)}, u32[]{:S(2)}) collective-permute-start(bf16[128,2048]{1,0:T(8,128)(2,1)S(1)} %get-tuple-element.243), channel_id=1, source_target_pairs={{0,1},{1,0},{2,3},{3,2},{4,5},{5,4},{6,7},{7,6},{8,9},{9,8},{10,11... | collective-permute-start | bytes 1572872 | tf_op jit(solution)/shard_map/ppermute | solution.py:388
  106.1 14.8 %collective-permute-start.25 = (bf16[128,2048]{1,0:T(8,128)(2,1)S(1)}, bf16[128,2048]{1,0:T(8,128)(2,1)S(1)}, u32[]{:S(2)}, u32[]{:S(2)}) collective-permute-start(bf16[128,2048]{1,0:T(8,128)(2,1)S(1)} %pad_maximum_fusion), channel_id=1, source_target_pairs={{0,2},{1,3},{2,0},{3,1},{4,6},{5,7},{6,4},{7,5},{8,10},{9,11},{10,... | collective-permute-start | bytes 1572872 | tf_op jit(solution)/shard_map/ppermute | solution.py:388
  107.7 16.5 %collective-permute-start.30 = (bf16[128,2048]{1,0:T(8,128)(2,1)S(1)}, bf16[128,2048]{1,0:T(8,128)(2,1)S(1)}, u32[]{:S(2)}, u32[]{:S(2)}) collective-permute-start(bf16[128,2048]{1,0:T(8,128)(2,1)S(1)} %get-tuple-element.237), channel_id=1, source_target_pairs={{0,1},{1,0},{2,3},{3,2},{4,5},{5,4},{6,7},{7,6},{8,9},{9,8},{10,11... | collective-permute-start | bytes 1572872 | tf_op jit(solution)/shard_map/ppermute | solution.py:388
  108.2 23.6 %collective-permute-start.31 = (bf16[128,2048]{1,0:T(8,128)(2,1)S(1)}, bf16[128,2048]{1,0:T(8,128)(2,1)S(1)}, u32[]{:S(2)}, u32[]{:S(2)}) collective-permute-start(bf16[128,2048]{1,0:T(8,128)(2,1)S(1)} %add_convert_fusion.2), channel_id=1, source_target_pairs={{0,2},{1,3},{2,0},{3,1},{4,6},{5,7},{6,4},{7,5},{8,10},{9,11},{10,... | collective-permute-start | bytes 1572872 | tf_op jit(solution)/shard_map/ppermute | solution.py:388
  111.8 24.7 %collective-permute-start.35 = (bf16[128,2048]{1,0:T(8,128)(2,1)S(1)}, bf16[128,2048]{1,0:T(8,128)(2,1)S(1)}, u32[]{:S(2)}, u32[]{:S(2)}) collective-permute-start(bf16[128,2048]{1,0:T(8,128)(2,1)S(1)} %add_convert_fusion), channel_id=1, source_target_pairs={{0,12},{1,13},{2,14},{3,15},{4,0},{5,1},{6,2},{7,3},{8,4},{9,5},{1... | collective-permute-start | bytes 1572872 | tf_op jit(solution)/shard_map/ppermute | solution.py:388
  121.2 15.3 %collective-permute-start.33 = (bf16[128,2048]{1,0:T(8,128)(2,1)S(1)}, bf16[128,2048]{1,0:T(8,128)(2,1)S(1)}, u32[]{:S(2)}, u32[]{:S(2)}) collective-permute-start(bf16[128,2048]{1,0:T(8,128)(2,1)S(1)} %add_convert_fusion.1), channel_id=1, source_target_pairs={{0,4},{1,5},{2,6},{3,7},{4,8},{5,9},{6,10},{7,11},{8,12},{9,13},{1... | collective-permute-start | bytes 1572872 | tf_op jit(solution)/shard_map/ppermute | solution.py:388
